TPU v7x, 32 devices: a whole 2x2x4 slice. The times are simulated.
32 devices in a mesh: queue: 16 (over z, y, core), space: 2 (over x).
Axes of the slice: x: 2, y: 2, z: 4, core: 2. Of those that a mesh axis runs over, the one named last changes fastest.
Arguments:
- latents: float32 [16, 96, 16], P('queue', 'space'), may hold values from -6 to 6
- fresh_noise: float32 [2, 96, 16], P(None, 'space'), may hold values from -6 to 6
- levels: int32 [16], replicated, may hold values from 1 to 1000, as said below
- modulation_weight: bfloat16 [256, 6912], P(None, 'space'), may hold values from -0.375 to 0.375
- embed_weight: bfloat16 [16, 1152], replicated, may hold values from -1.5 to 1.5
- attention_weights: bfloat16 [8, 1152, 1152], P(None, 'space')
- final_weight: bfloat16 [1152, 16], replicated, may hold values from -0.1875 to 0.1875
Outputs:
- queue_after: float32 [16, 96, 16], P('queue', 'space')
- velocity: float32 [2, 16, 96, 16], P(None, 'queue', 'space')
Inputs may be any that keep to these rules, and one draw needn't show every extreme that they name: levels rise strictly along the queue, and the last one is 1000.
All inputs are finite; a program needn't handle non-finite values.
Results may differ from a plain program's by a relative error of at most 0.034.
Values may be sent and summed in bfloat16 or wider, within the bound.
No kernel may reach another device: no remote copies, remote signals or barrier semaphores. Data moves between devices by JAX's collectives and lax.ppermute only.
A program may use at most 64 MiB of HBM per device.

v0:
```python
import math

import jax
import jax.numpy as jnp
from jax import lax
from jax.sharding import PartitionSpec as P

HEAD = 72
FREQ = 256
STEPS = 2
REACH = 4
LEVELS = 1000


def passed_along(x, axis, by):
    peers = lax.axis_size(axis)
    pairs = [(i, i + by) for i in range(peers) if 0 <= i + by < peers]
    return lax.ppermute(x, axis, pairs)


def layer_norm(values):
    average = jnp.mean(values, -1, keepdims=True)
    centred = values - average
    variance = jnp.mean(centred * centred, -1, keepdims=True)
    return centred * lax.rsqrt(variance + 1e-06)


def time_features(level_values):
    times = level_values.astype(jnp.float32) / LEVELS
    half_size = FREQ // 2
    frequency = jnp.exp(-math.log(10000.0) * jnp.arange(half_size).astype(jnp.float32) / half_size)
    angles = (times * 1000.0)[:, None] * frequency[None, :]
    return jnp.concatenate([jnp.cos(angles), jnp.sin(angles)], -1).astype(jnp.bfloat16)


def spatial_attend(query, key_rows, values):
    scores = jnp.einsum("qhd,khd->hqk", query, key_rows, preferred_element_type=jnp.float32) * (
        1.0 / math.sqrt(HEAD)
    )
    probabilities = jax.nn.softmax(scores, axis=-1).astype(jnp.bfloat16)
    return jnp.einsum(
        "hqk,khd->qhd", probabilities, values, preferred_element_type=jnp.float32
    ).astype(jnp.bfloat16)


def temporal_attend(query, key_rows, values, usable):
    scores = jnp.einsum("shd,gshd->shg", query, key_rows, preferred_element_type=jnp.float32) * (
        1.0 / math.sqrt(HEAD)
    )
    scores = jnp.where(usable[None, None, :], scores, -1e30)
    probabilities = jax.nn.softmax(scores, axis=-1).astype(jnp.bfloat16)
    return jnp.einsum(
        "shg,gshd->shd", probabilities, values, preferred_element_type=jnp.float32
    ).astype(jnp.bfloat16)


def right_product(rows, stacked):
    return lax.dot_general(
        rows, stacked, (((1,), (1,)), ((), ())), preferred_element_type=jnp.float32
    )


def local(
    latents, fresh_noise, levels, modulation_weight, embed_weight, attention_weights, final_weight
):
    queue_index = lax.axis_index("queue")
    queue_count = lax.axis_size("queue")
    space_index = lax.axis_index("space")
    own_level = lax.dynamic_index_in_dim(levels, queue_index, keepdims=False)
    below = lax.dynamic_index_in_dim(levels, jnp.maximum(queue_index - 1, 0), keepdims=False)
    next_level = jnp.where(queue_index > 0, below, 0)
    step_size = (next_level - own_level).astype(jnp.float32) / LEVELS
    modulation_share = jnp.dot(
        time_features(own_level.reshape(1)), modulation_weight, preferred_element_type=jnp.float32
    )[0]
    conditioning = lax.all_gather(modulation_share, "space", axis=0, tiled=True)
    width = embed_weight.shape[1]
    local_width = attention_weights.shape[1]
    head_count = local_width // HEAD
    spatial_weights = jnp.concatenate(
        [attention_weights[0], attention_weights[1], attention_weights[2]], 0
    )
    temporal_weights = jnp.concatenate(
        [attention_weights[4], attention_weights[5], attention_weights[6]], 0
    )
    spatial_exit = attention_weights[3]
    temporal_exit = attention_weights[7]
    current = latents[0]
    own_rows = current.shape[0]
    row_start = space_index * own_rows
    offsets = jnp.arange(2 * REACH + 1) - REACH + queue_index
    usable = (offsets >= 0) & (offsets < queue_count)
    velocities = []
    for iteration in range(STEPS):
        frame_tokens = lax.all_gather(current.astype(jnp.bfloat16), "space", axis=0, tiled=True)
        stream_in = jnp.dot(frame_tokens, embed_weight, preferred_element_type=jnp.float32)
        total = stream_in.shape[0]
        normed = (
            layer_norm(stream_in) * (1.0 + conditioning[width : 2 * width]) + conditioning[0:width]
        ).astype(jnp.bfloat16)
        spatial_proj = right_product(normed, spatial_weights).astype(jnp.bfloat16)
        spatial_proj = spatial_proj.reshape(total, 3, head_count, HEAD)
        spatial = spatial_attend(
            spatial_proj[:, 0], spatial_proj[:, 1], spatial_proj[:, 2]
        ).reshape(total, local_width)
        own_stream = lax.dynamic_slice_in_dim(stream_in, row_start, own_rows, 0)
        stream_mid = own_stream + conditioning[2 * width : 3 * width] * lax.psum_scatter(
            jnp.dot(spatial, spatial_exit, preferred_element_type=jnp.float32).astype(jnp.bfloat16),
            "space",
            scatter_dimension=0,
            tiled=True,
        ).astype(jnp.float32)
        normed_temporal = (
            layer_norm(stream_mid) * (1.0 + conditioning[4 * width : 5 * width])
            + conditioning[3 * width : 4 * width]
        ).astype(jnp.bfloat16)
        temporal_proj = right_product(
            lax.all_gather(normed_temporal, "space", axis=0, tiled=True), temporal_weights
        ).astype(jnp.bfloat16)
        temporal_query = temporal_proj[:, :local_width].reshape(total, head_count, HEAD)
        pairs = temporal_proj[:, local_width:]
        lower = []
        upper = []
        for distance in range(1, REACH + 1):
            lower.append(passed_along(pairs, "queue", distance))
            upper.append(passed_along(pairs, "queue", -distance))
        window = jnp.stack(lower[::-1] + [pairs] + upper, 0)
        key_window = window[..., :local_width].reshape(2 * REACH + 1, total, head_count, HEAD)
        value_window = window[..., local_width:].reshape(2 * REACH + 1, total, head_count, HEAD)
        temporal = temporal_attend(temporal_query, key_window, value_window, usable).reshape(
            total, local_width
        )
        stream_out = stream_mid + conditioning[5 * width : 6 * width] * lax.psum_scatter(
            jnp.dot(temporal, temporal_exit, preferred_element_type=jnp.float32).astype(
                jnp.bfloat16
            ),
            "space",
            scatter_dimension=0,
            tiled=True,
        ).astype(jnp.float32)
        velocity = jnp.dot(
            layer_norm(stream_out).astype(jnp.bfloat16),
            final_weight,
            preferred_element_type=jnp.float32,
        )
        velocities.append(velocity)
        updated = current + step_size * velocity
        arriving = passed_along(updated, "queue", -1)
        current = jnp.where(queue_index == queue_count - 1, fresh_noise[iteration], arriving)
    return (current[None], jnp.stack(velocities, 0)[:, None])


def solution(mesh):
    in_specs = (
        P("queue", "space", None),
        P(None, "space", None),
        P(),
        P(None, "space"),
        P(),
        P(None, "space", None),
        P(),
    )
    out_specs = (P("queue", "space", None), P(None, "queue", "space", None))
    return jax.shard_map(local, mesh=mesh, in_specs=in_specs, out_specs=out_specs, check_vma=False)
```

profile of v0, /device:TPU:0, one launch (start us, length us, event | category | flops | bytes accessed | tf_op | source)
XLA Modules:
  0.0 221.8 jit_solution(7170032820609461348)
XLA Ops:
  7.3 5.8 %slice_bitcast_fusion.2 = (bf16[576,1152]{1,0:T(8,128)(2,1)}, bf16[576,1152]{1,0:T(8,128)(2,1)}, bf16[576,1152]{1,0:T(8,128)(2,1)}, bf16[576,1152]{1,0:T(8,128)(...) fusion(bf16[8,576,1152]{2,1,0:T(8,128)(2,1)} %param.12), kind=kLoop, calls=%fused_computation.23 | loop fusion | bytes 15925248 | tf_op jit(solution)/shard_map/squeeze | solution.py:84
  13.1 5.2 %all-gather = bf16[2,48,16]{1,2,0:T(8,128)(2,1)S(1)} all-gather(bf16[1,48,16]{1,2,0:T(8,128)(2,1)S(1)} %fusion.39), channel_id=1, replica_groups=mesh['queue'=16,'space'=2] {'space'}, dimensions={0}, use_global_device_ids=true | all-gather | bytes 4608 | tf_op jit(solution)/shard_map/all_gather | solution.py:95
  20.1 4.4 %all-gather.1 = f32[2,1,3456]{2,1,0:T(1,128)S(1)} all-gather(f32[1,1,3456]{2,1,0:T(1,128)S(1)} %convolution_bitcast_fusion), channel_id=1, replica_groups=mesh['queue'=16,'space'=2] {'space'}, dimensions={0}, use_global_device_ids=true | all-gather | bytes 41472 | tf_op jit(solution)/shard_map/all_gather | solution.py:76
  25.3 3.4 %convolution_convert_fusion.7 = bf16[96,1728]{1,0:T(8,128)(2,1)S(1)} fusion(bf16[576,1152]{1,0:T(8,128)(2,1)} %get-tuple-element.16, bf16[576,1152]{1,0:T(8,128)(2,1)} %get-tuple-element.17, bf16[576,1152]{1,0:T(8,128)(2,1)} %get-tuple-element.18, f32[96,1152]{1,0:T(8,128)S(1)} %get-tuple-element.33, f32[1152]{0:T(1024)S(1)} %get-tuple-element.27, ...), kind=kOutput, calls=%fused_computation.16 | convolution fusion | flops 394868736 | bytes 4765440 | tf_op jit(solution)/shard_map/dot_general | solution.py:58
  29.8 2.4 %convolution_convert_fusion.6 = bf16[96,1152]{1,0:T(8,128)(2,1)} fusion(bf16[96,576]{0,1:T(8,128)(2,1)S(1)} %bitcast.186, bf16[8,576,1152]{2,1,0:T(8,128)(2,1)} %param.12), kind=kOutput, calls=%fused_computation.15 | convolution fusion | flops 127512576 | bytes 1658880 | tf_op jit(solution)/shard_map/dot_general | solution.py:108
  32.4 13.1 %reduce-scatter.5.cloned.1.call-done = bf16[48,1152]{1,0:T(8,128)(2,1)} async-done(((bf16[96,1152]{1,0:T(8,128)(2,1)}), bf16[48,1152]{1,0:T(8,128)(2,1)}) %reduce-scatter.5.cloned.1.call-update) | async-done | bytes 110608 | tf_op jit(solution)/shard_map/reduce_scatter | solution.py:107
  46.8 5.5 %all_gather.17 = bf16[96,1152]{1,0:T(8,128)(2,1)S(1)} all-gather(bf16[48,1152]{1,0:T(8,128)(2,1)S(1)} %add_convert_fusion.5), channel_id=1, replica_groups=mesh['queue'=16,'space'=2] {'space'}, dimensions={0}, use_global_device_ids=true | all-gather | bytes 331776 | tf_op jit(solution)/shard_map/all_gather | solution.py:118
  52.3 3.4 %convolution_convert_fusion.5 = bf16[96,1728]{1,0:T(8,128)(2,1)S(1)} fusion(bf16[96,1152]{1,0:T(8,128)(2,1)S(1)} %all_gather.17, bf16[576,1152]{1,0:T(8,128)(2,1)} %get-tuple-element.19, bf16[576,1152]{1,0:T(8,128)(2,1)} %get-tuple-element.15, bf16[576,1152]{1,0:T(8,128)(2,1)} %get-tuple-element.14), kind=kOutput, calls=%fused_computation.14 | convolution fusion | flops 394315776 | bytes 4534272 | tf_op jit(solution)/shard_map/dot_general | solution.py:58
  55.9 4.1 %collective-permute-start = (bf16[96,1152]{1,0:T(8,128)(2,1)S(1)}, bf16[96,1152]{1,0:T(8,128)(2,1)}, u32[]{:S(2)}, u32[]{:S(2)}) collective-permute-start(bf16[96,1152]{1,0:T(8,128)(2,1)S(1)} %slice.136), channel_id=1, source_target_pairs={{0,8},{2,10},{4,12},{6,14},{8,16},{10,18},{12,20},{14,22},{16,24},... | collective-permute-start | bytes 663560 | tf_op jit(solution)/shard_map/ppermute | solution.py:18
  60.5 2.4 %collective-permute-start.1 = (bf16[96,1152]{1,0:T(8,128)(2,1)S(1)}, bf16[96,1152]{1,0:T(8,128)(2,1)}, u32[]{:S(2)}, u32[]{:S(2)}) collective-permute-start(bf16[96,1152]{1,0:T(8,128)(2,1)S(1)} %slice.136), channel_id=1, source_target_pairs={{0,6},{2,8},{4,10},{6,12},{8,14},{10,16},{12,18},{14,20},{16,22},{... | collective-permute-start | bytes 663560 | tf_op jit(solution)/shard_map/ppermute | solution.py:18
  62.9 3.0 %collective-permute-start.2 = (bf16[96,1152]{1,0:T(8,128)(2,1)S(1)}, bf16[96,1152]{1,0:T(8,128)(2,1)S(1)}, u32[]{:S(2)}, u32[]{:S(2)}) collective-permute-start(bf16[96,1152]{1,0:T(8,128)(2,1)S(1)} %slice.136), channel_id=1, source_target_pairs={{0,4},{2,6},{4,8},{6,10},{8,12},{10,14},{12,16},{14,18},{16,20},{1... | collective-permute-start | bytes 663560 | tf_op jit(solution)/shard_map/ppermute | solution.py:18
  65.9 2.5 %collective-permute-start.3 = (bf16[96,1152]{1,0:T(8,128)(2,1)S(1)}, bf16[96,1152]{1,0:T(8,128)(2,1)S(1)}, u32[]{:S(2)}, u32[]{:S(2)}) collective-permute-start(bf16[96,1152]{1,0:T(8,128)(2,1)S(1)} %slice.136), channel_id=1, source_target_pairs={{0,2},{2,4},{4,6},{6,8},{8,10},{10,12},{12,14},{14,16},{16,18},{18... | collective-permute-start | bytes 663560 | tf_op jit(solution)/shard_map/ppermute | solution.py:18
  68.4 1.3 collective-permute-start.4
  72.9 1.3 collective-permute-start.6
  75.1 1.3 collective-permute-start.7
  76.7 4.5 %collective-permute-done.5 = bf16[96,1152]{1,0:T(8,128)(2,1)S(1)} collective-permute-done((bf16[96,1152]{1,0:T(8,128)(2,1)S(1)}, bf16[96,1152]{1,0:T(8,128)(2,1)S(1)}, u32[]{:S(2)}, u32[]{:S(2)}) %collective-permute-start.5) | collective-permute-done | bytes 221216 | tf_op jit(solution)/shard_map/ppermute | solution.py:18
  81.2 2.1 collective-permute-done.6
  83.4 8.0 %collective-permute-done.7 = bf16[96,1152]{1,0:T(8,128)(2,1)S(1)} collective-permute-done((bf16[96,1152]{1,0:T(8,128)(2,1)S(1)}, bf16[96,1152]{1,0:T(8,128)(2,1)S(1)}, u32[]{:S(2)}, u32[]{:S(2)}) %collective-permute-start.7) | collective-permute-done | bytes 221216 | tf_op jit(solution)/shard_map/ppermute | solution.py:18
  91.4 2.0 fusion.51
  93.4 2.3 %copy.82 = bf16[9,96,576]{1,2,0:T(8,128)(2,1)S(1)} copy(bf16[9,96,576]{2,1,0:T(8,128)(2,1)} %get-tuple-element.23) | data formatting | bytes 1990656
  95.7 2.6 %copy.81 = bf16[9,96,576]{1,2,0:T(8,128)(2,1)} copy(bf16[9,96,576]{2,1,0:T(8,128)(2,1)} %get-tuple-element.22) | data formatting | bytes 1990656
  98.3 1.8 multiply_reduce_fusion.3
  100.8 2.4 %convolution_convert_fusion.4 = bf16[96,1152]{1,0:T(8,128)(2,1)} fusion(bf16[96,576]{0,1:T(8,128)(2,1)S(1)} %bitcast.182, bf16[8,576,1152]{2,1,0:T(8,128)(2,1)} %param.12), kind=kOutput, calls=%fused_computation.13 | convolution fusion | flops 127512576 | bytes 1658880 | tf_op jit(solution)/shard_map/dot_general | solution.py:134
  104.6 7.0 %reduce-scatter.7.cloned.1.call-done = bf16[48,1152]{1,0:T(8,128)(2,1)} async-done(((bf16[96,1152]{1,0:T(8,128)(2,1)}), bf16[48,1152]{1,0:T(8,128)(2,1)}) %reduce-scatter.7.cloned.1.call-update) | async-done | bytes 110608 | tf_op jit(solution)/shard_map/reduce_scatter | solution.py:133
  113.8 1.7 bitcast_add_fusion
  116.8 1.8 collective-permute-done.8
  119.3 4.3 %all-gather.2 = bf16[2,48,16]{1,2,0:T(8,128)(2,1)S(1)} all-gather(bf16[1,48,16]{1,2,0:T(8,128)(2,1)S(1)} %convert_bitcast_fusion), channel_id=1, replica_groups=mesh['queue'=16,'space'=2] {'space'}, dimensions={0}, use_global_device_ids=true | all-gather | bytes 4608 | tf_op jit(solution)/shard_map/all_gather | solution.py:95
  124.3 3.4 %convolution_convert_fusion.3 = bf16[96,1728]{1,0:T(8,128)(2,1)S(1)} fusion(bf16[576,1152]{1,0:T(8,128)(2,1)} %get-tuple-element.16, bf16[576,1152]{1,0:T(8,128)(2,1)} %get-tuple-element.17, bf16[576,1152]{1,0:T(8,128)(2,1)} %get-tuple-element.18, f32[96,1152]{1,0:T(8,128)S(1)} %get-tuple-element.37, f32[96]{0:T(128)S(1)} %add_rsqrt_fusion.2, ...), kind=kOutput, calls=%fused_computation.12 | convolution fusion | flops 394868736 | bytes 4765440 | tf_op jit(solution)/shard_map/dot_general | solution.py:58
  128.9 2.4 %convolution_convert_fusion.2 = bf16[96,1152]{1,0:T(8,128)(2,1)} fusion(bf16[96,576]{0,1:T(8,128)(2,1)S(1)} %bitcast.187, bf16[8,576,1152]{2,1,0:T(8,128)(2,1)} %param.12), kind=kOutput, calls=%fused_computation.11 | convolution fusion | flops 127512576 | bytes 1658880 | tf_op jit(solution)/shard_map/dot_general | solution.py:108
  131.4 11.5 %reduce-scatter.9.cloned.1.call-done = bf16[48,1152]{1,0:T(8,128)(2,1)} async-done(((bf16[96,1152]{1,0:T(8,128)(2,1)}), bf16[48,1152]{1,0:T(8,128)(2,1)}) %reduce-scatter.9.cloned.1.call-update) | async-done | bytes 110608 | tf_op jit(solution)/shard_map/reduce_scatter | solution.py:107
  144.3 5.5 %all_gather.19 = bf16[96,1152]{1,0:T(8,128)(2,1)S(1)} all-gather(bf16[48,1152]{1,0:T(8,128)(2,1)S(1)} %add_convert_fusion.4), channel_id=1, replica_groups=mesh['queue'=16,'space'=2] {'space'}, dimensions={0}, use_global_device_ids=true | all-gather | bytes 331776 | tf_op jit(solution)/shard_map/all_gather | solution.py:118
  149.8 3.4 %convolution_convert_fusion.1 = bf16[96,1728]{1,0:T(8,128)(2,1)S(1)} fusion(bf16[96,1152]{1,0:T(8,128)(2,1)S(1)} %all_gather.19, bf16[576,1152]{1,0:T(8,128)(2,1)} %get-tuple-element.19, bf16[576,1152]{1,0:T(8,128)(2,1)} %get-tuple-element.15, bf16[576,1152]{1,0:T(8,128)(2,1)} %get-tuple-element.14), kind=kOutput, calls=%fused_computation.10 | convolution fusion | flops 394315776 | bytes 4534272 | tf_op jit(solution)/shard_map/dot_general | solution.py:58
  153.3 4.1 %collective-permute-start.9 = (bf16[96,1152]{1,0:T(8,128)(2,1)S(1)}, bf16[96,1152]{1,0:T(8,128)(2,1)}, u32[]{:S(2)}, u32[]{:S(2)}) collective-permute-start(bf16[96,1152]{1,0:T(8,128)(2,1)S(1)} %slice.143), channel_id=1, source_target_pairs={{0,8},{2,10},{4,12},{6,14},{8,16},{10,18},{12,20},{14,22},{16,24},... | collective-permute-start | bytes 663560 | tf_op jit(solution)/shard_map/ppermute | solution.py:18
  157.4 2.4 %collective-permute-start.10 = (bf16[96,1152]{1,0:T(8,128)(2,1)S(1)}, bf16[96,1152]{1,0:T(8,128)(2,1)}, u32[]{:S(2)}, u32[]{:S(2)}) collective-permute-start(bf16[96,1152]{1,0:T(8,128)(2,1)S(1)} %slice.143), channel_id=1, source_target_pairs={{0,6},{2,8},{4,10},{6,12},{8,14},{10,16},{12,18},{14,20},{16,22},{... | collective-permute-start | bytes 663560 | tf_op jit(solution)/shard_map/ppermute | solution.py:18
  159.7 3.0 %collective-permute-start.11 = (bf16[96,1152]{1,0:T(8,128)(2,1)S(1)}, bf16[96,1152]{1,0:T(8,128)(2,1)S(1)}, u32[]{:S(2)}, u32[]{:S(2)}) collective-permute-start(bf16[96,1152]{1,0:T(8,128)(2,1)S(1)} %slice.143), channel_id=1, source_target_pairs={{0,4},{2,6},{4,8},{6,10},{8,12},{10,14},{12,16},{14,18},{16,20},{1... | collective-permute-start | bytes 663560 | tf_op jit(solution)/shard_map/ppermute | solution.py:18
  162.8 2.5 %collective-permute-start.12 = (bf16[96,1152]{1,0:T(8,128)(2,1)S(1)}, bf16[96,1152]{1,0:T(8,128)(2,1)S(1)}, u32[]{:S(2)}, u32[]{:S(2)}) collective-permute-start(bf16[96,1152]{1,0:T(8,128)(2,1)S(1)} %slice.143), channel_id=1, source_target_pairs={{0,2},{2,4},{4,6},{6,8},{8,10},{10,12},{12,14},{14,16},{16,18},{18... | collective-permute-start | bytes 663560 | tf_op jit(solution)/shard_map/ppermute | solution.py:18
  165.3 1.5 collective-permute-start.13
  169.9 1.3 collective-permute-start.15
  173.8 4.6 %collective-permute-done.14 = bf16[96,1152]{1,0:T(8,128)(2,1)S(1)} collective-permute-done((bf16[96,1152]{1,0:T(8,128)(2,1)S(1)}, bf16[96,1152]{1,0:T(8,128)(2,1)S(1)}, u32[]{:S(2)}, u32[]{:S(2)}) %collective-permute-start.14) | collective-permute-done | bytes 221216 | tf_op jit(solution)/shard_map/ppermute | solution.py:18
  178.4 2.0 collective-permute-done.15
  180.4 8.0 %collective-permute-done.16 = bf16[96,1152]{1,0:T(8,128)(2,1)S(1)} collective-permute-done((bf16[96,1152]{1,0:T(8,128)(2,1)S(1)}, bf16[96,1152]{1,0:T(8,128)(2,1)S(1)}, u32[]{:S(2)}, u32[]{:S(2)}) %collective-permute-start.16) | collective-permute-done | bytes 221216 | tf_op jit(solution)/shard_map/ppermute | solution.py:18
  188.4 1.9 fusion.50
  190.3 2.3 %copy.84 = bf16[9,96,576]{1,2,0:T(8,128)(2,1)S(1)} copy(bf16[9,96,576]{2,1,0:T(8,128)(2,1)} %get-tuple-element.21) | data formatting | bytes 1990656
  192.6 2.5 %copy.83 = bf16[9,96,576]{1,2,0:T(8,128)(2,1)} copy(bf16[9,96,576]{2,1,0:T(8,128)(2,1)} %get-tuple-element.20) | data formatting | bytes 1990656
  195.1 1.8 multiply_reduce_fusion.1
  197.6 2.4 %convolution_convert_fusion = bf16[96,1152]{1,0:T(8,128)(2,1)} fusion(bf16[96,576]{0,1:T(8,128)(2,1)S(1)} %bitcast.183, bf16[8,576,1152]{2,1,0:T(8,128)(2,1)} %param.12), kind=kOutput, calls=%fused_computation.9 | convolution fusion | flops 127512576 | bytes 1658880 | tf_op jit(solution)/shard_map/dot_general | solution.py:134
  200.1 8.2 %reduce-scatter.11.cloned.1.call-done = bf16[48,1152]{1,0:T(8,128)(2,1)} async-done(((bf16[96,1152]{1,0:T(8,128)(2,1)}), bf16[48,1152]{1,0:T(8,128)(2,1)}) %reduce-scatter.11.cloned.1.call-update) | async-done | bytes 110608 | tf_op jit(solution)/shard_map/reduce_scatter | solution.py:133
  211.6 1.3 collective-permute-start.17
  (153 shorter events, 29.7 us)
Async XLA Ops:
  7.2 12.6 %copy-start = (bf16[256,3456]{1,0:T(8,128)(2,1)S(1)}, bf16[256,3456]{1,0:T(8,128)(2,1)}, u32[]{:S(2)}) copy-start(bf16[256,3456]{1,0:T(8,128)(2,1)} %param.10) | copy-start | bytes 5308420
  7.2 38.3 %reduce-scatter.5.cloned.1.call-start = ((), (), s32[]{:S(2)}) async-start(), calls=%async_computation.4 | async-start | bytes 331776 | tf_op jit(solution)/shard_map/reduce_scatter | solution.py:107
  7.2 5.8 %copy-start.9 = (f32[1,48,16]{1,2,0:T(8,128)S(1)}, f32[1,48,16]{1,2,0:T(8,128)}, u32[]{:S(2)}) copy-start(f32[1,48,16]{1,2,0:T(8,128)} %param.7) | copy-start | bytes 9220
  7.2 11.2 %copy-start.21 = (s32[16]{0:T(128)S(1)}, s32[16]{0:T(128)}, u32[]{:S(2)}) copy-start(s32[16]{0:T(128)} %param.9) | copy-start | bytes 196
  13.1 11.6 %copy-start.1 = (bf16[16,1152]{1,0:T(8,128)(2,1)S(1)}, bf16[16,1152]{1,0:T(8,128)(2,1)}, u32[]{:S(2)}) copy-start(bf16[16,1152]{1,0:T(8,128)(2,1)} %param.11) | copy-start | bytes 110596
  24.7 4.0 %copy-start.17 = (f32[1152]{0:T(1024)}, f32[1152]{0:T(1024)S(1)}, u32[]{:S(2)}) copy-start(f32[1152]{0:T(1024)S(1)} %get-tuple-element.27) | copy-start | bytes 13828
  24.7 4.0 %copy-start.19 = (f32[1152]{0:T(1024)}, f32[1152]{0:T(1024)S(1)}, u32[]{:S(2)}) copy-start(f32[1152]{0:T(1024)S(1)} %get-tuple-element.28) | copy-start | bytes 13828
  24.7 22.0 %copy-start.5 = (f32[1152]{0:T(1024)}, f32[1152]{0:T(1024)S(1)}, u32[]{:S(2)}) copy-start(f32[1152]{0:T(1024)S(1)} %get-tuple-element.25) | copy-start | bytes 13828
  24.7 22.0 %copy-start.7 = (f32[1152]{0:T(1024)}, f32[1152]{0:T(1024)S(1)}, u32[]{:S(2)}) copy-start(f32[1152]{0:T(1024)S(1)} %get-tuple-element.26) | copy-start | bytes 13828
  32.3 79.3 %reduce-scatter.7.cloned.1.call-start = ((), (), s32[]{:S(2)}) async-start(), calls=%async_computation.5 | async-start | bytes 331776 | tf_op jit(solution)/shard_map/reduce_scatter | solution.py:133
  55.9 14.8 %collective-permute-start = (bf16[96,1152]{1,0:T(8,128)(2,1)S(1)}, bf16[96,1152]{1,0:T(8,128)(2,1)}, u32[]{:S(2)}, u32[]{:S(2)}) collective-permute-start(bf16[96,1152]{1,0:T(8,128)(2,1)S(1)} %slice.136), channel_id=1, source_target_pairs={{0,8},{2,10},{4,12},{6,14},{8,16},{10,18},{12,20},{14,22},{16,24},... | collective-permute-start | bytes 663560 | tf_op jit(solution)/shard_map/ppermute | solution.py:18
  60.5 12.4 %collective-permute-start.1 = (bf16[96,1152]{1,0:T(8,128)(2,1)S(1)}, bf16[96,1152]{1,0:T(8,128)(2,1)}, u32[]{:S(2)}, u32[]{:S(2)}) collective-permute-start(bf16[96,1152]{1,0:T(8,128)(2,1)S(1)} %slice.136), channel_id=1, source_target_pairs={{0,6},{2,8},{4,10},{6,12},{8,14},{10,16},{12,18},{14,20},{16,22},{... | collective-permute-start | bytes 663560 | tf_op jit(solution)/shard_map/ppermute | solution.py:18
  62.9 12.2 %collective-permute-start.2 = (bf16[96,1152]{1,0:T(8,128)(2,1)S(1)}, bf16[96,1152]{1,0:T(8,128)(2,1)S(1)}, u32[]{:S(2)}, u32[]{:S(2)}) collective-permute-start(bf16[96,1152]{1,0:T(8,128)(2,1)S(1)} %slice.136), channel_id=1, source_target_pairs={{0,4},{2,6},{4,8},{6,10},{8,12},{10,14},{12,16},{14,18},{16,20},{1... | collective-permute-start | bytes 663560 | tf_op jit(solution)/shard_map/ppermute | solution.py:18
  65.9 10.6 %collective-permute-start.3 = (bf16[96,1152]{1,0:T(8,128)(2,1)S(1)}, bf16[96,1152]{1,0:T(8,128)(2,1)S(1)}, u32[]{:S(2)}, u32[]{:S(2)}) collective-permute-start(bf16[96,1152]{1,0:T(8,128)(2,1)S(1)} %slice.136), channel_id=1, source_target_pairs={{0,2},{2,4},{4,6},{6,8},{8,10},{10,12},{12,14},{14,16},{16,18},{18... | collective-permute-start | bytes 663560 | tf_op jit(solution)/shard_map/ppermute | solution.py:18
  68.4 8.3 %collective-permute-start.4 = (bf16[96,1152]{1,0:T(8,128)(2,1)S(1)}, bf16[96,1152]{1,0:T(8,128)(2,1)S(1)}, u32[]{:S(2)}, u32[]{:S(2)}) collective-permute-start(bf16[96,1152]{1,0:T(8,128)(2,1)S(1)} %slice.136), channel_id=1, source_target_pairs={{2,0},{4,2},{6,4},{8,6},{10,8},{12,10},{14,12},{16,14},{18,16},{20... | collective-permute-start | bytes 663560 | tf_op jit(solution)/shard_map/ppermute | solution.py:18
  70.6 10.6 %collective-permute-start.5 = (bf16[96,1152]{1,0:T(8,128)(2,1)S(1)}, bf16[96,1152]{1,0:T(8,128)(2,1)S(1)}, u32[]{:S(2)}, u32[]{:S(2)}) collective-permute-start(bf16[96,1152]{1,0:T(8,128)(2,1)S(1)} %slice.136), channel_id=1, source_target_pairs={{4,0},{6,2},{8,4},{10,6},{12,8},{14,10},{16,12},{18,14},{20,16},{2... | collective-permute-start | bytes 663560 | tf_op jit(solution)/shard_map/ppermute | solution.py:18
  72.9 10.5 %collective-permute-start.6 = (bf16[96,1152]{1,0:T(8,128)(2,1)S(1)}, bf16[96,1152]{1,0:T(8,128)(2,1)S(1)}, u32[]{:S(2)}, u32[]{:S(2)}) collective-permute-start(bf16[96,1152]{1,0:T(8,128)(2,1)S(1)} %slice.136), channel_id=1, source_target_pairs={{6,0},{8,2},{10,4},{12,6},{14,8},{16,10},{18,12},{20,14},{22,16},{... | collective-permute-start | bytes 663560 | tf_op jit(solution)/shard_map/ppermute | solution.py:18
  75.1 16.2 %collective-permute-start.7 = (bf16[96,1152]{1,0:T(8,128)(2,1)S(1)}, bf16[96,1152]{1,0:T(8,128)(2,1)S(1)}, u32[]{:S(2)}, u32[]{:S(2)}) collective-permute-start(bf16[96,1152]{1,0:T(8,128)(2,1)S(1)} %slice.136), channel_id=1, source_target_pairs={{8,0},{10,2},{12,4},{14,6},{16,8},{18,10},{20,12},{22,14},{24,16},... | collective-permute-start | bytes 663560 | tf_op jit(solution)/shard_map/ppermute | solution.py:18
  95.7 4.4 %copy-start.15 = (pred[9]{0:T(512)(128)(4,1)S(1)}, pred[9]{0:T(512)(128)(4,1)}, u32[]{:S(2)}) copy-start(pred[9]{0:T(512)(128)(4,1)} %compare_and_fusion) | copy-start | bytes 31
  100.3 13.4 %copy-start.3 = (bf16[1152,16]{0,1:T(8,128)(2,1)S(1)}, bf16[1152,16]{0,1:T(8,128)(2,1)}, u32[]{:S(2)}) copy-start(bf16[1152,16]{0,1:T(8,128)(2,1)} %param.13) | copy-start | bytes 110596
  100.3 13.4 %copy-start.10 = (f32[1,48,16]{1,2,0:T(8,128)S(1)}, f32[1,48,16]{1,2,0:T(8,128)}, u32[]{:S(2)}) copy-start(f32[1,48,16]{1,2,0:T(8,128)} %param.7) | copy-start | bytes 9220
  100.4 23.4 %copy-start.2 = (bf16[16,1152]{1,0:T(8,128)(2,1)S(1)}, bf16[16,1152]{1,0:T(8,128)(2,1)}, u32[]{:S(2)}) copy-start(bf16[16,1152]{1,0:T(8,128)(2,1)} %param.11) | copy-start | bytes 110596
  100.8 23.5 %copy-start.18 = (f32[1152]{0:T(1024)S(1)}, f32[1152]{0:T(1024)}, u32[]{:S(2)}) copy-start(f32[1152]{0:T(1024)} %copy-done.17) | copy-start | bytes 13828
  100.8 23.5 %copy-start.20 = (f32[1152]{0:T(1024)S(1)}, f32[1152]{0:T(1024)}, u32[]{:S(2)}) copy-start(f32[1152]{0:T(1024)} %copy-done.19) | copy-start | bytes 13828
  103.2 39.7 %reduce-scatter.9.cloned.1.call-start = ((), (), s32[]{:S(2)}) async-start(), calls=%async_computation.6 | async-start | bytes 331776 | tf_op jit(solution)/shard_map/reduce_scatter | solution.py:107
  115.5 3.1 %collective-permute-start.8 = (f32[48,16]{0,1:T(8,128)S(1)}, f32[48,16]{0,1:T(8,128)S(1)}, u32[]{:S(2)}, u32[]{:S(2)}) collective-permute-start(f32[48,16]{0,1:T(8,128)S(1)} %get-tuple-element.34), channel_id=1, source_target_pairs={{2,0},{4,2},{6,4},{8,6},{10,8},{12,10},{14,12},{16,14},{18,16},{20... | collective-permute-start | bytes 9224 | tf_op jit(solution)/shard_map/ppermute | solution.py:18
  118.6 9.1 %copy-start.11 = (f32[48,16]{0,1:T(8,128)}, f32[48,16]{0,1:T(8,128)S(1)}, u32[]{:S(2)}) copy-start(f32[48,16]{0,1:T(8,128)S(1)} %collective-permute-done.8) | copy-start | bytes 9220
  128.6 15.6 %copy-start.6 = (f32[1152]{0:T(1024)S(1)}, f32[1152]{0:T(1024)}, u32[]{:S(2)}) copy-start(f32[1152]{0:T(1024)} %copy-done.5) | copy-start | bytes 13828
  128.6 15.6 %copy-start.8 = (f32[1152]{0:T(1024)S(1)}, f32[1152]{0:T(1024)}, u32[]{:S(2)}) copy-start(f32[1152]{0:T(1024)} %copy-done.7) | copy-start | bytes 13828
  131.3 77.0 %reduce-scatter.11.cloned.1.call-start = ((), (), s32[]{:S(2)}) async-start(), calls=%async_computation.7 | async-start | bytes 331776 | tf_op jit(solution)/shard_map/reduce_scatter | solution.py:133
  153.3 14.4 %collective-permute-start.9 = (bf16[96,1152]{1,0:T(8,128)(2,1)S(1)}, bf16[96,1152]{1,0:T(8,128)(2,1)}, u32[]{:S(2)}, u32[]{:S(2)}) collective-permute-start(bf16[96,1152]{1,0:T(8,128)(2,1)S(1)} %slice.143), channel_id=1, source_target_pairs={{0,8},{2,10},{4,12},{6,14},{8,16},{10,18},{12,20},{14,22},{16,24},... | collective-permute-start | bytes 663560 | tf_op jit(solution)/shard_map/ppermute | solution.py:18
  157.4 12.5 %collective-permute-start.10 = (bf16[96,1152]{1,0:T(8,128)(2,1)S(1)}, bf16[96,1152]{1,0:T(8,128)(2,1)}, u32[]{:S(2)}, u32[]{:S(2)}) collective-permute-start(bf16[96,1152]{1,0:T(8,128)(2,1)S(1)} %slice.143), channel_id=1, source_target_pairs={{0,6},{2,8},{4,10},{6,12},{8,14},{10,16},{12,18},{14,20},{16,22},{... | collective-permute-start | bytes 663560 | tf_op jit(solution)/shard_map/ppermute | solution.py:18
  159.7 12.4 %collective-permute-start.11 = (bf16[96,1152]{1,0:T(8,128)(2,1)S(1)}, bf16[96,1152]{1,0:T(8,128)(2,1)S(1)}, u32[]{:S(2)}, u32[]{:S(2)}) collective-permute-start(bf16[96,1152]{1,0:T(8,128)(2,1)S(1)} %slice.143), channel_id=1, source_target_pairs={{0,4},{2,6},{4,8},{6,10},{8,12},{10,14},{12,16},{14,18},{16,20},{1... | collective-permute-start | bytes 663560 | tf_op jit(solution)/shard_map/ppermute | solution.py:18
  162.8 10.8 %collective-permute-start.12 = (bf16[96,1152]{1,0:T(8,128)(2,1)S(1)}, bf16[96,1152]{1,0:T(8,128)(2,1)S(1)}, u32[]{:S(2)}, u32[]{:S(2)}) collective-permute-start(bf16[96,1152]{1,0:T(8,128)(2,1)S(1)} %slice.143), channel_id=1, source_target_pairs={{0,2},{2,4},{4,6},{6,8},{8,10},{10,12},{12,14},{14,16},{16,18},{18... | collective-permute-start | bytes 663560 | tf_op jit(solution)/shard_map/ppermute | solution.py:18
  165.3 8.4 %collective-permute-start.13 = (bf16[96,1152]{1,0:T(8,128)(2,1)S(1)}, bf16[96,1152]{1,0:T(8,128)(2,1)S(1)}, u32[]{:S(2)}, u32[]{:S(2)}) collective-permute-start(bf16[96,1152]{1,0:T(8,128)(2,1)S(1)} %slice.143), channel_id=1, source_target_pairs={{2,0},{4,2},{6,4},{8,6},{10,8},{12,10},{14,12},{16,14},{18,16},{20... | collective-permute-start | bytes 663560 | tf_op jit(solution)/shard_map/ppermute | solution.py:18
  167.7 10.7 %collective-permute-start.14 = (bf16[96,1152]{1,0:T(8,128)(2,1)S(1)}, bf16[96,1152]{1,0:T(8,128)(2,1)S(1)}, u32[]{:S(2)}, u32[]{:S(2)}) collective-permute-start(bf16[96,1152]{1,0:T(8,128)(2,1)S(1)} %slice.143), channel_id=1, source_target_pairs={{4,0},{6,2},{8,4},{10,6},{12,8},{14,10},{16,12},{18,14},{20,16},{2... | collective-permute-start | bytes 663560 | tf_op jit(solution)/shard_map/ppermute | solution.py:18
  169.9 10.5 %collective-permute-start.15 = (bf16[96,1152]{1,0:T(8,128)(2,1)S(1)}, bf16[96,1152]{1,0:T(8,128)(2,1)S(1)}, u32[]{:S(2)}, u32[]{:S(2)}) collective-permute-start(bf16[96,1152]{1,0:T(8,128)(2,1)S(1)} %slice.143), channel_id=1, source_target_pairs={{6,0},{8,2},{10,4},{12,6},{14,8},{16,10},{18,12},{20,14},{22,16},{... | collective-permute-start | bytes 663560 | tf_op jit(solution)/shard_map/ppermute | solution.py:18
  172.2 16.2 %collective-permute-start.16 = (bf16[96,1152]{1,0:T(8,128)(2,1)S(1)}, bf16[96,1152]{1,0:T(8,128)(2,1)S(1)}, u32[]{:S(2)}, u32[]{:S(2)}) collective-permute-start(bf16[96,1152]{1,0:T(8,128)(2,1)S(1)} %slice.143), channel_id=1, source_target_pairs={{8,0},{10,2},{12,4},{14,6},{16,8},{18,10},{20,12},{22,14},{24,16},... | collective-permute-start | bytes 663560 | tf_op jit(solution)/shard_map/ppermute | solution.py:18
  192.6 4.3 %copy-start.16 = (pred[9]{0:T(512)(128)(4,1)S(1)}, pred[9]{0:T(512)(128)(4,1)}, u32[]{:S(2)}) copy-start(pred[9]{0:T(512)(128)(4,1)} %compare_and_fusion) | copy-start | bytes 31
  197.2 13.2 %copy-start.4 = (bf16[1152,16]{0,1:T(8,128)(2,1)S(1)}, bf16[1152,16]{0,1:T(8,128)(2,1)}, u32[]{:S(2)}) copy-start(bf16[1152,16]{0,1:T(8,128)(2,1)} %param.13) | copy-start | bytes 110596
  197.2 13.2 %copy-start.12 = (f32[48,16]{0,1:T(8,128)S(1)}, f32[48,16]{0,1:T(8,128)}, u32[]{:S(2)}) copy-start(f32[48,16]{0,1:T(8,128)} %copy-done.11) | copy-start | bytes 9220
  197.2 13.2 %copy-start.14 = (f32[2,48,16]{1,2,0:T(8,128)S(1)}, f32[2,48,16]{1,2,0:T(8,128)}, u32[]{:S(2)}) copy-start(f32[2,48,16]{1,2,0:T(8,128)} %param.8) | copy-start | bytes 18436
  197.2 15.7 %copy-start.13 = (f32[48,16]{0,1:T(8,128)S(1)}, f32[48,16]{0,1:T(8,128)}, u32[]{:S(2)}) copy-start(f32[48,16]{0,1:T(8,128)} %get-tuple-element.35) | copy-start | bytes 9220
  211.6 3.1 %collective-permute-start.17 = (f32[48,16]{0,1:T(8,128)S(1)}, f32[48,16]{0,1:T(8,128)S(1)}, u32[]{:S(2)}, u32[]{:S(2)}) collective-permute-start(f32[48,16]{0,1:T(8,128)S(1)} %get-tuple-element.38), channel_id=1, source_target_pairs={{2,0},{4,2},{6,4},{8,6},{10,8},{12,10},{14,12},{16,14},{18,16},{20... | collective-permute-start | bytes 9224 | tf_op jit(solution)/shard_map/ppermute | solution.py:18
Sparse Core Ops, SparseCore 0:
  32.4 12.9 reduce-scatter.4
  103.4 8.2 reduce-scatter.6
  131.5 11.4 reduce-scatter.8
  200.2 8.0 reduce-scatter.10
where the time goes:
time: 224 us; the launch traced here: 222 us
  waiting for transfers between devices  72 us (32%)
  starting transfers between devices  37.1 us (17%)
  matrix products  28.9 us (13%)
  local copies, waits for them, and re-layouts  25.8 us (12%)
  blocking collectives  24.9 us (11%)
  between operations  16.6 us (7%)
  other arithmetic  16.5 us (7%)
    ppermute x18, starting transfers between devices, passed_along(): return lax.ppermute(x, axis, pairs)  37 us
    ppermute x18, waiting for transfers between devices, passed_along(): return lax.ppermute(x, axis, pairs)  32.1 us
    reduce_scatter x2, waiting for transfers between devices, local(): lax.psum_scatter(jnp.dot(spatial, spatial_exit, preferred_element_type=jn...  24.6 us
    reduce_scatter x2, waiting for transfers between devices, local(): lax.psum_scatter(jnp.dot(temporal, temporal_exit, preferred_element_type=...  15.2 us
    unnamed x67, local copies, waits for them, and re-layouts  14.3 us
    dot_general x4, matrix products, right_product(): lax.dot_general(rows, stacked, (((1,), (1,)), ((), ())), preferred_elemen...  13.5 us
    all_gather x2, blocking collectives, local(): lax.all_gather(normed_temporal, 'space', axis=0, tiled=True)  11 us
    all_gather x2, blocking collectives, local(): lax.all_gather(current.astype(jnp.bfloat16), 'space', axis=0, tiled=True)  9.56 us
  transfers between devices with their start and end apart: 22, of which 12 were waited for; matrix products, arithmetic and copies ran while one was open for 3% of the time, Pallas kernels for 0%

commit v1 on v0

v1 whole, which is shorter than its diff:
```python
import functools
import math

import jax
import jax.numpy as jnp
from jax import lax
from jax.experimental import pallas as pl
from jax.experimental.pallas import tpu as pltpu
from jax.sharding import PartitionSpec as P

HEAD = 72
FREQ = 256
STEPS = 2
REACH = 4
LEVELS = 1000
CH = 16
PIECES = 6
LANES = 128
SLOTS = 32
GROUP = 8
MIB = 1024 * 1024
F32 = jnp.float32
BF16 = jnp.bfloat16
EXACT = lax.Precision.HIGHEST


def time_features(level_values):
    times = level_values.astype(F32) / LEVELS
    half_size = FREQ // 2
    frequency = jnp.exp(-math.log(10000.0) * jnp.arange(half_size).astype(F32) / half_size)
    angles = (times * 1000.0)[:, None] * frequency[None, :]
    return jnp.concatenate([jnp.cos(angles), jnp.sin(angles)], -1).astype(BF16)


def layer_norm(values):
    average = jnp.mean(values, -1, keepdims=True)
    centred = values - average
    variance = jnp.mean(centred * centred, -1, keepdims=True)
    return centred * lax.rsqrt(variance + 1e-06)


def iota(shape, dimension):
    return lax.broadcasted_iota(jnp.int32, shape, dimension)


def ones_where(condition, dtype=BF16):
    return jnp.where(condition, 1.0, 0.0).astype(dtype)


def rows_by(left, right, precision=None):
    return lax.dot_general(
        left, right, (((1,), (1,)), ((), ())), precision=precision, preferred_element_type=F32
    )


def product(left, right, precision=None):
    return jnp.dot(left, right, precision=precision, preferred_element_type=F32)


def over(count, body):
    if count <= 16:
        for at in range(count):
            body(at)
    else:
        lax.fori_loop(0, count, lambda at, _: body(at), None)


def rows_at(at, size):
    if isinstance(at, int):
        return slice(at * size, (at + 1) * size)
    return pl.ds(pl.multiple_of(at * size, size), size)


def piece_of(mods_ref, piece, share):
    blocks = mods_ref.shape[0] // PIECES
    return jnp.concatenate([mods_ref[piece * blocks : (piece + 1) * blocks, :]] * share, 0)


def scaled(latents, cov):
    x = latents.astype(BF16).astype(F32)
    variance = jnp.sum(x * product(x, cov, EXACT), -1, keepdims=True)
    return x * lax.rsqrt(jnp.maximum(variance, 0.0) + 1e-06)


def loader_kernel(first, weights_ref, held_ref, semaphores):
    copies = [
        pltpu.make_async_copy(weights_ref.at[first + at], held_ref.at[at], semaphores.at[at])
        for at in range(held_ref.shape[0])
    ]
    for copy in copies:
        copy.start()
    for copy in copies:
        copy.wait()


def opening_kernel(
    levels_hbm, weight_hbm, latents_hbm, embed_hbm, vectors_ref, sizes_ref, packed_ref, embed_ref,
    levels_ref, weight_ref, latents_ref, semaphores,
):
    pairs = (
        (levels_hbm, levels_ref),
        (latents_hbm, latents_ref),
        (weight_hbm, weight_ref),
        (embed_hbm, embed_ref),
    )
    copies = [
        pltpu.make_async_copy(source, target, semaphores.at[at])
        for at, (source, target) in enumerate(pairs)
    ]
    for copy in copies:
        copy.start()
    copies[0].wait()
    blocks = vectors_ref.shape[0]
    shape = (blocks, FREQ // 2)
    frequency = jnp.exp(-math.log(10000.0) * iota(shape, 1).astype(F32) / (FREQ // 2))
    row = iota(shape, 0)
    level = jnp.zeros(shape, jnp.int32)
    below = jnp.zeros(shape, jnp.int32)
    for block in range(blocks):
        level = jnp.where(row == block, levels_ref[block], level)
        if block:
            below = jnp.where(row == block, levels_ref[block - 1], below)
    sizes_ref[...] = (below - level).astype(F32) / LEVELS
    angles = (level.astype(F32) / LEVELS * 1000.0) * frequency
    features = jnp.concatenate([jnp.cos(angles), jnp.sin(angles)], -1).astype(BF16)
    copies[1].wait()
    shard = latents_ref.shape[2]
    gap = jnp.zeros((CH // 2, LANES // 2 - shard), F32)
    packed = [latents_ref[0, : CH // 2], gap, latents_ref[0, CH // 2 :], gap]
    packed_ref[0] = jnp.concatenate(packed, 1)
    copies[2].wait()
    vectors_ref[...] = product(features, weight_ref[...]).astype(BF16)
    copies[3].wait()


def join_kernel(*refs):
    *parts, joined_ref = refs
    count = parts[0].shape[0]
    for at, part in enumerate(parts):
        joined_ref[at * count : (at + 1) * count] = part[...]


def basis_kernel(sources, *refs):
    vectors, refs = refs[:sources], refs[sources:]
    embed_ref, weights_ref, mods_ref, cov_ref, rows_ref, last_ref = refs
    blocks = last_ref.shape[1]
    width = weights_ref.shape[2]
    if sources == 2:
        first = lax.axis_index("space") == 0
        mine, theirs = vectors[0][...].astype(F32), vectors[1][...].astype(F32)
        lower = jnp.where(first, mine, theirs)
        upper = jnp.where(first, theirs, mine)
        for piece in range(PIECES):
            part = (lower if piece < 3 else upper)[:, piece % 3 * width : (piece % 3 + 1) * width]
            mods_ref[piece * blocks : (piece + 1) * blocks, :] = part
    else:
        mods_ref[...] = vectors[0][...]
    embed = embed_ref[...].astype(F32)
    centred = embed - jnp.mean(embed, -1, keepdims=True)
    cov_ref[...] = rows_by(centred, centred, EXACT) / width
    scale = 1.0 + mods_ref[blocks : 2 * blocks, :]
    spread = [(centred * scale[block : block + 1, :]).astype(BF16) for block in range(blocks)]
    spread = jnp.concatenate(spread + [mods_ref[0:blocks, :].astype(BF16)], 0)
    for matrix in range(3):
        through = rows_by(spread, weights_ref[matrix])
        rows_ref[matrix] = through[: blocks * CH].astype(BF16)
        last_ref[matrix] = through[blocks * CH :]


def forms_kernel(rows_ref, last_ref, scores_ref, values_ref):
    blocks = scores_ref.shape[0]
    local_width = rows_ref.shape[2]
    share = (LANES - SLOTS) // CH
    head_count = local_width // HEAD
    head_mask = iota((head_count * SLOTS, local_width), 0) // SLOTS == (
        iota((head_count * SLOTS, local_width), 1) // HEAD
    )

    def per_block(block):
        def constant(matrix, size):
            row = last_ref[matrix, pl.ds(block, 1), :]
            return jnp.where(iota((size, local_width), 0) == 0, row, 0.0).astype(BF16)

        def tiled(matrix):
            rows = rows_ref[matrix, rows_at(block, CH), :]
            return jnp.concatenate([rows] * share + [constant(matrix, SLOTS)], 0)

        query = jnp.concatenate([rows_ref[0, rows_at(block, CH), :], constant(0, SLOTS - CH)], 0)
        query = jnp.where(head_mask, jnp.concatenate([query] * head_count, 0), 0.0).astype(BF16)
        scores_ref[block] = rows_by(query, tiled(1)).astype(BF16)
        values_ref[block] = tiled(2)

    over(blocks, per_block)


def spatial_kernel(first, turned, share, *refs):
    if first:
        gathered_ref, cov_ref, scores_ref, values_ref, weights_ref, *refs = refs
    else:
        gathered_ref, own_ref, cov_ref, scores_ref, values_ref, weights_ref, *refs = refs
    if first:
        term_ref, own_ref, attended_ref, asked_ref, keys_ref, natural_ref = refs
    else:
        term_ref, attended_ref, asked_ref, keys_ref = refs
    blocks = scores_ref.shape[0]
    local_width = values_ref.shape[2]
    head_count = local_width // HEAD
    devices = lax.axis_size("queue")
    tokens = share * devices
    here = lax.axis_index("queue")
    cov = cov_ref[...]

    if first:
        parts = gathered_ref.shape[0] // blocks
        shard = tokens // parts
        base = here * parts + lax.axis_index("space") if turned else 0
        filling = jnp.zeros((share * CH - CH, tokens), BF16)
        constant = ones_where(iota((SLOTS, tokens), 0) == 0)

        def keys_of(block):
            pieces = [
                gathered_ref[jnp.bitwise_xor(base, block * parts + part)] for part in range(parts)
            ]
            top = jnp.concatenate([piece[:, :shard] for piece in pieces], 1)
            low = jnp.concatenate(
                [piece[:, LANES // 2 : LANES // 2 + shard] for piece in pieces], 1
            )
            raw = jnp.concatenate([top, low], 0)
            natural_ref[block] = raw.T
            x = raw.astype(BF16).astype(F32)
            variance = jnp.sum(x * product(cov, x, EXACT), 0, keepdims=True)
            hat = x * lax.rsqrt(jnp.maximum(variance, 0.0) + 1e-06)
            keys_ref[block] = jnp.concatenate([hat.astype(BF16), filling, constant], 0)

        over(blocks, keys_of)

        def own_of(block):
            for position in range(share):
                own_ref[pl.ds(position * blocks + block, 1), :] = natural_ref[
                    block, pl.ds(position * devices + here, 1), :
                ]

        over(blocks, own_of)
    else:
        lane = iota((devices, LANES), 1) // CH
        held = gathered_ref[...].reshape(devices * blocks, LANES)
        if turned:
            row, column = iota((devices * blocks,) * 2, 0), iota((devices * blocks,) * 2, 1)
            moved = ones_where(column == row % devices * blocks + row // devices)
            held = product(moved, held).astype(BF16)
        natural = held.reshape(blocks, devices, LANES)
        for block in range(blocks):
            keys_ref[block] = jnp.concatenate(
                [
                    jnp.where((lane == position) | (lane == share), natural[block], 0.0).astype(BF16)
                    for position in range(share)
                ],
                0,
            )

    rows = share * blocks
    hat = scaled(own_ref[...], cov).astype(BF16)
    lanes = head_count * SLOTS
    wide = product(hat, ones_where(iota((CH, lanes), 1) % SLOTS == iota((CH, lanes), 0)))
    wide = jnp.where(iota((rows, lanes), 1) % SLOTS == CH, 1.0, wide).astype(BF16)
    row, column = iota((blocks * 8, rows), 0), iota((blocks * 8, rows), 1)
    moved = ones_where((row % 8 == column // blocks) & (row // 8 == column % blocks))
    asked_ref[...] = product(moved, wide)
    asked_mask = iota((head_count * 8, lanes), 0) // 8 == iota((head_count * 8, lanes), 1) // SLOTS
    head_of = iota((8, local_width), 1) // HEAD

    def asked_of(block):
        asked = jnp.concatenate([asked_ref[rows_at(block, 8), :]] * head_count, 0)
        return jnp.where(asked_mask, asked, 0.0).astype(BF16)

    def softmax(scores):
        scores = scores * (1.0 / math.sqrt(HEAD))
        raised = jnp.exp(scores - jnp.max(scores, -1, keepdims=True))
        return (raised / jnp.sum(raised, -1, keepdims=True)).astype(BF16)

    def attend(group):
        members = [group * GROUP + at for at in range(GROUP)]
        queries = [product(asked_of(block), scores_ref[block]).astype(BF16) for block in members]
        meet = product if first else rows_by
        scores = [meet(query, keys_ref[block]) for query, block in zip(queries, members)]
        shares = [softmax(score) for score in scores]
        mix = rows_by if first else product
        mixed = [mix(part, keys_ref[block]).astype(BF16) for part, block in zip(shares, members)]
        mixed = [product(part, values_ref[block]) for part, block in zip(mixed, members)]
        for part, block in zip(mixed, members):
            total = part[0:8]
            for head in range(1, head_count):
                total = jnp.where(head_of == head, part[head * 8 : (head + 1) * 8], total)
            attended_ref[rows_at(block, 8), :] = total

    over(blocks // GROUP, attend)
    row, column = iota((rows, blocks * 8), 0), iota((rows, blocks * 8), 1)
    moved = ones_where((row // blocks == column % 8) & (row % blocks == column // 8))
    attended = product(moved, attended_ref[...].astype(BF16)).astype(BF16)
    term_ref[...] = product(attended, weights_ref[3]).astype(BF16)


def summed(terms):
    total = terms[0][...].astype(F32)
    for term in terms[1:]:
        total = total + term[...].astype(F32)
    return total


def own_half(rows):
    count = rows.shape[0] // 2
    return jnp.where(lax.axis_index("space") == 0, rows[:count], rows[count:])


def attend(half, blocks, query_ref, keys_ref, values_ref, weights_ref):
    rows = query_ref.shape[0]
    local_width = query_ref.shape[1]
    head_count = local_width // HEAD
    kept = slice(0, rows)
    if half is not None:
        rows = rows // 2
        kept = pl.ds(pl.multiple_of(half * rows, rows), rows)
    query = query_ref[kept, :]
    head_of = iota((rows, local_width), 1) // HEAD
    asked = [jnp.where(head_of == head, query, 0.0).astype(BF16) for head in range(head_count)]
    scores = rows_by(jnp.concatenate(asked, 0), keys_ref[kept, :]) * (1.0 / math.sqrt(HEAD))
    row, column = iota(scores.shape, 0) % rows, iota(scores.shape, 1)
    near = (row // blocks == column // blocks) & (jnp.abs(row - column) <= REACH)
    scores = jnp.where(near, scores, -1e30)
    raised = jnp.exp(scores - jnp.max(scores, -1, keepdims=True))
    shares = (raised / jnp.sum(raised, -1, keepdims=True)).astype(BF16)
    mixed = product(shares, values_ref[kept, :])
    total = mixed[0:rows]
    for head in range(1, head_count):
        total = jnp.where(head_of == head, mixed[head * rows : (head + 1) * rows], total)
    return product(total.astype(BF16), weights_ref[3]).astype(BF16)


def temporal_kernel(share, halved, term_count, own_ref, mods_ref, embed_ref, weights_ref, *refs):
    terms, (stream_ref, term_ref, query_ref, keys_ref, values_ref) = (
        refs[:term_count],
        refs[term_count:],
    )
    blocks = mods_ref.shape[0] // PIECES
    stream = product(own_ref[...].astype(BF16), embed_ref[...])
    stream = stream + piece_of(mods_ref, 2, share) * summed(terms)
    stream_ref[...] = own_half(stream) if halved else stream
    normed = layer_norm(stream) * (1.0 + piece_of(mods_ref, 4, share)) + piece_of(mods_ref, 3, share)
    normed = normed.astype(BF16)
    query_ref[...] = rows_by(normed, weights_ref[0]).astype(BF16)
    keys_ref[...] = rows_by(normed, weights_ref[1]).astype(BF16)
    values_ref[...] = rows_by(normed, weights_ref[2]).astype(BF16)
    half = 1 - lax.axis_index("space") if halved else None
    term_ref[...] = attend(half, blocks, query_ref, keys_ref, values_ref, weights_ref)


def kept_kernel(blocks, query_ref, keys_ref, values_ref, weights_ref, term_ref):
    half = lax.axis_index("space")
    term_ref[...] = attend(half, blocks, query_ref, keys_ref, values_ref, weights_ref)


def side_by_side(rows, blocks, share):
    parts = [rows[position * blocks : (position + 1) * blocks] for position in range(share)]
    return jnp.concatenate(parts + [jnp.zeros((blocks, LANES - share * CH), rows.dtype)], 1)


def final_kernel(share, halved, term_count, own_ref, stream_ref, mods_ref, final_ref, sizes_ref, *refs):
    terms, refs = refs[:term_count], refs[term_count:]
    blocks = mods_ref.shape[0] // PIECES
    rows = share * blocks
    own = own_half(own_ref[...]) if halved else own_ref[...]
    stream = stream_ref[...] + piece_of(mods_ref, 5, share) * summed(terms)
    velocity = rows_by(layer_norm(stream).astype(BF16), final_ref[...])
    sizes = jnp.concatenate([sizes_ref[:, :CH]] * share, 0)
    updated = own + sizes * velocity
    moved = jnp.concatenate([updated[1:], updated[:1]], 0)
    return blocks, rows, velocity, moved, refs


def between_kernel(share, term_count, iteration, noise_count, *refs):
    blocks, rows, velocity, moved, refs = final_kernel(share, False, term_count, *refs)
    noises, (cov_ref, velocity_ref, next_ref, sent_ref, noise_ref) = (
        refs[:noise_count],
        refs[noise_count:],
    )
    velocity_ref[...] = velocity
    devices = lax.axis_size("queue")
    here = lax.axis_index("queue")
    if noise_count == 2:
        mine, theirs = noises[0][iteration], noises[1][iteration]
        first = lax.axis_index("space") == 0
        noise = jnp.concatenate(
            [jnp.where(first, mine, theirs), jnp.where(first, theirs, mine)], 1
        )
    else:
        noise = noises[0][iteration]
    noise_ref[...] = noise.T
    next_ref[...] = moved
    for position in range(share):
        next_ref[(position + 1) * blocks - 1 : (position + 1) * blocks, :] = noise_ref[
            pl.ds(position * devices + here, 1), :
        ]
    hat = side_by_side(scaled(next_ref[...], cov_ref[...]), blocks, share)
    hat = jnp.where(iota((blocks, LANES), 1) == share * CH, 1.0, hat)
    sent_ref[...] = jnp.broadcast_to(hat.astype(BF16), sent_ref.shape)


def ending_kernel(share, halved, term_count, *refs):
    blocks, rows, velocity, moved, refs = final_kernel(share, halved, term_count, *refs)
    *earlier, sent_ref = refs
    pick = own_half if halved else lambda rows: rows
    sent_ref[...] = jnp.zeros_like(sent_ref)
    for at, values in enumerate([pick(ref[...]) for ref in earlier] + [velocity, moved]):
        wide = side_by_side(values, blocks, share)
        sent_ref[:, at : at + 1, :] = wide.reshape(blocks, 1, LANES)


def finish_kernel(share, arrived_ref, noise_ref, queue_ref, velocities_ref):
    devices = arrived_ref.shape[0]
    outs = []
    for at in range(STEPS + 1):
        turned = arrived_ref[:, at : at + 1, :].reshape(devices, LANES).T
        parts = [turned[position * CH : (position + 1) * CH] for position in range(share)]
        outs.append(jnp.concatenate(parts, 1))
    for step in range(STEPS):
        velocities_ref[step, 0] = outs[step]
    last = lax.axis_index("queue") == devices - 1
    queue_ref[0] = jnp.where(last, noise_ref[STEPS - 1], outs[STEPS])


def small(limit):
    return pltpu.CompilerParams(vmem_limit_bytes=limit * MIB)


def in_hbm(operands):
    return [pltpu.with_memory_space_constraint(operand, pltpu.HBM) for operand in operands]


def load(weights, first, count):
    shape = (count,) + weights.shape[1:]
    return pl.pallas_call(
        functools.partial(loader_kernel, first),
        out_shape=pltpu.VMEM(shape, weights.dtype),
        in_specs=[pl.BlockSpec(memory_space=pltpu.HBM)],
        out_specs=pl.BlockSpec(memory_space=pltpu.VMEM),
        scratch_shapes=[pltpu.SemaphoreType.DMA((count,))],
        compiler_params=small(1),
        cost_estimate=pl.CostEstimate(
            flops=0, bytes_accessed=2 * math.prod(shape), transcendentals=0
        ),
    )(*in_hbm([weights]))


def call(kernel, outs, operands, scratch=(), limit=8, held=True, from_hbm=()):
    specs = [pl.BlockSpec(memory_space=pltpu.VMEM)] * len(operands)
    specs += [pl.BlockSpec(memory_space=pltpu.HBM)] * len(from_hbm)
    if held:
        operands = [pltpu.with_memory_space_constraint(operand, pltpu.VMEM) for operand in operands]
    place = pltpu.VMEM if held else jax.ShapeDtypeStruct
    return pl.pallas_call(
        kernel,
        out_shape=[place(shape, dtype) for shape, dtype in outs],
        in_specs=specs,
        out_specs=[pl.BlockSpec(memory_space=pltpu.VMEM)] * len(outs),
        scratch_shapes=list(scratch),
        compiler_params=small(limit),
    )(*operands, *in_hbm(from_hbm))


def local(
    latents, fresh_noise, levels, modulation_weight, embed_weight, attention_weights, final_weight
):
    devices = lax.axis_size("queue")
    space_count = lax.axis_size("space")
    blocks = devices
    width = embed_weight.shape[1]
    local_width = attention_weights.shape[1]
    head_count = local_width // HEAD
    shard = latents.shape[1]
    tokens = shard * space_count
    share = tokens // devices
    rows = share * blocks
    wide_rows = share * CH + SLOTS
    run = functools.partial(call, limit=12 if rows <= 128 else 40)
    final_rows = final_weight.T
    latents = jnp.swapaxes(latents, 1, 2)
    fresh_noise = jnp.swapaxes(fresh_noise, 1, 2)

    def over_space(x):
        if space_count == 2:
            return [x, lax.ppermute(x, "space", [(0, 1), (1, 0)])]
        gathered = lax.all_gather(x, "space", axis=0, tiled=False)
        return [jnp.sum(gathered.astype(F32), 0)]

    def apart(x, mask):
        count = devices * space_count
        return lax.ppermute(x, ("queue", "space"), [(i, i ^ mask) for i in range(count)])

    def joined(*parts):
        shape = (len(parts) * parts[0].shape[0],) + parts[0].shape[1:]
        return run(join_kernel, [(shape, parts[0].dtype)], list(parts))[0]

    def after(x, *others):
        return lax.optimization_barrier((x, *others))[0]

    def basis(vectors, held):
        return run(
            functools.partial(basis_kernel, len(vectors)),
            [
                ((PIECES * blocks, width), F32),
                ((CH, CH), F32),
                ((3, blocks * CH, local_width), BF16),
                ((3, blocks, local_width), F32),
            ],
            [*vectors, embed_weight, held],
        )

    def forms(seen):
        return run(
            forms_kernel,
            [
                ((blocks, head_count * SLOTS, wide_rows), BF16),
                ((blocks, wide_rows, local_width), BF16),
            ],
            list(seen),
        )

    paired = space_count == 2 and devices == 16
    if paired:
        operands = (levels, modulation_weight, latents, embed_weight)
        vectors, sizes, packed, embed_weight = run(
            opening_kernel,
            [
                ((blocks, modulation_weight.shape[1]), BF16),
                ((blocks, LANES), F32),
                ((1, CH // 2, LANES), F32),
                (embed_weight.shape, BF16),
            ],
            [],
            [
                pltpu.SMEM(levels.shape, levels.dtype),
                pltpu.VMEM(modulation_weight.shape, modulation_weight.dtype),
                pltpu.VMEM(latents.shape, latents.dtype),
                pltpu.SemaphoreType.DMA((len(operands),)),
            ],
            from_hbm=operands,
        )
        vectors = over_space(vectors)
        spatial_weights = load(after(attention_weights, packed), 0, 4)
        gathered = joined(packed, after(apart(packed, 1), spatial_weights))
        arrivals = [apart(gathered, mask) for mask in (2, 4, 6)]
        mods, cov, *seen = basis(vectors, spatial_weights)
        arrivals[-1] = after(arrivals[-1], *seen)
        gathered = joined(gathered, *arrivals)
        arrivals = [apart(gathered, mask) for mask in (8, 16, 24)]
        scores, values = forms(seen)
        arrivals[-1] = after(arrivals[-1], scores)
        gathered = [joined(gathered, *arrivals)]
    else:
        below = jnp.concatenate([jnp.zeros((1,), levels.dtype), levels[:-1]])
        sizes = jnp.broadcast_to(((below - levels).astype(F32) / LEVELS)[:, None], (blocks, LANES))
        part = product(time_features(levels), modulation_weight)
        part = lax.all_gather(part, "space", axis=1, tiled=True).reshape(blocks, PIECES, width)
        vectors = [jnp.swapaxes(part, 0, 1).reshape(PIECES * blocks, width)]
        gap = jnp.zeros((CH // 2, LANES // 2 - shard), F32)
        packed = jnp.concatenate([latents[0, : CH // 2], gap, latents[0, CH // 2 :], gap], 1)
        noises = [lax.all_gather(fresh_noise, "space", axis=2, tiled=True)]
        gathered = lax.all_gather(packed, ("queue", "space"), axis=0, tiled=False)
        gathered = [gathered.reshape(devices * space_count, CH // 2, LANES)]
        spatial_weights = load(attention_weights, 0, 4)
        mods, cov, *seen = basis(vectors, spatial_weights)
        scores, values = forms(seen)
    temporal_weights = None
    own = None
    velocities = []
    for iteration in range(STEPS):
        first = iteration == 0
        outs = [((rows, width), BF16)]
        scratch = [
            pltpu.VMEM((blocks * 8, local_width), F32),
            pltpu.VMEM((blocks * 8, head_count * SLOTS), F32),
            pltpu.VMEM((blocks, wide_rows, tokens) if first else (blocks, tokens, LANES), BF16),
        ]
        if first:
            outs.append(((rows, CH), F32))
            scratch.append(pltpu.VMEM((blocks, tokens, CH), F32))
        spatial_term, *new = run(
            functools.partial(spatial_kernel, first, paired, share),
            outs,
            [*gathered, *([] if first else [own]), cov, scores, values, spatial_weights],
            scratch,
        )
        if first:
            (own,) = new
            held, noise, spatial_term = lax.optimization_barrier(
                (attention_weights, fresh_noise, spatial_term)
            )
            temporal_weights = load(held, 4, 4)
            if paired:
                noises = over_space(noise)
        spatial_terms = over_space(spatial_term)
        if first and paired:
            spatial_terms[-1] = after(spatial_terms[-1], noises[-1])
        last = iteration == STEPS - 1
        halved = last and paired
        held_rows = rows // 2 if halved else rows
        asked = [((rows, local_width), BF16)] * 3
        stream, temporal_term, *asked = run(
            functools.partial(temporal_kernel, share, halved, len(spatial_terms)),
            [((held_rows, width), F32), ((held_rows, width), BF16)] + (asked if halved else []),
            [own, mods, embed_weight, temporal_weights, *spatial_terms],
            [] if halved else [pltpu.VMEM(shape, dtype) for shape, dtype in asked],
        )
        temporal_terms = over_space(temporal_term)
        if halved:
            temporal_terms[:1] = run(
                functools.partial(kept_kernel, blocks),
                [((held_rows, width), BF16)],
                [*asked, temporal_weights],
            )
        operands = [own, stream, mods, final_rows, sizes, *temporal_terms]
        if not last:
            velocity, own, sent = run(
                functools.partial(
                    between_kernel, share, len(temporal_terms), iteration, len(noises)
                ),
                [
                    ((rows, CH), F32),
                    ((rows, CH), F32),
                    ((devices if paired else 1, blocks, LANES), BF16),
                ],
                operands + [*noises, cov],
                [pltpu.VMEM((tokens, CH), F32)],
            )
            velocities.append(velocity)
            if paired:
                gathered = [lax.all_to_all(sent, "queue", 0, 0, tiled=True)]
            else:
                gathered = lax.all_gather(sent[0], "queue", axis=0, tiled=False)
                gathered = [jnp.swapaxes(gathered, 0, 1).reshape(devices * blocks, LANES)]
        else:
            (sent,) = run(
                functools.partial(
                    ending_kernel, share // 2 if halved else share, halved, len(temporal_terms)
                ),
                [((blocks, 8, LANES), F32)],
                operands + velocities,
            )
    arrived = lax.all_to_all(sent, "queue", 0, 0, tiled=True)
    if paired:
        queue_out, velocity_out = run(
            functools.partial(finish_kernel, share // 2),
            [((1, CH, shard), F32), ((STEPS, 1, CH, shard), F32)],
            [arrived, fresh_noise],
            held=False,
        )
    else:
        arrived = arrived[:, : STEPS + 1, : share * CH].reshape(devices, STEPS + 1, share, CH)
        arrived = arrived.transpose(1, 3, 2, 0).reshape(STEPS + 1, CH, tokens)
        arrived = lax.dynamic_slice_in_dim(arrived, lax.axis_index("space") * shard, shard, 2)
        velocity_out = arrived[:STEPS, None]
        last = lax.axis_index("queue") == devices - 1
        queue_out = jnp.where(last, fresh_noise[STEPS - 1], arrived[STEPS])[None]
    return jnp.swapaxes(queue_out, 1, 2), jnp.swapaxes(velocity_out, 2, 3)


def solution(mesh):
    in_specs = (
        P("queue", "space", None),
        P(None, "space", None),
        P(),
        P(None, "space"),
        P(),
        P(None, "space", None),
        P(),
    )
    out_specs = (P("queue", "space", None), P(None, "queue", "space", None))
    return jax.shard_map(local, mesh=mesh, in_specs=in_specs, out_specs=out_specs, check_vma=False)
```

time: 224 us -> 80.6 us (0.36)
  waiting for transfers between devices: 72 us -> 18.3 us
  matrix products: 28.9 us -> 0 us
  Pallas kernels: 0 us -> 25.9 us
  local copies, waits for them, and re-layouts: 25.8 us -> 0.01 us
  starting transfers between devices: 37.1 us -> 15.5 us
  other arithmetic: 16.5 us -> 0 us
  between operations: 16.6 us -> 0.79 us
  blocking collectives: 24.9 us -> 19.9 us
    reduce_scatter x4 -> x0, waiting for transfers between devices: 39.9 us -> none  [the longest x2 24.6 us: local(): lax.psum_scatter(jnp.dot(spatial, spatial_exit, preferred_element_type=jn...]
    dot_general x17 -> x0, matrix products: 28.2 us -> none  [the longest x4 13.5 us: right_product(): lax.dot_general(rows, stacked, (((1,), (1,)), ((), ())), preferred_elemen...]
    pallas_call x0 -> x16, Pallas kernels: none -> 25.9 us  [the longest x14 20.8 us: call(): pl.pallas_call(kernel, out_shape=[place(shape, dtype) for shape, dtype in...]
    all_gather x5 -> x0, blocking collectives: 24.9 us -> none  [the longest x2 11 us: local(): lax.all_gather(normed_temporal, 'space', axis=0, tiled=True)]
    ppermute x18 -> x13, starting transfers between devices: 37 us -> 15.5 us  [the longest x6 9.12 us: over_space(): return [x, lax.ppermute(x, 'space', [(0, 1), (1, 0)])]]
    all_to_all x0 -> x2, blocking collectives: none -> 19.9 us  [the longest x1 10.4 us: local(): gathered = [lax.all_to_all(sent, 'queue', 0, 0, tiled=True)]]
    unnamed x67 -> x4, local copies, waits for them, and re-layouts: 14.3 us -> 0.01 us
    ppermute x18 -> x13, waiting for transfers between devices: 32.1 us -> 18.3 us  [the longest x6 14.9 us: over_space(): return [x, lax.ppermute(x, 'space', [(0, 1), (1, 0)])]]
  transfers between devices with their start and end apart: 22 -> 13, of which waited for: 12 -> 6; matrix products, arithmetic and copies ran while one was open for 3% -> 0% of each run, Pallas kernels for 0% -> 12%
where the time goes in v1:
time: 80.6 us; the launch traced here: 80.4 us
  Pallas kernels  25.9 us (32%)
  blocking collectives  19.9 us (25%)
  waiting for transfers between devices  18.3 us (23%)
  starting transfers between devices  15.5 us (19%)
    pallas_call x14, Pallas kernels, call(): pl.pallas_call(kernel, out_shape=[place(shape, dtype) for shape, dtype in...  20.8 us
    ppermute x6, waiting for transfers between devices, over_space(): return [x, lax.ppermute(x, 'space', [(0, 1), (1, 0)])]  14.9 us
    all_to_all x1, blocking collectives, local(): gathered = [lax.all_to_all(sent, 'queue', 0, 0, tiled=True)]  10.4 us
    all_to_all x1, blocking collectives, local(): arrived = lax.all_to_all(sent, 'queue', 0, 0, tiled=True)  9.48 us
    ppermute x6, starting transfers between devices, over_space(): return [x, lax.ppermute(x, 'space', [(0, 1), (1, 0)])]  9.12 us
    ppermute x7, starting transfers between devices, apart(): lax.ppermute(x, ('queue', 'space'), [(i, i ^ mask) for i in range(count)])  6.39 us
    pallas_call x2, Pallas kernels, load(): pl.pallas_call(functools.partial(loader_kernel, first), out_shape=pltpu.V...  5.11 us
    ppermute x7, waiting for transfers between devices, apart(): lax.ppermute(x, ('queue', 'space'), [(i, i ^ mask) for i in range(count)])  3.41 us
  transfers between devices with their start and end apart: 13, of which 6 were waited for; matrix products, arithmetic and copies ran while one was open for 0% of the time, Pallas kernels for 12%

profile of v1, /device:TPU:0, one launch (start us, length us, event | category | flops | bytes accessed | tf_op | source)
XLA Modules:
  0.0 80.4 jit_solution(4585236253043553322)
XLA Ops:
  0.6 1.9 %shard_map.86 = (bf16[16,3456]{1,0:T(8,128)(2,1)S(1)}, f32[16,128]{1,0:T(8,128)S(1)}, f32[1,8,128]{2,1,0:T(8,128)S(1)}, bf16[16,1152]{1,0:T(8,128)(2,1)S(1)}) custom-call(s32[16]{0:T(128)} %levels_hbm.1, bf16[256,3456]{1,0:T(8,128)(2,1)} %weight_hbm.1, f32[1,16,48]{2,1,0:T(8,128)} %bitcast.10, bf16[16,1152]{1,0:T(8,128)(2,1)} %embed_hbm.1), custom_call_target="tpu_custom_call" | custom-call | tf_op jit(solution)/shard_map/pallas_call | solution.py:460
  2.5 3.0 %collective-permute-start.4 = (bf16[16,3456]{1,0:T(8,128)(2,1)S(1)}, bf16[16,3456]{1,0:T(8,128)(2,1)S(1)}, u32[]{:S(2)}, u32[]{:S(2)}) collective-permute-start(bf16[16,3456]{1,0:T(8,128)(2,1)S(1)} %get-tuple-element.37.refs_0_), channel_id=1, source_target_pairs={{0,1},{1,0},{2,3},{3,2},{4,5},{5,4},{6,7},{7,6},{8,9},{9,8},{10,11... | collective-permute-start | bytes 331784 | tf_op jit(solution)/shard_map/ppermute | solution.py:491
  5.5 0.1 collective-permute-start
  5.6 2.6 %shard_map.87.refs_3_.refs_4_.refs_5_ = bf16[4,576,1152]{2,1,0:T(8,128)(2,1)S(1)} custom-call(bf16[8,576,1152]{2,1,0:T(8,128)(2,1)} %weights_ref.1), custom_call_target="tpu_custom_call" | custom-call | bytes 5308416 | tf_op jit(solution)/shard_map/pallas_call | solution.py:441
  8.2 1.0 %collective-permute-done.refs_1_ = f32[1,8,128]{2,1,0:T(8,128)S(1)} collective-permute-done((f32[1,8,128]{2,1,0:T(8,128)S(1)}, f32[1,8,128]{2,1,0:T(8,128)S(1)}, u32[]{:S(2)}, u32[]{:S(2)}) %collective-permute-start) | collective-permute-done | bytes 4128 | tf_op jit(solution)/shard_map/ppermute | solution.py:497
  9.1 0.0 collective-permute-start.3
  9.1 1.6 %collective-permute-start.2 = (f32[2,8,128]{2,1,0:T(8,128)S(1)}, f32[2,8,128]{2,1,0:T(8,128)S(1)}, u32[]{:S(2)}, u32[]{:S(2)}) collective-permute-start(f32[2,8,128]{2,1,0:T(8,128)S(1)} %shard_map.88.refs_0_), channel_id=1, source_target_pairs={{0,4},{1,5},{2,6},{3,7},{4,0},{5,1},{6,2},{7,3},{8,12},{9,13},{10,... | collective-permute-start | bytes 24584 | tf_op jit(solution)/shard_map/ppermute | solution.py:497
  10.7 0.3 collective-permute-start.1
  11.0 0.0 collective-permute-done.4.refs_1_
  11.0 2.0 %shard_map.89 = (f32[96,1152]{1,0:T(8,128)S(1)}, f32[16,16]{1,0:T(8,128)S(1)}, bf16[3,256,576]{2,1,0:T(8,128)(2,1)S(1)}, f32[3,16,576]{2,1,0:T(8,128)S(1)}) custom-call(bf16[16,3456]{1,0:T(8,128)(2,1)S(1)} %get-tuple-element.37.refs_0_, bf16[16,3456]{1,0:T(8,128)(2,1)S(1)} %collective-permute-done.4.refs_1_, ...), custom_call_target="tpu_custom_call" | custom-call | tf_op jit(solution)/shard_map/pallas_call | solution.py:460
  13.0 0.0 copy-start.1
  13.0 0.0 collective-permute-done.3.refs_3_
  13.1 0.0 collective-permute-done.2.refs_2_
  13.1 0.0 collective-permute-done.1.refs_1_
  13.1 3.7 %collective-permute-start.7 = (f32[8,8,128]{2,1,0:T(8,128)S(1)}, f32[8,8,128]{2,1,0:T(8,128)S(1)}, u32[]{:S(2)}, u32[]{:S(2)}) collective-permute-start(f32[8,8,128]{2,1,0:T(8,128)S(1)} %shard_map.90.refs_0_), channel_id=1, source_target_pairs={{0,24},{1,25},{2,26},{3,27},{4,28},{5,29},{6,30},{7,31},{8,16},{9,... | collective-permute-start | bytes 98312 | tf_op jit(solution)/shard_map/ppermute | solution.py:497
  16.8 0.0 collective-permute-start.6
  16.8 0.8 collective-permute-start.5
  17.5 1.6 %shard_map.91 = (bf16[16,256,128]{2,1,0:T(8,128)(2,1)S(1)}, bf16[16,128,576]{2,1,0:T(8,128)(2,1)S(1)}) custom-call(bf16[3,256,576]{2,1,0:T(8,128)(2,1)S(1)} %get-tuple-element.39.rows_ref, f32[3,16,576]{2,1,0:T(8,128)S(1)} %get-tuple-element.40.last_ref), custom_call_target="tpu_custom_call" | custom-call | tf_op jit(solution)/shard_map/pallas_call | solution.py:460
  19.1 0.0 collective-permute-done.7.refs_3_
  19.1 2.4 %collective-permute-done.6.refs_2_ = f32[8,8,128]{2,1,0:T(8,128)S(1)} collective-permute-done((f32[8,8,128]{2,1,0:T(8,128)S(1)}, f32[8,8,128]{2,1,0:T(8,128)S(1)}, u32[]{:S(2)}, u32[]{:S(2)}) %collective-permute-start.6) | collective-permute-done | bytes 32800 | tf_op jit(solution)/shard_map/ppermute | solution.py:497
  21.6 0.0 collective-permute-done.5.refs_1_
  21.6 3.4 %shard_map.93 = (bf16[96,1152]{1,0:T(8,128)(2,1)S(1)}, f32[96,16]{1,0:T(8,128)S(1)}) custom-call(f32[32,8,128]{2,1,0:T(8,128)S(1)} %shard_map.92.refs_0_, f32[16,16]{1,0:T(8,128)S(1)} %get-tuple-element.44.refs_1_.refs_9_.refs_2_, bf16[16,256,128]{2,1,0:T(8,128)(2,1)S(1)} %get-tuple-element.42.refs_2_.refs_3_, ...), custom_call_target="tpu_custom_call" | custom-call | tf_op jit(solution)/shard_map/pallas_call | solution.py:460
  25.0 1.3 %collective-permute-start.8 = (bf16[96,1152]{1,0:T(8,128)(2,1)S(1)}, bf16[96,1152]{1,0:T(8,128)(2,1)S(1)}, u32[]{:S(2)}, u32[]{:S(2)}) collective-permute-start(bf16[96,1152]{1,0:T(8,128)(2,1)S(1)} %get-tuple-element.50.refs_0_), channel_id=1, source_target_pairs={{0,1},{1,0},{2,3},{3,2},{4,5},{5,4},{6,7},{7,6},{8,9},{9,8},{10,11... | collective-permute-start | bytes 663560 | tf_op jit(solution)/shard_map/ppermute | solution.py:491
  26.3 0.0 copy-done.1
  26.3 0.7 collective-permute-start.9
  27.1 2.6 %shard_map.94.weights_ref = bf16[4,576,1152]{2,1,0:T(8,128)(2,1)S(1)} custom-call(bf16[8,576,1152]{2,1,0:T(8,128)(2,1)} %weights_ref.1), custom_call_target="tpu_custom_call" | custom-call | bytes 5308416 | tf_op jit(solution)/shard_map/pallas_call | solution.py:441
  29.6 0.0 copy-start
  29.6 2.2 %collective-permute-done.9.refs_8_ = f32[2,16,48]{2,1,0:T(8,128)S(1)} collective-permute-done((f32[2,16,48]{2,1,0:T(8,128)S(1)}, f32[2,16,48]{2,1,0:T(8,128)S(1)}, u32[]{:S(2)}, u32[]{:S(2)}) %collective-permute-start.9) | collective-permute-done | bytes 6176 | tf_op jit(solution)/shard_map/ppermute | solution.py:491
  31.9 0.0 collective-permute-done.8.refs_1_
  31.9 3.3 %shard_map.95 = (f32[96,1152]{1,0:T(8,128)S(1)}, bf16[96,1152]{1,0:T(8,128)(2,1)S(1)}) custom-call(f32[96,16]{1,0:T(8,128)S(1)} %get-tuple-element.46.own_ref.refs_0_, f32[96,1152]{1,0:T(8,128)S(1)} %get-tuple-element.47.mods_ref.refs_2_, bf16[16,1152]{1,0:T(8,128)(2,1)S(1)} %get-tuple-element.38.refs_2_.embed_ref, ...), custom_call_target="tpu_custom_call" | custom-call | tf_op jit(solution)/shard_map/pallas_call | solution.py:460
  35.1 1.3 %collective-permute-start.10 = (bf16[96,1152]{1,0:T(8,128)(2,1)S(1)}, bf16[96,1152]{1,0:T(8,128)(2,1)S(1)}, u32[]{:S(2)}, u32[]{:S(2)}) collective-permute-start(bf16[96,1152]{1,0:T(8,128)(2,1)S(1)} %get-tuple-element.55.refs_5_), channel_id=1, source_target_pairs={{0,1},{1,0},{2,3},{3,2},{4,5},{5,4},{6,7},{7,6},{8,9},{9,8},{10,11... | collective-permute-start | bytes 663560 | tf_op jit(solution)/shard_map/ppermute | solution.py:491
  36.5 4.7 %collective-permute-done.10.refs_6_ = bf16[96,1152]{1,0:T(8,128)(2,1)S(1)} collective-permute-done((bf16[96,1152]{1,0:T(8,128)(2,1)S(1)}, bf16[96,1152]{1,0:T(8,128)(2,1)S(1)}, u32[]{:S(2)}, u32[]{:S(2)}) %collective-permute-start.10) | collective-permute-done | bytes 221216 | tf_op jit(solution)/shard_map/ppermute | solution.py:491
  41.1 0.0 copy-done
  41.1 0.8 %shard_map.96 = (f32[96,16]{1,0:T(8,128)S(1)}, f32[96,16]{1,0:T(8,128)S(1)}, bf16[16,16,128]{2,1,0:T(8,128)(2,1)S(1)}) custom-call(f32[96,16]{1,0:T(8,128)S(1)} %get-tuple-element.46.own_ref.refs_0_, f32[96,1152]{1,0:T(8,128)S(1)} %get-tuple-element.53.refs_1_, f32[96,1152]{1,0:T(8,128)S(1)} %get-tuple-element.47.mods_ref.refs_2_, ...), custom_call_target="tpu_custom_call" | custom-call | tf_op jit(solution)/shard_map/pallas_call | solution.py:460
  42.0 10.4 %all_to_all.10.refs_0_ = bf16[16,16,128]{2,1,0:T(8,128)(2,1)S(1)} all-to-all(bf16[16,16,128]{2,1,0:T(8,128)(2,1)S(1)} %get-tuple-element.57), channel_id=1, replica_groups=mesh['queue'=16,'space'=2] {'queue'}, dimensions={0} | all-to-all | bytes 131072 | tf_op jit(solution)/shard_map/all_to_all | solution.py:637
  52.4 2.8 %shard_map.97.refs_0_ = bf16[96,1152]{1,0:T(8,128)(2,1)S(1)} custom-call(bf16[16,16,128]{2,1,0:T(8,128)(2,1)S(1)} %all_to_all.10.refs_0_, f32[96,16]{1,0:T(8,128)S(1)} %get-tuple-element.56.refs_1_.own_ref.refs_0_, f32[16,16]{1,0:T(8,128)S(1)} %get-tuple-element.44.refs_1_.refs_9_.refs_2_, bf16[16,256,128]{2,1,0:T(8,128)(2,1)S(1)} %get-tuple-element.42.refs_2_.refs_3_, ...), custom_call_target="tpu_custom_call" | custom-call | tf_op jit(solution)/shard_map/pallas_call | solution.py:460
  55.2 1.4 %collective-permute-start.11 = (bf16[96,1152]{1,0:T(8,128)(2,1)S(1)}, bf16[96,1152]{1,0:T(8,128)(2,1)S(1)}, u32[]{:S(2)}, u32[]{:S(2)}) collective-permute-start(bf16[96,1152]{1,0:T(8,128)(2,1)S(1)} %shard_map.97.refs_0_), channel_id=1, source_target_pairs={{0,1},{1,0},{2,3},{3,2},{4,5},{5,4},{6,7},{7,6},{8,9},{9,8},{10,11... | collective-permute-start | bytes 663560 | tf_op jit(solution)/shard_map/ppermute | solution.py:491
  56.6 5.6 %collective-permute-done.11.refs_1_ = bf16[96,1152]{1,0:T(8,128)(2,1)S(1)} collective-permute-done((bf16[96,1152]{1,0:T(8,128)(2,1)S(1)}, bf16[96,1152]{1,0:T(8,128)(2,1)S(1)}, u32[]{:S(2)}, u32[]{:S(2)}) %collective-permute-start.11) | collective-permute-done | bytes 221216 | tf_op jit(solution)/shard_map/ppermute | solution.py:491
  62.2 2.6 %shard_map.98 = (f32[48,1152]{1,0:T(8,128)S(1)}, bf16[48,1152]{1,0:T(8,128)(2,1)S(1)}, bf16[96,576]{1,0:T(8,128)(2,1)S(1)}, bf16[96,576]{1,0:T(8,128)(2,1)S(1)}, bf16[96,576]{1,0:T(8,128)(2,1)S(1)}) custom-call(f32[96,16]{1,0:T(8,128)S(1)} %get-tuple-element.56.refs_1_.own_ref.refs_0_, f32[96,1152]{1,0:T(8,128)S(1)} %get-tuple-element.47.mods_ref.refs_2_, ...), custom_call_target="tpu_custom_call" | custom-call | tf_op jit(solution)/shard_map/pallas_call | solution.py:460
  64.9 1.3 %collective-permute-start.12 = (bf16[48,1152]{1,0:T(8,128)(2,1)S(1)}, bf16[48,1152]{1,0:T(8,128)(2,1)S(1)}, u32[]{:S(2)}, u32[]{:S(2)}) collective-permute-start(bf16[48,1152]{1,0:T(8,128)(2,1)S(1)} %get-tuple-element.62), channel_id=1, source_target_pairs={{0,1},{1,0},{2,3},{3,2},{4,5},{5,4},{6,7},{7,6},{8,9},{9,8},{10,11... | collective-permute-start | bytes 331784 | tf_op jit(solution)/shard_map/ppermute | solution.py:491
  66.2 1.1 %shard_map.99.refs_5_ = bf16[48,1152]{1,0:T(8,128)(2,1)S(1)} custom-call(bf16[96,576]{1,0:T(8,128)(2,1)S(1)} %get-tuple-element.59.query_ref, bf16[96,576]{1,0:T(8,128)(2,1)S(1)} %get-tuple-element.60.keys_ref, bf16[96,576]{1,0:T(8,128)(2,1)S(1)} %get-tuple-element.61.values_ref, bf16[4,576,1152]{2,1,0:T(8,128)(2,1)S(1)} %shard_map.94.weights_ref), custom_call_target="tpu_custom_call" | custom-call | tf_op jit(solution)/shard_map/pallas_call | solution.py:460
  67.3 2.4 %collective-permute-done.12.refs_6_ = bf16[48,1152]{1,0:T(8,128)(2,1)S(1)} collective-permute-done((bf16[48,1152]{1,0:T(8,128)(2,1)S(1)}, bf16[48,1152]{1,0:T(8,128)(2,1)S(1)}, u32[]{:S(2)}, u32[]{:S(2)}) %collective-permute-start.12) | collective-permute-done | bytes 110624 | tf_op jit(solution)/shard_map/ppermute | solution.py:491
  69.7 0.5 shard_map.100
  70.1 9.5 %all_to_all.11.arrived_ref = f32[16,8,128]{2,1,0:T(8,128)S(1)} all-to-all(f32[16,8,128]{2,1,0:T(8,128)S(1)} %shard_map.100), channel_id=1, replica_groups=mesh['queue'=16,'space'=2] {'queue'}, dimensions={0} | all-to-all | bytes 131072 | tf_op jit(solution)/shard_map/all_to_all | solution.py:649
  79.6 0.8 shard_map.101
  (3 shorter events, 0.0 us)
Async XLA Ops:
  2.5 8.5 %collective-permute-start.4 = (bf16[16,3456]{1,0:T(8,128)(2,1)S(1)}, bf16[16,3456]{1,0:T(8,128)(2,1)S(1)}, u32[]{:S(2)}, u32[]{:S(2)}) collective-permute-start(bf16[16,3456]{1,0:T(8,128)(2,1)S(1)} %get-tuple-element.37.refs_0_), channel_id=1, source_target_pairs={{0,1},{1,0},{2,3},{3,2},{4,5},{5,4},{6,7},{7,6},{8,9},{9,8},{10,11... | collective-permute-start | bytes 331784 | tf_op jit(solution)/shard_map/ppermute | solution.py:491
  5.5 3.6 %collective-permute-start = (f32[1,8,128]{2,1,0:T(8,128)S(1)}, f32[1,8,128]{2,1,0:T(8,128)S(1)}, u32[]{:S(2)}, u32[]{:S(2)}) collective-permute-start(f32[1,8,128]{2,1,0:T(8,128)S(1)} %get-tuple-element.34.refs_0_), channel_id=1, source_target_pairs={{0,1},{1,0},{2,3},{3,2},{4,5},{5,4},{6,7},{7,6},{8,9},{9,8},{10,11... | collective-permute-start | bytes 12296 | tf_op jit(solution)/shard_map/ppermute | solution.py:497
  9.1 3.9 %collective-permute-start.3 = (f32[2,8,128]{2,1,0:T(8,128)S(1)}, f32[2,8,128]{2,1,0:T(8,128)S(1)}, u32[]{:S(2)}, u32[]{:S(2)}) collective-permute-start(f32[2,8,128]{2,1,0:T(8,128)S(1)} %shard_map.88.refs_0_), channel_id=1, source_target_pairs={{0,6},{1,7},{2,4},{3,5},{4,2},{5,3},{6,0},{7,1},{8,14},{9,15},{10,... | collective-permute-start | bytes 24584 | tf_op jit(solution)/shard_map/ppermute | solution.py:497
  9.1 3.9 %collective-permute-start.2 = (f32[2,8,128]{2,1,0:T(8,128)S(1)}, f32[2,8,128]{2,1,0:T(8,128)S(1)}, u32[]{:S(2)}, u32[]{:S(2)}) collective-permute-start(f32[2,8,128]{2,1,0:T(8,128)S(1)} %shard_map.88.refs_0_), channel_id=1, source_target_pairs={{0,4},{1,5},{2,6},{3,7},{4,0},{5,1},{6,2},{7,3},{8,12},{9,13},{10,... | collective-permute-start | bytes 24584 | tf_op jit(solution)/shard_map/ppermute | solution.py:497
  10.7 2.4 %collective-permute-start.1 = (f32[2,8,128]{2,1,0:T(8,128)S(1)}, f32[2,8,128]{2,1,0:T(8,128)S(1)}, u32[]{:S(2)}, u32[]{:S(2)}) collective-permute-start(f32[2,8,128]{2,1,0:T(8,128)S(1)} %shard_map.88.refs_0_), channel_id=1, source_target_pairs={{0,2},{1,3},{2,0},{3,1},{4,6},{5,7},{6,4},{7,5},{8,10},{9,11},{10,... | collective-permute-start | bytes 24584 | tf_op jit(solution)/shard_map/ppermute | solution.py:497
  13.0 13.3 %copy-start.1 = (f32[2,48,16]{1,2,0:T(8,128)S(1)}, f32[2,48,16]{1,2,0:T(8,128)}, u32[]{:S(2)}) copy-start(f32[2,48,16]{1,2,0:T(8,128)} %param.8) | copy-start | bytes 18436
  13.1 6.1 %collective-permute-start.7 = (f32[8,8,128]{2,1,0:T(8,128)S(1)}, f32[8,8,128]{2,1,0:T(8,128)S(1)}, u32[]{:S(2)}, u32[]{:S(2)}) collective-permute-start(f32[8,8,128]{2,1,0:T(8,128)S(1)} %shard_map.90.refs_0_), channel_id=1, source_target_pairs={{0,24},{1,25},{2,26},{3,27},{4,28},{5,29},{6,30},{7,31},{8,16},{9,... | collective-permute-start | bytes 98312 | tf_op jit(solution)/shard_map/ppermute | solution.py:497
  16.8 4.8 %collective-permute-start.6 = (f32[8,8,128]{2,1,0:T(8,128)S(1)}, f32[8,8,128]{2,1,0:T(8,128)S(1)}, u32[]{:S(2)}, u32[]{:S(2)}) collective-permute-start(f32[8,8,128]{2,1,0:T(8,128)S(1)} %shard_map.90.refs_0_), channel_id=1, source_target_pairs={{0,16},{1,17},{2,18},{3,19},{4,20},{5,21},{6,22},{7,23},{8,24},{9,... | collective-permute-start | bytes 98312 | tf_op jit(solution)/shard_map/ppermute | solution.py:497
  16.8 4.8 %collective-permute-start.5 = (f32[8,8,128]{2,1,0:T(8,128)S(1)}, f32[8,8,128]{2,1,0:T(8,128)S(1)}, u32[]{:S(2)}, u32[]{:S(2)}) collective-permute-start(f32[8,8,128]{2,1,0:T(8,128)S(1)} %shard_map.90.refs_0_), channel_id=1, source_target_pairs={{0,8},{1,9},{2,10},{3,11},{4,12},{5,13},{6,14},{7,15},{8,0},{9,1},... | collective-permute-start | bytes 98312 | tf_op jit(solution)/shard_map/ppermute | solution.py:497
  25.0 6.9 %collective-permute-start.8 = (bf16[96,1152]{1,0:T(8,128)(2,1)S(1)}, bf16[96,1152]{1,0:T(8,128)(2,1)S(1)}, u32[]{:S(2)}, u32[]{:S(2)}) collective-permute-start(bf16[96,1152]{1,0:T(8,128)(2,1)S(1)} %get-tuple-element.50.refs_0_), channel_id=1, source_target_pairs={{0,1},{1,0},{2,3},{3,2},{4,5},{5,4},{6,7},{7,6},{8,9},{9,8},{10,11... | collective-permute-start | bytes 663560 | tf_op jit(solution)/shard_map/ppermute | solution.py:491
  26.3 5.5 %collective-permute-start.9 = (f32[2,16,48]{2,1,0:T(8,128)S(1)}, f32[2,16,48]{2,1,0:T(8,128)S(1)}, u32[]{:S(2)}, u32[]{:S(2)}) collective-permute-start(f32[2,16,48]{2,1,0:T(8,128)S(1)} %bitcast.7), channel_id=1, source_target_pairs={{0,1},{1,0},{2,3},{3,2},{4,5},{5,4},{6,7},{7,6},{8,9},{9,8},{10,11... | collective-permute-start | bytes 18440 | tf_op jit(solution)/shard_map/ppermute | solution.py:491
  29.6 11.5 %copy-start = (bf16[1152,16]{0,1:T(8,128)(2,1)S(1)}, bf16[1152,16]{0,1:T(8,128)(2,1)}, u32[]{:S(2)}) copy-start(bf16[1152,16]{0,1:T(8,128)(2,1)} %param.13) | copy-start | bytes 110596
  35.1 6.0 %collective-permute-start.10 = (bf16[96,1152]{1,0:T(8,128)(2,1)S(1)}, bf16[96,1152]{1,0:T(8,128)(2,1)S(1)}, u32[]{:S(2)}, u32[]{:S(2)}) collective-permute-start(bf16[96,1152]{1,0:T(8,128)(2,1)S(1)} %get-tuple-element.55.refs_5_), channel_id=1, source_target_pairs={{0,1},{1,0},{2,3},{3,2},{4,5},{5,4},{6,7},{7,6},{8,9},{9,8},{10,11... | collective-permute-start | bytes 663560 | tf_op jit(solution)/shard_map/ppermute | solution.py:491
  55.2 7.0 %collective-permute-start.11 = (bf16[96,1152]{1,0:T(8,128)(2,1)S(1)}, bf16[96,1152]{1,0:T(8,128)(2,1)S(1)}, u32[]{:S(2)}, u32[]{:S(2)}) collective-permute-start(bf16[96,1152]{1,0:T(8,128)(2,1)S(1)} %shard_map.97.refs_0_), channel_id=1, source_target_pairs={{0,1},{1,0},{2,3},{3,2},{4,5},{5,4},{6,7},{7,6},{8,9},{9,8},{10,11... | collective-permute-start | bytes 663560 | tf_op jit(solution)/shard_map/ppermute | solution.py:491
  64.9 4.8 %collective-permute-start.12 = (bf16[48,1152]{1,0:T(8,128)(2,1)S(1)}, bf16[48,1152]{1,0:T(8,128)(2,1)S(1)}, u32[]{:S(2)}, u32[]{:S(2)}) collective-permute-start(bf16[48,1152]{1,0:T(8,128)(2,1)S(1)} %get-tuple-element.62), channel_id=1, source_target_pairs={{0,1},{1,0},{2,3},{3,2},{4,5},{5,4},{6,7},{7,6},{8,9},{9,8},{10,11... | collective-permute-start | bytes 331784 | tf_op jit(solution)/shard_map/ppermute | solution.py:491

commit v2 on v1

--- a/solution.py
+++ b/solution.py
@@ -17,7 +17,7 @@
 PIECES = 6
 LANES = 128
 SLOTS = 32
-GROUP = 8
+GROUP = 16
 MIB = 1024 * 1024
 F32 = jnp.float32
 BF16 = jnp.bfloat16
@@ -55,6 +55,12 @@
 
 def product(left, right, precision=None):
     return jnp.dot(left, right, precision=precision, preferred_element_type=F32)
+
+
+def projected(rows, weights_ref):
+    local_width, width = weights_ref.shape[1:]
+    through = rows_by(rows, weights_ref[0:3].reshape(3 * local_width, width))
+    return [through[:, at * local_width : (at + 1) * local_width] for at in range(3)]
 
 
 def over(count, body):
@@ -161,8 +167,7 @@
     scale = 1.0 + mods_ref[blocks : 2 * blocks, :]
     spread = [(centred * scale[block : block + 1, :]).astype(BF16) for block in range(blocks)]
     spread = jnp.concatenate(spread + [mods_ref[0:blocks, :].astype(BF16)], 0)
-    for matrix in range(3):
-        through = rows_by(spread, weights_ref[matrix])
+    for matrix, through in enumerate(projected(spread, weights_ref)):
         rows_ref[matrix] = through[: blocks * CH].astype(BF16)
         last_ref[matrix] = through[blocks * CH :]
 
@@ -347,9 +352,8 @@
     stream_ref[...] = own_half(stream) if halved else stream
     normed = layer_norm(stream) * (1.0 + piece_of(mods_ref, 4, share)) + piece_of(mods_ref, 3, share)
     normed = normed.astype(BF16)
-    query_ref[...] = rows_by(normed, weights_ref[0]).astype(BF16)
-    keys_ref[...] = rows_by(normed, weights_ref[1]).astype(BF16)
-    values_ref[...] = rows_by(normed, weights_ref[2]).astype(BF16)
+    for ref, through in zip((query_ref, keys_ref, values_ref), projected(normed, weights_ref)):
+        ref[...] = through.astype(BF16)
     half = 1 - lax.axis_index("space") if halved else None
     term_ref[...] = attend(half, blocks, query_ref, keys_ref, values_ref, weights_ref)
 
@@ -547,12 +551,11 @@
         )
         vectors = over_space(vectors)
         spatial_weights = load(after(attention_weights, packed), 0, 4)
-        gathered = joined(packed, after(apart(packed, 1), spatial_weights))
-        arrivals = [apart(gathered, mask) for mask in (2, 4, 6)]
+        arrivals = [apart(packed, mask) for mask in range(1, 8)]
+        arrivals[-1] = after(arrivals[-1], spatial_weights)
+        gathered = joined(packed, *arrivals)
+        arrivals = [apart(gathered, mask) for mask in (8, 16, 24)]
         mods, cov, *seen = basis(vectors, spatial_weights)
-        arrivals[-1] = after(arrivals[-1], *seen)
-        gathered = joined(gathered, *arrivals)
-        arrivals = [apart(gathered, mask) for mask in (8, 16, 24)]
         scores, values = forms(seen)
         arrivals[-1] = after(arrivals[-1], scores)
         gathered = [joined(gathered, *arrivals)]

time: 80.6 us -> 83.3 us (1.033)
  starting transfers between devices: 15.5 us -> 19.7 us
  waiting for transfers between devices: 18.3 us -> 16.4 us
  blocking collectives: 19.9 us -> 21.4 us
  Pallas kernels: 25.9 us -> 24.7 us
    ppermute x7 -> x10, starting transfers between devices: 6.39 us -> 11.7 us  [apart(): lax.ppermute(x, ('queue', 'space'), [(i, i ^ mask) for i in range(count)])]
    ppermute x7 -> x10, waiting for transfers between devices: 3.41 us -> 1.26 us  [apart(): lax.ppermute(x, ('queue', 'space'), [(i, i ^ mask) for i in range(count)])]
    all_to_all x1, blocking collectives: 10.4 us -> 11.9 us  [local(): gathered = [lax.all_to_all(sent, 'queue', 0, 0, tiled=True)]]
    pallas_call x14 -> x13, Pallas kernels: 20.8 us -> 19.6 us  [call(): pl.pallas_call(kernel, out_shape=[place(shape, dtype) for shape, dtype in...]
    ppermute x6, starting transfers between devices: 9.12 us -> 8.08 us  [over_space(): return [x, lax.ppermute(x, 'space', [(0, 1), (1, 0)])]]
  transfers between devices with their start and end apart: 13 -> 16, of which waited for: 6 -> 6; matrix products, arithmetic and copies ran while one was open for 0% -> 0% of each run, Pallas kernels for 12% -> 11%
where the time goes in v2:
time: 83.3 us; the launch traced here: 83.1 us
  Pallas kernels  24.7 us (30%)
  blocking collectives  21.4 us (26%)
  starting transfers between devices  19.7 us (24%)
  waiting for transfers between devices  16.4 us (20%)
    pallas_call x13, Pallas kernels, call(): pl.pallas_call(kernel, out_shape=[place(shape, dtype) for shape, dtype in...  19.6 us
    ppermute x6, waiting for transfers between devices, over_space(): return [x, lax.ppermute(x, 'space', [(0, 1), (1, 0)])]  15.2 us
    all_to_all x1, blocking collectives, local(): gathered = [lax.all_to_all(sent, 'queue', 0, 0, tiled=True)]  11.9 us
    ppermute x10, starting transfers between devices, apart(): lax.ppermute(x, ('queue', 'space'), [(i, i ^ mask) for i in range(count)])  11.7 us
    all_to_all x1, blocking collectives, local(): arrived = lax.all_to_all(sent, 'queue', 0, 0, tiled=True)  9.48 us
    ppermute x6, starting transfers between devices, over_space(): return [x, lax.ppermute(x, 'space', [(0, 1), (1, 0)])]  8.08 us
    pallas_call x2, Pallas kernels, load(): pl.pallas_call(functools.partial(loader_kernel, first), out_shape=pltpu.V...  5.11 us
  transfers between devices with their start and end apart: 16, of which 6 were waited for; matrix products, arithmetic and copies ran while one was open for 0% of the time, Pallas kernels for 11%

profile of v2, /device:TPU:0, one launch (start us, length us, event | category | flops | bytes accessed | tf_op | source)
XLA Modules:
  0.0 83.1 jit_solution(12501189676660649018)
XLA Ops:
  0.6 1.9 %shard_map.86 = (bf16[16,3456]{1,0:T(8,128)(2,1)S(1)}, f32[16,128]{1,0:T(8,128)S(1)}, f32[1,8,128]{2,1,0:T(8,128)S(1)}, bf16[16,1152]{1,0:T(8,128)(2,1)S(1)}) custom-call(s32[16]{0:T(128)} %levels_hbm.1, bf16[256,3456]{1,0:T(8,128)(2,1)} %weight_hbm.1, f32[1,16,48]{2,1,0:T(8,128)} %bitcast.10, bf16[16,1152]{1,0:T(8,128)(2,1)} %embed_hbm.1), custom_call_target="tpu_custom_call" | custom-call | tf_op jit(solution)/shard_map/pallas_call | solution.py:464
  2.5 3.0 %collective-permute-start.10 = (bf16[16,3456]{1,0:T(8,128)(2,1)S(1)}, bf16[16,3456]{1,0:T(8,128)(2,1)S(1)}, u32[]{:S(2)}, u32[]{:S(2)}) collective-permute-start(bf16[16,3456]{1,0:T(8,128)(2,1)S(1)} %get-tuple-element.36.refs_0_), channel_id=1, source_target_pairs={{0,1},{1,0},{2,3},{3,2},{4,5},{5,4},{6,7},{7,6},{8,9},{9,8},{10,11... | collective-permute-start | bytes 331784 | tf_op jit(solution)/shard_map/ppermute | solution.py:495
  5.5 0.7 collective-permute-start.6
  6.2 0.6 collective-permute-start.5
  6.8 2.9 %collective-permute-start.4 = (f32[1,8,128]{2,1,0:T(8,128)S(1)}, f32[1,8,128]{2,1,0:T(8,128)S(1)}, u32[]{:S(2)}, u32[]{:S(2)}) collective-permute-start(f32[1,8,128]{2,1,0:T(8,128)S(1)} %get-tuple-element.33.refs_0_), channel_id=1, source_target_pairs={{0,5},{1,4},{2,7},{3,6},{4,1},{5,0},{6,3},{7,2},{8,13},{9,12},{10,... | collective-permute-start | bytes 12296 | tf_op jit(solution)/shard_map/ppermute | solution.py:501
  9.7 0.5 collective-permute-start.3
  10.2 0.0 collective-permute-done.6.refs_7_
  10.2 0.6 collective-permute-start.2
  10.8 0.0 collective-permute-done.5.refs_6_
  10.8 0.0 collective-permute-start.1
  10.8 0.5 collective-permute-done.4.refs_5_
  11.3 1.9 %collective-permute-start = (f32[1,8,128]{2,1,0:T(8,128)S(1)}, f32[1,8,128]{2,1,0:T(8,128)S(1)}, u32[]{:S(2)}, u32[]{:S(2)}) collective-permute-start(f32[1,8,128]{2,1,0:T(8,128)S(1)} %get-tuple-element.33.refs_0_), channel_id=1, source_target_pairs={{0,1},{1,0},{2,3},{3,2},{4,5},{5,4},{6,7},{7,6},{8,9},{9,8},{10,11... | collective-permute-start | bytes 12296 | tf_op jit(solution)/shard_map/ppermute | solution.py:501
  13.2 2.6 %shard_map.87.refs_3_.refs_4_.refs_5_ = bf16[4,576,1152]{2,1,0:T(8,128)(2,1)S(1)} custom-call(bf16[8,576,1152]{2,1,0:T(8,128)(2,1)} %weights_ref.1), custom_call_target="tpu_custom_call" | custom-call | bytes 5308416 | tf_op jit(solution)/shard_map/pallas_call | solution.py:445
  15.8 0.0 collective-permute-done.3.refs_4_
  15.8 0.0 collective-permute-done.2.refs_3_
  15.8 0.0 collective-permute-done.1.refs_2_
  15.8 0.0 collective-permute-done.refs_1_
  15.9 3.7 %collective-permute-start.9 = (f32[8,8,128]{2,1,0:T(8,128)S(1)}, f32[8,8,128]{2,1,0:T(8,128)S(1)}, u32[]{:S(2)}, u32[]{:S(2)}) collective-permute-start(f32[8,8,128]{2,1,0:T(8,128)S(1)} %shard_map.88.refs_0_), channel_id=1, source_target_pairs={{0,24},{1,25},{2,26},{3,27},{4,28},{5,29},{6,30},{7,31},{8,16},{9,... | collective-permute-start | bytes 98312 | tf_op jit(solution)/shard_map/ppermute | solution.py:501
  19.5 0.0 collective-permute-start.8
  19.5 0.8 collective-permute-start.7
  20.3 0.0 collective-permute-done.10.refs_1_
  20.3 1.7 %shard_map.89 = (f32[96,1152]{1,0:T(8,128)S(1)}, f32[16,16]{1,0:T(8,128)S(1)}, bf16[3,256,576]{2,1,0:T(8,128)(2,1)S(1)}, f32[3,16,576]{2,1,0:T(8,128)S(1)}) custom-call(bf16[16,3456]{1,0:T(8,128)(2,1)S(1)} %get-tuple-element.36.refs_0_, bf16[16,3456]{1,0:T(8,128)(2,1)S(1)} %collective-permute-done.10.refs_1_, ...), custom_call_target="tpu_custom_call" | custom-call | tf_op jit(solution)/shard_map/pallas_call | solution.py:464
  22.0 0.0 copy-start.1
  22.0 1.6 %shard_map.90 = (bf16[16,256,128]{2,1,0:T(8,128)(2,1)S(1)}, bf16[16,128,576]{2,1,0:T(8,128)(2,1)S(1)}) custom-call(bf16[3,256,576]{2,1,0:T(8,128)(2,1)S(1)} %get-tuple-element.38.rows_ref, f32[3,16,576]{2,1,0:T(8,128)S(1)} %get-tuple-element.39.last_ref), custom_call_target="tpu_custom_call" | custom-call | tf_op jit(solution)/shard_map/pallas_call | solution.py:464
  23.6 0.0 collective-permute-done.9.refs_3_
  23.6 0.7 collective-permute-done.8.refs_2_
  24.4 3.1 %shard_map.92 = (bf16[96,1152]{1,0:T(8,128)(2,1)S(1)}, f32[96,16]{1,0:T(8,128)S(1)}) custom-call(f32[32,8,128]{2,1,0:T(8,128)S(1)} %shard_map.91.refs_0_, f32[16,16]{1,0:T(8,128)S(1)} %get-tuple-element.42.refs_1_.refs_9_.refs_2_, bf16[16,256,128]{2,1,0:T(8,128)(2,1)S(1)} %get-tuple-element.40.refs_2_.refs_3_, ...), custom_call_target="tpu_custom_call" | custom-call | tf_op jit(solution)/shard_map/pallas_call | solution.py:464
  27.4 1.0 %collective-permute-start.11 = (bf16[96,1152]{1,0:T(8,128)(2,1)S(1)}, bf16[96,1152]{1,0:T(8,128)(2,1)S(1)}, u32[]{:S(2)}, u32[]{:S(2)}) collective-permute-start(bf16[96,1152]{1,0:T(8,128)(2,1)S(1)} %get-tuple-element.48.refs_0_), channel_id=1, source_target_pairs={{0,1},{1,0},{2,3},{3,2},{4,5},{5,4},{6,7},{7,6},{8,9},{9,8},{10,11... | collective-permute-start | bytes 663560 | tf_op jit(solution)/shard_map/ppermute | solution.py:495
  28.4 1.1 %collective-permute-start.12 = (f32[2,16,48]{2,1,0:T(8,128)S(1)}, f32[2,16,48]{2,1,0:T(8,128)S(1)}, u32[]{:S(2)}, u32[]{:S(2)}) collective-permute-start(f32[2,16,48]{2,1,0:T(8,128)S(1)} %bitcast.7), channel_id=1, source_target_pairs={{0,1},{1,0},{2,3},{3,2},{4,5},{5,4},{6,7},{7,6},{8,9},{9,8},{10,11... | collective-permute-start | bytes 18440 | tf_op jit(solution)/shard_map/ppermute | solution.py:495
  29.5 2.6 %shard_map.93.weights_ref = bf16[4,576,1152]{2,1,0:T(8,128)(2,1)S(1)} custom-call(bf16[8,576,1152]{2,1,0:T(8,128)(2,1)} %weights_ref.1), custom_call_target="tpu_custom_call" | custom-call | bytes 5308416 | tf_op jit(solution)/shard_map/pallas_call | solution.py:445
  32.1 0.0 copy-start
  32.1 1.5 %collective-permute-done.12.refs_8_ = f32[2,16,48]{2,1,0:T(8,128)S(1)} collective-permute-done((f32[2,16,48]{2,1,0:T(8,128)S(1)}, f32[2,16,48]{2,1,0:T(8,128)S(1)}, u32[]{:S(2)}, u32[]{:S(2)}) %collective-permute-start.12) | collective-permute-done | bytes 6176 | tf_op jit(solution)/shard_map/ppermute | solution.py:495
  33.6 0.0 collective-permute-done.11.refs_1_
  33.6 3.1 %shard_map.94 = (f32[96,1152]{1,0:T(8,128)S(1)}, bf16[96,1152]{1,0:T(8,128)(2,1)S(1)}) custom-call(f32[96,16]{1,0:T(8,128)S(1)} %get-tuple-element.44.own_ref.refs_0_, f32[96,1152]{1,0:T(8,128)S(1)} %get-tuple-element.45.mods_ref.refs_2_, bf16[16,1152]{1,0:T(8,128)(2,1)S(1)} %get-tuple-element.37.refs_2_.embed_ref, ...), custom_call_target="tpu_custom_call" | custom-call | tf_op jit(solution)/shard_map/pallas_call | solution.py:464
  36.7 1.0 %collective-permute-start.13 = (bf16[96,1152]{1,0:T(8,128)(2,1)S(1)}, bf16[96,1152]{1,0:T(8,128)(2,1)S(1)}, u32[]{:S(2)}, u32[]{:S(2)}) collective-permute-start(bf16[96,1152]{1,0:T(8,128)(2,1)S(1)} %get-tuple-element.53.refs_5_), channel_id=1, source_target_pairs={{0,1},{1,0},{2,3},{3,2},{4,5},{5,4},{6,7},{7,6},{8,9},{9,8},{10,11... | collective-permute-start | bytes 663560 | tf_op jit(solution)/shard_map/ppermute | solution.py:495
  37.7 5.0 %collective-permute-done.13.refs_6_ = bf16[96,1152]{1,0:T(8,128)(2,1)S(1)} collective-permute-done((bf16[96,1152]{1,0:T(8,128)(2,1)S(1)}, bf16[96,1152]{1,0:T(8,128)(2,1)S(1)}, u32[]{:S(2)}, u32[]{:S(2)}) %collective-permute-start.13) | collective-permute-done | bytes 221216 | tf_op jit(solution)/shard_map/ppermute | solution.py:495
  42.7 0.8 shard_map.95
  43.5 11.9 %all_to_all.10.refs_0_ = bf16[16,16,128]{2,1,0:T(8,128)(2,1)S(1)} all-to-all(bf16[16,16,128]{2,1,0:T(8,128)(2,1)S(1)} %get-tuple-element.55), channel_id=1, replica_groups=mesh['queue'=16,'space'=2] {'queue'}, dimensions={0} | all-to-all | bytes 131072 | tf_op jit(solution)/shard_map/all_to_all | solution.py:640
  55.5 2.4 %shard_map.96.refs_0_ = bf16[96,1152]{1,0:T(8,128)(2,1)S(1)} custom-call(bf16[16,16,128]{2,1,0:T(8,128)(2,1)S(1)} %all_to_all.10.refs_0_, f32[96,16]{1,0:T(8,128)S(1)} %get-tuple-element.54.refs_1_.own_ref.refs_0_, f32[16,16]{1,0:T(8,128)S(1)} %get-tuple-element.42.refs_1_.refs_9_.refs_2_, bf16[16,256,128]{2,1,0:T(8,128)(2,1)S(1)} %get-tuple-element.40.refs_2_.refs_3_, ...), custom_call_target="tpu_custom_call" | custom-call | tf_op jit(solution)/shard_map/pallas_call | solution.py:464
  57.9 1.0 %collective-permute-start.14 = (bf16[96,1152]{1,0:T(8,128)(2,1)S(1)}, bf16[96,1152]{1,0:T(8,128)(2,1)S(1)}, u32[]{:S(2)}, u32[]{:S(2)}) collective-permute-start(bf16[96,1152]{1,0:T(8,128)(2,1)S(1)} %shard_map.96.refs_0_), channel_id=1, source_target_pairs={{0,1},{1,0},{2,3},{3,2},{4,5},{5,4},{6,7},{7,6},{8,9},{9,8},{10,11... | collective-permute-start | bytes 663560 | tf_op jit(solution)/shard_map/ppermute | solution.py:495
  58.9 6.0 %collective-permute-done.14.refs_1_ = bf16[96,1152]{1,0:T(8,128)(2,1)S(1)} collective-permute-done((bf16[96,1152]{1,0:T(8,128)(2,1)S(1)}, bf16[96,1152]{1,0:T(8,128)(2,1)S(1)}, u32[]{:S(2)}, u32[]{:S(2)}) %collective-permute-start.14) | collective-permute-done | bytes 221216 | tf_op jit(solution)/shard_map/ppermute | solution.py:495
  64.8 2.7 %shard_map.97 = (f32[48,1152]{1,0:T(8,128)S(1)}, bf16[48,1152]{1,0:T(8,128)(2,1)S(1)}, bf16[96,576]{1,0:T(8,128)(2,1)S(1)}, bf16[96,576]{1,0:T(8,128)(2,1)S(1)}, bf16[96,576]{1,0:T(8,128)(2,1)S(1)}) custom-call(f32[96,16]{1,0:T(8,128)S(1)} %get-tuple-element.54.refs_1_.own_ref.refs_0_, f32[96,1152]{1,0:T(8,128)S(1)} %get-tuple-element.45.mods_ref.refs_2_, ...), custom_call_target="tpu_custom_call" | custom-call | tf_op jit(solution)/shard_map/pallas_call | solution.py:464
  67.6 1.0 %collective-permute-start.15 = (bf16[48,1152]{1,0:T(8,128)(2,1)S(1)}, bf16[48,1152]{1,0:T(8,128)(2,1)S(1)}, u32[]{:S(2)}, u32[]{:S(2)}) collective-permute-start(bf16[48,1152]{1,0:T(8,128)(2,1)S(1)} %get-tuple-element.60), channel_id=1, source_target_pairs={{0,1},{1,0},{2,3},{3,2},{4,5},{5,4},{6,7},{7,6},{8,9},{9,8},{10,11... | collective-permute-start | bytes 331784 | tf_op jit(solution)/shard_map/ppermute | solution.py:495
  68.6 1.1 %shard_map.98.refs_5_ = bf16[48,1152]{1,0:T(8,128)(2,1)S(1)} custom-call(bf16[96,576]{1,0:T(8,128)(2,1)S(1)} %get-tuple-element.57.query_ref, bf16[96,576]{1,0:T(8,128)(2,1)S(1)} %get-tuple-element.58.keys_ref, bf16[96,576]{1,0:T(8,128)(2,1)S(1)} %get-tuple-element.59.values_ref, bf16[4,576,1152]{2,1,0:T(8,128)(2,1)S(1)} %shard_map.93.weights_ref), custom_call_target="tpu_custom_call" | custom-call | tf_op jit(solution)/shard_map/pallas_call | solution.py:464
  69.7 2.7 %collective-permute-done.15.refs_6_ = bf16[48,1152]{1,0:T(8,128)(2,1)S(1)} collective-permute-done((bf16[48,1152]{1,0:T(8,128)(2,1)S(1)}, bf16[48,1152]{1,0:T(8,128)(2,1)S(1)}, u32[]{:S(2)}, u32[]{:S(2)}) %collective-permute-start.15) | collective-permute-done | bytes 110624 | tf_op jit(solution)/shard_map/ppermute | solution.py:495
  72.4 0.5 shard_map.99
  72.8 9.5 %all_to_all.11.arrived_ref = f32[16,8,128]{2,1,0:T(8,128)S(1)} all-to-all(f32[16,8,128]{2,1,0:T(8,128)S(1)} %shard_map.99), channel_id=1, replica_groups=mesh['queue'=16,'space'=2] {'queue'}, dimensions={0} | all-to-all | bytes 131072 | tf_op jit(solution)/shard_map/all_to_all | solution.py:652
  82.3 0.8 shard_map.100
  (5 shorter events, 0.0 us)
Async XLA Ops:
  2.5 17.8 %collective-permute-start.10 = (bf16[16,3456]{1,0:T(8,128)(2,1)S(1)}, bf16[16,3456]{1,0:T(8,128)(2,1)S(1)}, u32[]{:S(2)}, u32[]{:S(2)}) collective-permute-start(bf16[16,3456]{1,0:T(8,128)(2,1)S(1)} %get-tuple-element.36.refs_0_), channel_id=1, source_target_pairs={{0,1},{1,0},{2,3},{3,2},{4,5},{5,4},{6,7},{7,6},{8,9},{9,8},{10,11... | collective-permute-start | bytes 331784 | tf_op jit(solution)/shard_map/ppermute | solution.py:495
  5.5 4.7 %collective-permute-start.6 = (f32[1,8,128]{2,1,0:T(8,128)S(1)}, f32[1,8,128]{2,1,0:T(8,128)S(1)}, u32[]{:S(2)}, u32[]{:S(2)}) collective-permute-start(f32[1,8,128]{2,1,0:T(8,128)S(1)} %get-tuple-element.33.refs_0_), channel_id=1, source_target_pairs={{0,7},{1,6},{2,5},{3,4},{4,3},{5,2},{6,1},{7,0},{8,15},{9,14},{10,... | collective-permute-start | bytes 12296 | tf_op jit(solution)/shard_map/ppermute | solution.py:501
  6.2 4.6 %collective-permute-start.5 = (f32[1,8,128]{2,1,0:T(8,128)S(1)}, f32[1,8,128]{2,1,0:T(8,128)S(1)}, u32[]{:S(2)}, u32[]{:S(2)}) collective-permute-start(f32[1,8,128]{2,1,0:T(8,128)S(1)} %get-tuple-element.33.refs_0_), channel_id=1, source_target_pairs={{0,6},{1,7},{2,4},{3,5},{4,2},{5,3},{6,0},{7,1},{8,14},{9,15},{10,... | collective-permute-start | bytes 12296 | tf_op jit(solution)/shard_map/ppermute | solution.py:501
  6.8 4.5 %collective-permute-start.4 = (f32[1,8,128]{2,1,0:T(8,128)S(1)}, f32[1,8,128]{2,1,0:T(8,128)S(1)}, u32[]{:S(2)}, u32[]{:S(2)}) collective-permute-start(f32[1,8,128]{2,1,0:T(8,128)S(1)} %get-tuple-element.33.refs_0_), channel_id=1, source_target_pairs={{0,5},{1,4},{2,7},{3,6},{4,1},{5,0},{6,3},{7,2},{8,13},{9,12},{10,... | collective-permute-start | bytes 12296 | tf_op jit(solution)/shard_map/ppermute | solution.py:501
  9.7 6.1 %collective-permute-start.3 = (f32[1,8,128]{2,1,0:T(8,128)S(1)}, f32[1,8,128]{2,1,0:T(8,128)S(1)}, u32[]{:S(2)}, u32[]{:S(2)}) collective-permute-start(f32[1,8,128]{2,1,0:T(8,128)S(1)} %get-tuple-element.33.refs_0_), channel_id=1, source_target_pairs={{0,4},{1,5},{2,6},{3,7},{4,0},{5,1},{6,2},{7,3},{8,12},{9,13},{10,... | collective-permute-start | bytes 12296 | tf_op jit(solution)/shard_map/ppermute | solution.py:501
  10.2 5.6 %collective-permute-start.2 = (f32[1,8,128]{2,1,0:T(8,128)S(1)}, f32[1,8,128]{2,1,0:T(8,128)S(1)}, u32[]{:S(2)}, u32[]{:S(2)}) collective-permute-start(f32[1,8,128]{2,1,0:T(8,128)S(1)} %get-tuple-element.33.refs_0_), channel_id=1, source_target_pairs={{0,3},{1,2},{2,1},{3,0},{4,7},{5,6},{6,5},{7,4},{8,11},{9,10},{10,... | collective-permute-start | bytes 12296 | tf_op jit(solution)/shard_map/ppermute | solution.py:501
  10.8 5.0 %collective-permute-start.1 = (f32[1,8,128]{2,1,0:T(8,128)S(1)}, f32[1,8,128]{2,1,0:T(8,128)S(1)}, u32[]{:S(2)}, u32[]{:S(2)}) collective-permute-start(f32[1,8,128]{2,1,0:T(8,128)S(1)} %get-tuple-element.33.refs_0_), channel_id=1, source_target_pairs={{0,2},{1,3},{2,0},{3,1},{4,6},{5,7},{6,4},{7,5},{8,10},{9,11},{10,... | collective-permute-start | bytes 12296 | tf_op jit(solution)/shard_map/ppermute | solution.py:501
  11.3 4.5 %collective-permute-start = (f32[1,8,128]{2,1,0:T(8,128)S(1)}, f32[1,8,128]{2,1,0:T(8,128)S(1)}, u32[]{:S(2)}, u32[]{:S(2)}) collective-permute-start(f32[1,8,128]{2,1,0:T(8,128)S(1)} %get-tuple-element.33.refs_0_), channel_id=1, source_target_pairs={{0,1},{1,0},{2,3},{3,2},{4,5},{5,4},{6,7},{7,6},{8,9},{9,8},{10,11... | collective-permute-start | bytes 12296 | tf_op jit(solution)/shard_map/ppermute | solution.py:501
  15.9 7.7 %collective-permute-start.9 = (f32[8,8,128]{2,1,0:T(8,128)S(1)}, f32[8,8,128]{2,1,0:T(8,128)S(1)}, u32[]{:S(2)}, u32[]{:S(2)}) collective-permute-start(f32[8,8,128]{2,1,0:T(8,128)S(1)} %shard_map.88.refs_0_), channel_id=1, source_target_pairs={{0,24},{1,25},{2,26},{3,27},{4,28},{5,29},{6,30},{7,31},{8,16},{9,... | collective-permute-start | bytes 98312 | tf_op jit(solution)/shard_map/ppermute | solution.py:501
  19.5 4.8 %collective-permute-start.8 = (f32[8,8,128]{2,1,0:T(8,128)S(1)}, f32[8,8,128]{2,1,0:T(8,128)S(1)}, u32[]{:S(2)}, u32[]{:S(2)}) collective-permute-start(f32[8,8,128]{2,1,0:T(8,128)S(1)} %shard_map.88.refs_0_), channel_id=1, source_target_pairs={{0,16},{1,17},{2,18},{3,19},{4,20},{5,21},{6,22},{7,23},{8,24},{9,... | collective-permute-start | bytes 98312 | tf_op jit(solution)/shard_map/ppermute | solution.py:501
  19.5 4.8 %collective-permute-start.7 = (f32[8,8,128]{2,1,0:T(8,128)S(1)}, f32[8,8,128]{2,1,0:T(8,128)S(1)}, u32[]{:S(2)}, u32[]{:S(2)}) collective-permute-start(f32[8,8,128]{2,1,0:T(8,128)S(1)} %shard_map.88.refs_0_), channel_id=1, source_target_pairs={{0,8},{1,9},{2,10},{3,11},{4,12},{5,13},{6,14},{7,15},{8,0},{9,1},... | collective-permute-start | bytes 98312 | tf_op jit(solution)/shard_map/ppermute | solution.py:501
  22.0 6.4 %copy-start.1 = (f32[2,48,16]{1,2,0:T(8,128)S(1)}, f32[2,48,16]{1,2,0:T(8,128)}, u32[]{:S(2)}) copy-start(f32[2,48,16]{1,2,0:T(8,128)} %param.8) | copy-start | bytes 18436
  27.4 6.2 %collective-permute-start.11 = (bf16[96,1152]{1,0:T(8,128)(2,1)S(1)}, bf16[96,1152]{1,0:T(8,128)(2,1)S(1)}, u32[]{:S(2)}, u32[]{:S(2)}) collective-permute-start(bf16[96,1152]{1,0:T(8,128)(2,1)S(1)} %get-tuple-element.48.refs_0_), channel_id=1, source_target_pairs={{0,1},{1,0},{2,3},{3,2},{4,5},{5,4},{6,7},{7,6},{8,9},{9,8},{10,11... | collective-permute-start | bytes 663560 | tf_op jit(solution)/shard_map/ppermute | solution.py:495
  28.4 5.2 %collective-permute-start.12 = (f32[2,16,48]{2,1,0:T(8,128)S(1)}, f32[2,16,48]{2,1,0:T(8,128)S(1)}, u32[]{:S(2)}, u32[]{:S(2)}) collective-permute-start(f32[2,16,48]{2,1,0:T(8,128)S(1)} %bitcast.7), channel_id=1, source_target_pairs={{0,1},{1,0},{2,3},{3,2},{4,5},{5,4},{6,7},{7,6},{8,9},{9,8},{10,11... | collective-permute-start | bytes 18440 | tf_op jit(solution)/shard_map/ppermute | solution.py:495
  32.1 10.6 %copy-start = (bf16[1152,16]{0,1:T(8,128)(2,1)S(1)}, bf16[1152,16]{0,1:T(8,128)(2,1)}, u32[]{:S(2)}) copy-start(bf16[1152,16]{0,1:T(8,128)(2,1)} %param.13) | copy-start | bytes 110596
  36.7 6.0 %collective-permute-start.13 = (bf16[96,1152]{1,0:T(8,128)(2,1)S(1)}, bf16[96,1152]{1,0:T(8,128)(2,1)S(1)}, u32[]{:S(2)}, u32[]{:S(2)}) collective-permute-start(bf16[96,1152]{1,0:T(8,128)(2,1)S(1)} %get-tuple-element.53.refs_5_), channel_id=1, source_target_pairs={{0,1},{1,0},{2,3},{3,2},{4,5},{5,4},{6,7},{7,6},{8,9},{9,8},{10,11... | collective-permute-start | bytes 663560 | tf_op jit(solution)/shard_map/ppermute | solution.py:495
  57.9 7.0 %collective-permute-start.14 = (bf16[96,1152]{1,0:T(8,128)(2,1)S(1)}, bf16[96,1152]{1,0:T(8,128)(2,1)S(1)}, u32[]{:S(2)}, u32[]{:S(2)}) collective-permute-start(bf16[96,1152]{1,0:T(8,128)(2,1)S(1)} %shard_map.96.refs_0_), channel_id=1, source_target_pairs={{0,1},{1,0},{2,3},{3,2},{4,5},{5,4},{6,7},{7,6},{8,9},{9,8},{10,11... | collective-permute-start | bytes 663560 | tf_op jit(solution)/shard_map/ppermute | solution.py:495
  67.6 4.8 %collective-permute-start.15 = (bf16[48,1152]{1,0:T(8,128)(2,1)S(1)}, bf16[48,1152]{1,0:T(8,128)(2,1)S(1)}, u32[]{:S(2)}, u32[]{:S(2)}) collective-permute-start(bf16[48,1152]{1,0:T(8,128)(2,1)S(1)} %get-tuple-element.60), channel_id=1, source_target_pairs={{0,1},{1,0},{2,3},{3,2},{4,5},{5,4},{6,7},{7,6},{8,9},{9,8},{10,11... | collective-permute-start | bytes 331784 | tf_op jit(solution)/shard_map/ppermute | solution.py:495

commit v3 on v2

--- a/solution.py
+++ b/solution.py
@@ -99,16 +99,21 @@
         copy.wait()
 
 
+def pack_kernel(latents_hbm, packed_ref, latents_ref, semaphore):
+    copy = pltpu.make_async_copy(latents_hbm, latents_ref, semaphore)
+    copy.start()
+    copy.wait()
+    shard = latents_ref.shape[2]
+    gap = jnp.zeros((CH // 2, LANES // 2 - shard), F32)
+    packed = [latents_ref[0, : CH // 2], gap, latents_ref[0, CH // 2 :], gap]
+    packed_ref[0] = jnp.concatenate(packed, 1)
+
+
 def opening_kernel(
-    levels_hbm, weight_hbm, latents_hbm, embed_hbm, vectors_ref, sizes_ref, packed_ref, embed_ref,
-    levels_ref, weight_ref, latents_ref, semaphores,
+    levels_hbm, weight_hbm, embed_hbm, vectors_ref, sizes_ref, embed_ref,
+    levels_ref, weight_ref, semaphores,
 ):
-    pairs = (
-        (levels_hbm, levels_ref),
-        (latents_hbm, latents_ref),
-        (weight_hbm, weight_ref),
-        (embed_hbm, embed_ref),
-    )
+    pairs = ((levels_hbm, levels_ref), (weight_hbm, weight_ref), (embed_hbm, embed_ref))
     copies = [
         pltpu.make_async_copy(source, target, semaphores.at[at])
         for at, (source, target) in enumerate(pairs)
@@ -130,13 +135,8 @@
     angles = (level.astype(F32) / LEVELS * 1000.0) * frequency
     features = jnp.concatenate([jnp.cos(angles), jnp.sin(angles)], -1).astype(BF16)
     copies[1].wait()
-    shard = latents_ref.shape[2]
-    gap = jnp.zeros((CH // 2, LANES // 2 - shard), F32)
-    packed = [latents_ref[0, : CH // 2], gap, latents_ref[0, CH // 2 :], gap]
-    packed_ref[0] = jnp.concatenate(packed, 1)
+    vectors_ref[...] = product(features, weight_ref[...]).astype(BF16)
     copies[2].wait()
-    vectors_ref[...] = product(features, weight_ref[...]).astype(BF16)
-    copies[3].wait()
 
 
 def join_kernel(*refs):
@@ -352,8 +352,12 @@
     stream_ref[...] = own_half(stream) if halved else stream
     normed = layer_norm(stream) * (1.0 + piece_of(mods_ref, 4, share)) + piece_of(mods_ref, 3, share)
     normed = normed.astype(BF16)
-    for ref, through in zip((query_ref, keys_ref, values_ref), projected(normed, weights_ref)):
-        ref[...] = through.astype(BF16)
+    if halved:
+        parts = [rows_by(normed, weights_ref[matrix]) for matrix in range(3)]
+    else:
+        parts = projected(normed, weights_ref)
+    for ref, part in zip((query_ref, keys_ref, values_ref), parts):
+        ref[...] = part.astype(BF16)
     half = 1 - lax.axis_index("space") if halved else None
     term_ref[...] = attend(half, blocks, query_ref, keys_ref, values_ref, weights_ref)
 
@@ -381,28 +385,31 @@
     return blocks, rows, velocity, moved, refs
 
 
-def between_kernel(share, term_count, iteration, noise_count, *refs):
-    blocks, rows, velocity, moved, refs = final_kernel(share, False, term_count, *refs)
-    noises, (cov_ref, velocity_ref, next_ref, sent_ref, noise_ref) = (
-        refs[:noise_count],
-        refs[noise_count:],
-    )
-    velocity_ref[...] = velocity
+def noise_kernel(share, iteration, *refs):
+    *noises, rows_ref, noise_ref = refs
     devices = lax.axis_size("queue")
     here = lax.axis_index("queue")
-    if noise_count == 2:
-        mine, theirs = noises[0][iteration], noises[1][iteration]
+    noise = noises[0][iteration]
+    if len(noises) == 2:
+        theirs = noises[1][iteration]
         first = lax.axis_index("space") == 0
         noise = jnp.concatenate(
-            [jnp.where(first, mine, theirs), jnp.where(first, theirs, mine)], 1
+            [jnp.where(first, noise, theirs), jnp.where(first, theirs, noise)], 1
         )
-    else:
-        noise = noises[0][iteration]
     noise_ref[...] = noise.T
+    rows_ref[...] = jnp.zeros_like(rows_ref)
+    for position in range(share):
+        rows_ref[position : position + 1, :] = noise_ref[pl.ds(position * devices + here, 1), :]
+
+
+def between_kernel(share, term_count, *refs):
+    blocks, rows, velocity, moved, refs = final_kernel(share, False, term_count, *refs)
+    noise_ref, cov_ref, velocity_ref, next_ref, sent_ref = refs
+    velocity_ref[...] = velocity
     next_ref[...] = moved
     for position in range(share):
         next_ref[(position + 1) * blocks - 1 : (position + 1) * blocks, :] = noise_ref[
-            pl.ds(position * devices + here, 1), :
+            position : position + 1, :
         ]
     hat = side_by_side(scaled(next_ref[...], cov_ref[...]), blocks, share)
     hat = jnp.where(iota((blocks, LANES), 1) == share * CH, 1.0, hat)
@@ -531,29 +538,36 @@
 
     paired = space_count == 2 and devices == 16
     if paired:
-        operands = (levels, modulation_weight, latents, embed_weight)
-        vectors, sizes, packed, embed_weight = run(
+        (packed,) = run(
+            pack_kernel,
+            [((1, CH // 2, LANES), F32)],
+            [],
+            [pltpu.VMEM(latents.shape, latents.dtype), pltpu.SemaphoreType.DMA],
+            from_hbm=[latents],
+        )
+        other = apart(packed, 1)
+        operands = (after(levels, packed), modulation_weight, embed_weight)
+        vectors, sizes, embed_weight = run(
             opening_kernel,
             [
                 ((blocks, modulation_weight.shape[1]), BF16),
                 ((blocks, LANES), F32),
-                ((1, CH // 2, LANES), F32),
                 (embed_weight.shape, BF16),
             ],
             [],
             [
                 pltpu.SMEM(levels.shape, levels.dtype),
                 pltpu.VMEM(modulation_weight.shape, modulation_weight.dtype),
-                pltpu.VMEM(latents.shape, latents.dtype),
                 pltpu.SemaphoreType.DMA((len(operands),)),
             ],
             from_hbm=operands,
         )
-        vectors = over_space(vectors)
-        spatial_weights = load(after(attention_weights, packed), 0, 4)
-        arrivals = [apart(packed, mask) for mask in range(1, 8)]
+        gathered = joined(packed, after(other, vectors))
+        vectors = over_space(after(vectors, gathered))
+        arrivals = [apart(gathered, mask) for mask in (2, 4, 6)]
+        spatial_weights = load(after(attention_weights, gathered), 0, 4)
         arrivals[-1] = after(arrivals[-1], spatial_weights)
-        gathered = joined(packed, *arrivals)
+        gathered = joined(gathered, *arrivals)
         arrivals = [apart(gathered, mask) for mask in (8, 16, 24)]
         mods, cov, *seen = basis(vectors, spatial_weights)
         scores, values = forms(seen)
@@ -621,19 +635,25 @@
                 [((held_rows, width), BF16)],
                 [*asked, temporal_weights],
             )
+        if not last:
+            noises[0] = after(noises[0], temporal_term)
+            (noise,) = run(
+                functools.partial(noise_kernel, share, iteration),
+                [((8, CH), F32)],
+                noises,
+                [pltpu.VMEM((tokens, CH), F32)],
+            )
+            temporal_terms[-1] = after(temporal_terms[-1], noise)
         operands = [own, stream, mods, final_rows, sizes, *temporal_terms]
         if not last:
             velocity, own, sent = run(
-                functools.partial(
-                    between_kernel, share, len(temporal_terms), iteration, len(noises)
-                ),
+                functools.partial(between_kernel, share, len(temporal_terms)),
                 [
                     ((rows, CH), F32),
                     ((rows, CH), F32),
                     ((devices if paired else 1, blocks, LANES), BF16),
                 ],
-                operands + [*noises, cov],
-                [pltpu.VMEM((tokens, CH), F32)],
+                operands + [noise, cov],
             )
             velocities.append(velocity)
             if paired:

time: 83.3 us -> 80.7 us (0.969)
  starting transfers between devices: 19.7 us -> 14.9 us
  waiting for transfers between devices: 16.4 us -> 17.7 us
    ppermute x6, starting transfers between devices: 8.08 us -> 5.6 us  [over_space(): return [x, lax.ppermute(x, 'space', [(0, 1), (1, 0)])]]
    ppermute x10 -> x7, starting transfers between devices: 11.7 us -> 9.32 us  [apart(): lax.ppermute(x, ('queue', 'space'), [(i, i ^ mask) for i in range(count)])]
    ppermute x6, waiting for transfers between devices: 15.2 us -> 16.9 us  [over_space(): return [x, lax.ppermute(x, 'space', [(0, 1), (1, 0)])]]
    pallas_call x13 -> x16, Pallas kernels: 19.6 us -> 20.4 us  [call(): pl.pallas_call(kernel, out_shape=[place(shape, dtype) for shape, dtype in...]
  transfers between devices with their start and end apart: 16 -> 13, of which waited for: 6 -> 5; matrix products, arithmetic and copies ran while one was open for 0% -> 0% of each run, Pallas kernels for 11% -> 14%
where the time goes in v3:
time: 80.7 us; the launch traced here: 80.4 us
  Pallas kernels  25.5 us (32%)
  blocking collectives  21.4 us (27%)
  waiting for transfers between devices  17.7 us (22%)
  starting transfers between devices  14.9 us (18%)
  between operations  0.82 us (1%)
    pallas_call x16, Pallas kernels, call(): pl.pallas_call(kernel, out_shape=[place(shape, dtype) for shape, dtype in...  20.4 us
    ppermute x6, waiting for transfers between devices, over_space(): return [x, lax.ppermute(x, 'space', [(0, 1), (1, 0)])]  16.9 us
    all_to_all x1, blocking collectives, local(): gathered = [lax.all_to_all(sent, 'queue', 0, 0, tiled=True)]  12 us
    all_to_all x1, blocking collectives, local(): arrived = lax.all_to_all(sent, 'queue', 0, 0, tiled=True)  9.48 us
    ppermute x7, starting transfers between devices, apart(): lax.ppermute(x, ('queue', 'space'), [(i, i ^ mask) for i in range(count)])  9.32 us
    ppermute x6, starting transfers between devices, over_space(): return [x, lax.ppermute(x, 'space', [(0, 1), (1, 0)])]  5.6 us
    pallas_call x2, Pallas kernels, load(): pl.pallas_call(functools.partial(loader_kernel, first), out_shape=pltpu.V...  5.11 us
  transfers between devices with their start and end apart: 13, of which 5 were waited for; matrix products, arithmetic and copies ran while one was open for 0% of the time, Pallas kernels for 14%

profile of v3, /device:TPU:0, one launch (start us, length us, event | category | flops | bytes accessed | tf_op | source)
XLA Modules:
  0.0 80.4 jit_solution(5239525748245600500)
XLA Ops:
  0.6 0.8 shard_map.86.refs_0_
  1.4 3.0 %collective-permute-start = (f32[1,8,128]{2,1,0:T(8,128)S(1)}, f32[1,8,128]{2,1,0:T(8,128)S(1)}, u32[]{:S(2)}, u32[]{:S(2)}) collective-permute-start(f32[1,8,128]{2,1,0:T(8,128)S(1)} %shard_map.86.refs_0_), channel_id=1, source_target_pairs={{0,1},{1,0},{2,3},{3,2},{4,5},{5,4},{6,7},{7,6},{8,9},{9,8},{10,11... | collective-permute-start | bytes 12296 | tf_op jit(solution)/shard_map/ppermute | solution.py:508
  4.4 1.9 %shard_map.87 = (bf16[16,3456]{1,0:T(8,128)(2,1)S(1)}, f32[16,128]{1,0:T(8,128)S(1)}, bf16[16,1152]{1,0:T(8,128)(2,1)S(1)}) custom-call(s32[16]{0:T(128)} %levels_hbm, bf16[256,3456]{1,0:T(8,128)(2,1)} %weight_hbm.1, bf16[16,1152]{1,0:T(8,128)(2,1)} %embed_hbm.1), custom_call_target="tpu_custom_call" | custom-call | tf_op jit(solution)/shard_map/pallas_call | solution.py:471
  6.3 0.0 collective-permute-done.refs_1_
  6.3 1.7 %collective-permute-start.7 = (bf16[16,3456]{1,0:T(8,128)(2,1)S(1)}, bf16[16,3456]{1,0:T(8,128)(2,1)S(1)}, u32[]{:S(2)}, u32[]{:S(2)}) collective-permute-start(bf16[16,3456]{1,0:T(8,128)(2,1)S(1)} %get-tuple-element.42.refs_0_), channel_id=1, source_target_pairs={{0,1},{1,0},{2,3},{3,2},{4,5},{5,4},{6,7},{7,6},{8,9},{9,8},{10,11... | collective-permute-start | bytes 331784 | tf_op jit(solution)/shard_map/ppermute | solution.py:502
  8.0 0.0 collective-permute-start.3
  8.0 1.6 %collective-permute-start.2 = (f32[2,8,128]{2,1,0:T(8,128)S(1)}, f32[2,8,128]{2,1,0:T(8,128)S(1)}, u32[]{:S(2)}, u32[]{:S(2)}) collective-permute-start(f32[2,8,128]{2,1,0:T(8,128)S(1)} %shard_map.88.refs_0_), channel_id=1, source_target_pairs={{0,4},{1,5},{2,6},{3,7},{4,0},{5,1},{6,2},{7,3},{8,12},{9,13},{10,... | collective-permute-start | bytes 24584 | tf_op jit(solution)/shard_map/ppermute | solution.py:508
  9.6 0.3 collective-permute-start.1
  9.9 2.6 %shard_map.89.refs_3_.refs_4_.refs_5_ = bf16[4,576,1152]{2,1,0:T(8,128)(2,1)S(1)} custom-call(bf16[8,576,1152]{2,1,0:T(8,128)(2,1)} %weights_ref.1), custom_call_target="tpu_custom_call" | custom-call | bytes 5308416 | tf_op jit(solution)/shard_map/pallas_call | solution.py:452
  12.5 0.0 collective-permute-done.3.refs_3_
  12.5 0.0 collective-permute-done.2.refs_2_
  12.5 0.0 collective-permute-done.1.refs_1_
  12.5 3.7 %collective-permute-start.6 = (f32[8,8,128]{2,1,0:T(8,128)S(1)}, f32[8,8,128]{2,1,0:T(8,128)S(1)}, u32[]{:S(2)}, u32[]{:S(2)}) collective-permute-start(f32[8,8,128]{2,1,0:T(8,128)S(1)} %shard_map.90.refs_0_), channel_id=1, source_target_pairs={{0,24},{1,25},{2,26},{3,27},{4,28},{5,29},{6,30},{7,31},{8,16},{9,... | collective-permute-start | bytes 98312 | tf_op jit(solution)/shard_map/ppermute | solution.py:508
  16.2 0.0 collective-permute-start.5
  16.2 0.8 collective-permute-start.4
  17.0 0.0 collective-permute-done.7.refs_1_
  17.0 1.7 %shard_map.91 = (f32[96,1152]{1,0:T(8,128)S(1)}, f32[16,16]{1,0:T(8,128)S(1)}, bf16[3,256,576]{2,1,0:T(8,128)(2,1)S(1)}, f32[3,16,576]{2,1,0:T(8,128)S(1)}) custom-call(bf16[16,3456]{1,0:T(8,128)(2,1)S(1)} %get-tuple-element.42.refs_0_, bf16[16,3456]{1,0:T(8,128)(2,1)S(1)} %collective-permute-done.7.refs_1_, ...), custom_call_target="tpu_custom_call" | custom-call | tf_op jit(solution)/shard_map/pallas_call | solution.py:471
  18.6 0.0 copy-start.1
  18.6 1.6 %shard_map.92 = (bf16[16,256,128]{2,1,0:T(8,128)(2,1)S(1)}, bf16[16,128,576]{2,1,0:T(8,128)(2,1)S(1)}) custom-call(bf16[3,256,576]{2,1,0:T(8,128)(2,1)S(1)} %get-tuple-element.44.rows_ref, f32[3,16,576]{2,1,0:T(8,128)S(1)} %get-tuple-element.45.last_ref), custom_call_target="tpu_custom_call" | custom-call | tf_op jit(solution)/shard_map/pallas_call | solution.py:471
  20.2 0.0 collective-permute-done.6.refs_3_
  20.2 0.7 collective-permute-done.5.refs_2_
  21.0 0.0 collective-permute-done.4.refs_1_
  21.0 3.1 %shard_map.94 = (bf16[96,1152]{1,0:T(8,128)(2,1)S(1)}, f32[96,16]{1,0:T(8,128)S(1)}) custom-call(f32[32,8,128]{2,1,0:T(8,128)S(1)} %shard_map.93.refs_0_, f32[16,16]{1,0:T(8,128)S(1)} %get-tuple-element.48.refs_1_.refs_8_.refs_2_, bf16[16,256,128]{2,1,0:T(8,128)(2,1)S(1)} %get-tuple-element.46.refs_2_.refs_3_, ...), custom_call_target="tpu_custom_call" | custom-call | tf_op jit(solution)/shard_map/pallas_call | solution.py:471
  24.1 0.6 collective-permute-start.8
  24.7 0.0 copy-done.1
  24.7 1.5 %collective-permute-start.9 = (f32[2,16,48]{2,1,0:T(8,128)S(1)}, f32[2,16,48]{2,1,0:T(8,128)S(1)}, u32[]{:S(2)}, u32[]{:S(2)}) collective-permute-start(f32[2,16,48]{2,1,0:T(8,128)S(1)} %bitcast.7), channel_id=1, source_target_pairs={{0,1},{1,0},{2,3},{3,2},{4,5},{5,4},{6,7},{7,6},{8,9},{9,8},{10,11... | collective-permute-start | bytes 18440 | tf_op jit(solution)/shard_map/ppermute | solution.py:502
  26.2 2.6 %shard_map.95.weights_ref = bf16[4,576,1152]{2,1,0:T(8,128)(2,1)S(1)} custom-call(bf16[8,576,1152]{2,1,0:T(8,128)(2,1)} %weights_ref.1), custom_call_target="tpu_custom_call" | custom-call | bytes 5308416 | tf_op jit(solution)/shard_map/pallas_call | solution.py:452
  28.7 0.0 copy-start
  28.7 2.2 %collective-permute-done.9.refs_1_ = f32[2,16,48]{2,1,0:T(8,128)S(1)} collective-permute-done((f32[2,16,48]{2,1,0:T(8,128)S(1)}, f32[2,16,48]{2,1,0:T(8,128)S(1)}, u32[]{:S(2)}, u32[]{:S(2)}) %collective-permute-start.9) | collective-permute-done | bytes 6176 | tf_op jit(solution)/shard_map/ppermute | solution.py:502
  31.0 0.0 collective-permute-done.8.refs_1_
  31.0 3.1 %shard_map.96 = (f32[96,1152]{1,0:T(8,128)S(1)}, bf16[96,1152]{1,0:T(8,128)(2,1)S(1)}) custom-call(f32[96,16]{1,0:T(8,128)S(1)} %get-tuple-element.50.own_ref.refs_0_, f32[96,1152]{1,0:T(8,128)S(1)} %get-tuple-element.51.mods_ref.refs_2_, bf16[16,1152]{1,0:T(8,128)(2,1)S(1)} %get-tuple-element.43.refs_2_.embed_ref, ...), custom_call_target="tpu_custom_call" | custom-call | tf_op jit(solution)/shard_map/pallas_call | solution.py:471
  34.1 0.6 collective-permute-start.10
  34.7 0.2 shard_map.97.refs_7_
  34.8 5.2 %collective-permute-done.10.refs_6_ = bf16[96,1152]{1,0:T(8,128)(2,1)S(1)} collective-permute-done((bf16[96,1152]{1,0:T(8,128)(2,1)S(1)}, bf16[96,1152]{1,0:T(8,128)(2,1)S(1)}, u32[]{:S(2)}, u32[]{:S(2)}) %collective-permute-start.10) | collective-permute-done | bytes 221216 | tf_op jit(solution)/shard_map/ppermute | solution.py:502
  40.1 0.0 copy-done
  40.1 0.8 %shard_map.98 = (f32[96,16]{1,0:T(8,128)S(1)}, f32[96,16]{1,0:T(8,128)S(1)}, bf16[16,16,128]{2,1,0:T(8,128)(2,1)S(1)}) custom-call(f32[96,16]{1,0:T(8,128)S(1)} %get-tuple-element.50.own_ref.refs_0_, f32[96,1152]{1,0:T(8,128)S(1)} %get-tuple-element.57.refs_1_, f32[96,1152]{1,0:T(8,128)S(1)} %get-tuple-element.51.mods_ref.refs_2_, ...), custom_call_target="tpu_custom_call" | custom-call | tf_op jit(solution)/shard_map/pallas_call | solution.py:471
  40.9 12.0 %all_to_all.10.refs_0_ = bf16[16,16,128]{2,1,0:T(8,128)(2,1)S(1)} all-to-all(bf16[16,16,128]{2,1,0:T(8,128)(2,1)S(1)} %get-tuple-element.63), channel_id=1, replica_groups=mesh['queue'=16,'space'=2] {'queue'}, dimensions={0} | all-to-all | bytes 131072 | tf_op jit(solution)/shard_map/all_to_all | solution.py:660
  52.8 2.4 %shard_map.99.refs_0_ = bf16[96,1152]{1,0:T(8,128)(2,1)S(1)} custom-call(bf16[16,16,128]{2,1,0:T(8,128)(2,1)S(1)} %all_to_all.10.refs_0_, f32[96,16]{1,0:T(8,128)S(1)} %get-tuple-element.62.refs_1_.own_ref.refs_0_, f32[16,16]{1,0:T(8,128)S(1)} %get-tuple-element.48.refs_1_.refs_8_.refs_2_, bf16[16,256,128]{2,1,0:T(8,128)(2,1)S(1)} %get-tuple-element.46.refs_2_.refs_3_, ...), custom_call_target="tpu_custom_call" | custom-call | tf_op jit(solution)/shard_map/pallas_call | solution.py:471
  55.2 0.6 collective-permute-start.11
  55.8 6.4 %collective-permute-done.11.refs_1_ = bf16[96,1152]{1,0:T(8,128)(2,1)S(1)} collective-permute-done((bf16[96,1152]{1,0:T(8,128)(2,1)S(1)}, bf16[96,1152]{1,0:T(8,128)(2,1)S(1)}, u32[]{:S(2)}, u32[]{:S(2)}) %collective-permute-start.11) | collective-permute-done | bytes 221216 | tf_op jit(solution)/shard_map/ppermute | solution.py:502
  62.2 2.6 %shard_map.100 = (f32[48,1152]{1,0:T(8,128)S(1)}, bf16[48,1152]{1,0:T(8,128)(2,1)S(1)}, bf16[96,576]{1,0:T(8,128)(2,1)S(1)}, bf16[96,576]{1,0:T(8,128)(2,1)S(1)}, bf16[96,576]{1,0:T(8,128)(2,1)S(1)}) custom-call(f32[96,16]{1,0:T(8,128)S(1)} %get-tuple-element.62.refs_1_.own_ref.refs_0_, f32[96,1152]{1,0:T(8,128)S(1)} %get-tuple-element.51.mods_ref.refs_2_, ...), custom_call_target="tpu_custom_call" | custom-call | tf_op jit(solution)/shard_map/pallas_call | solution.py:471
  64.9 0.6 collective-permute-start.12
  65.5 1.1 %shard_map.101.refs_5_ = bf16[48,1152]{1,0:T(8,128)(2,1)S(1)} custom-call(bf16[96,576]{1,0:T(8,128)(2,1)S(1)} %get-tuple-element.65.query_ref, bf16[96,576]{1,0:T(8,128)(2,1)S(1)} %get-tuple-element.66.keys_ref, bf16[96,576]{1,0:T(8,128)(2,1)S(1)} %get-tuple-element.67.values_ref, bf16[4,576,1152]{2,1,0:T(8,128)(2,1)S(1)} %shard_map.95.weights_ref), custom_call_target="tpu_custom_call" | custom-call | tf_op jit(solution)/shard_map/pallas_call | solution.py:471
  66.6 3.1 %collective-permute-done.12.refs_6_ = bf16[48,1152]{1,0:T(8,128)(2,1)S(1)} collective-permute-done((bf16[48,1152]{1,0:T(8,128)(2,1)S(1)}, bf16[48,1152]{1,0:T(8,128)(2,1)S(1)}, u32[]{:S(2)}, u32[]{:S(2)}) %collective-permute-start.12) | collective-permute-done | bytes 110624 | tf_op jit(solution)/shard_map/ppermute | solution.py:502
  69.7 0.5 shard_map.102
  70.1 9.5 %all_to_all.11.arrived_ref = f32[16,8,128]{2,1,0:T(8,128)S(1)} all-to-all(f32[16,8,128]{2,1,0:T(8,128)S(1)} %shard_map.102), channel_id=1, replica_groups=mesh['queue'=16,'space'=2] {'queue'}, dimensions={0} | all-to-all | bytes 131072 | tf_op jit(solution)/shard_map/all_to_all | solution.py:672
  79.6 0.8 shard_map.103
  (3 shorter events, 0.0 us)
Async XLA Ops:
  1.4 4.9 %collective-permute-start = (f32[1,8,128]{2,1,0:T(8,128)S(1)}, f32[1,8,128]{2,1,0:T(8,128)S(1)}, u32[]{:S(2)}, u32[]{:S(2)}) collective-permute-start(f32[1,8,128]{2,1,0:T(8,128)S(1)} %shard_map.86.refs_0_), channel_id=1, source_target_pairs={{0,1},{1,0},{2,3},{3,2},{4,5},{5,4},{6,7},{7,6},{8,9},{9,8},{10,11... | collective-permute-start | bytes 12296 | tf_op jit(solution)/shard_map/ppermute | solution.py:508
  6.3 10.7 %collective-permute-start.7 = (bf16[16,3456]{1,0:T(8,128)(2,1)S(1)}, bf16[16,3456]{1,0:T(8,128)(2,1)S(1)}, u32[]{:S(2)}, u32[]{:S(2)}) collective-permute-start(bf16[16,3456]{1,0:T(8,128)(2,1)S(1)} %get-tuple-element.42.refs_0_), channel_id=1, source_target_pairs={{0,1},{1,0},{2,3},{3,2},{4,5},{5,4},{6,7},{7,6},{8,9},{9,8},{10,11... | collective-permute-start | bytes 331784 | tf_op jit(solution)/shard_map/ppermute | solution.py:502
  8.0 4.4 %collective-permute-start.3 = (f32[2,8,128]{2,1,0:T(8,128)S(1)}, f32[2,8,128]{2,1,0:T(8,128)S(1)}, u32[]{:S(2)}, u32[]{:S(2)}) collective-permute-start(f32[2,8,128]{2,1,0:T(8,128)S(1)} %shard_map.88.refs_0_), channel_id=1, source_target_pairs={{0,6},{1,7},{2,4},{3,5},{4,2},{5,3},{6,0},{7,1},{8,14},{9,15},{10,... | collective-permute-start | bytes 24584 | tf_op jit(solution)/shard_map/ppermute | solution.py:508
  8.0 4.4 %collective-permute-start.2 = (f32[2,8,128]{2,1,0:T(8,128)S(1)}, f32[2,8,128]{2,1,0:T(8,128)S(1)}, u32[]{:S(2)}, u32[]{:S(2)}) collective-permute-start(f32[2,8,128]{2,1,0:T(8,128)S(1)} %shard_map.88.refs_0_), channel_id=1, source_target_pairs={{0,4},{1,5},{2,6},{3,7},{4,0},{5,1},{6,2},{7,3},{8,12},{9,13},{10,... | collective-permute-start | bytes 24584 | tf_op jit(solution)/shard_map/ppermute | solution.py:508
  9.6 2.9 %collective-permute-start.1 = (f32[2,8,128]{2,1,0:T(8,128)S(1)}, f32[2,8,128]{2,1,0:T(8,128)S(1)}, u32[]{:S(2)}, u32[]{:S(2)}) collective-permute-start(f32[2,8,128]{2,1,0:T(8,128)S(1)} %shard_map.88.refs_0_), channel_id=1, source_target_pairs={{0,2},{1,3},{2,0},{3,1},{4,6},{5,7},{6,4},{7,5},{8,10},{9,11},{10,... | collective-permute-start | bytes 24584 | tf_op jit(solution)/shard_map/ppermute | solution.py:508
  12.5 7.7 %collective-permute-start.6 = (f32[8,8,128]{2,1,0:T(8,128)S(1)}, f32[8,8,128]{2,1,0:T(8,128)S(1)}, u32[]{:S(2)}, u32[]{:S(2)}) collective-permute-start(f32[8,8,128]{2,1,0:T(8,128)S(1)} %shard_map.90.refs_0_), channel_id=1, source_target_pairs={{0,24},{1,25},{2,26},{3,27},{4,28},{5,29},{6,30},{7,31},{8,16},{9,... | collective-permute-start | bytes 98312 | tf_op jit(solution)/shard_map/ppermute | solution.py:508
  16.2 4.8 %collective-permute-start.5 = (f32[8,8,128]{2,1,0:T(8,128)S(1)}, f32[8,8,128]{2,1,0:T(8,128)S(1)}, u32[]{:S(2)}, u32[]{:S(2)}) collective-permute-start(f32[8,8,128]{2,1,0:T(8,128)S(1)} %shard_map.90.refs_0_), channel_id=1, source_target_pairs={{0,16},{1,17},{2,18},{3,19},{4,20},{5,21},{6,22},{7,23},{8,24},{9,... | collective-permute-start | bytes 98312 | tf_op jit(solution)/shard_map/ppermute | solution.py:508
  16.2 4.8 %collective-permute-start.4 = (f32[8,8,128]{2,1,0:T(8,128)S(1)}, f32[8,8,128]{2,1,0:T(8,128)S(1)}, u32[]{:S(2)}, u32[]{:S(2)}) collective-permute-start(f32[8,8,128]{2,1,0:T(8,128)S(1)} %shard_map.90.refs_0_), channel_id=1, source_target_pairs={{0,8},{1,9},{2,10},{3,11},{4,12},{5,13},{6,14},{7,15},{8,0},{9,1},... | collective-permute-start | bytes 98312 | tf_op jit(solution)/shard_map/ppermute | solution.py:508
  18.6 6.1 %copy-start.1 = (f32[2,48,16]{1,2,0:T(8,128)S(1)}, f32[2,48,16]{1,2,0:T(8,128)}, u32[]{:S(2)}) copy-start(f32[2,48,16]{1,2,0:T(8,128)} %param.8) | copy-start | bytes 18436
  24.1 6.9 %collective-permute-start.8 = (bf16[96,1152]{1,0:T(8,128)(2,1)S(1)}, bf16[96,1152]{1,0:T(8,128)(2,1)S(1)}, u32[]{:S(2)}, u32[]{:S(2)}) collective-permute-start(bf16[96,1152]{1,0:T(8,128)(2,1)S(1)} %get-tuple-element.54.refs_0_), channel_id=1, source_target_pairs={{0,1},{1,0},{2,3},{3,2},{4,5},{5,4},{6,7},{7,6},{8,9},{9,8},{10,11... | collective-permute-start | bytes 663560 | tf_op jit(solution)/shard_map/ppermute | solution.py:502
  24.7 6.3 %collective-permute-start.9 = (f32[2,16,48]{2,1,0:T(8,128)S(1)}, f32[2,16,48]{2,1,0:T(8,128)S(1)}, u32[]{:S(2)}, u32[]{:S(2)}) collective-permute-start(f32[2,16,48]{2,1,0:T(8,128)S(1)} %bitcast.7), channel_id=1, source_target_pairs={{0,1},{1,0},{2,3},{3,2},{4,5},{5,4},{6,7},{7,6},{8,9},{9,8},{10,11... | collective-permute-start | bytes 18440 | tf_op jit(solution)/shard_map/ppermute | solution.py:502
  28.7 11.3 %copy-start = (bf16[1152,16]{0,1:T(8,128)(2,1)S(1)}, bf16[1152,16]{0,1:T(8,128)(2,1)}, u32[]{:S(2)}) copy-start(bf16[1152,16]{0,1:T(8,128)(2,1)} %param.13) | copy-start | bytes 110596
  34.1 6.0 %collective-permute-start.10 = (bf16[96,1152]{1,0:T(8,128)(2,1)S(1)}, bf16[96,1152]{1,0:T(8,128)(2,1)S(1)}, u32[]{:S(2)}, u32[]{:S(2)}) collective-permute-start(bf16[96,1152]{1,0:T(8,128)(2,1)S(1)} %get-tuple-element.59.refs_5_), channel_id=1, source_target_pairs={{0,1},{1,0},{2,3},{3,2},{4,5},{5,4},{6,7},{7,6},{8,9},{9,8},{10,11... | collective-permute-start | bytes 663560 | tf_op jit(solution)/shard_map/ppermute | solution.py:502
  55.2 7.0 %collective-permute-start.11 = (bf16[96,1152]{1,0:T(8,128)(2,1)S(1)}, bf16[96,1152]{1,0:T(8,128)(2,1)S(1)}, u32[]{:S(2)}, u32[]{:S(2)}) collective-permute-start(bf16[96,1152]{1,0:T(8,128)(2,1)S(1)} %shard_map.99.refs_0_), channel_id=1, source_target_pairs={{0,1},{1,0},{2,3},{3,2},{4,5},{5,4},{6,7},{7,6},{8,9},{9,8},{10,11... | collective-permute-start | bytes 663560 | tf_op jit(solution)/shard_map/ppermute | solution.py:502
  64.9 4.8 %collective-permute-start.12 = (bf16[48,1152]{1,0:T(8,128)(2,1)S(1)}, bf16[48,1152]{1,0:T(8,128)(2,1)S(1)}, u32[]{:S(2)}, u32[]{:S(2)}) collective-permute-start(bf16[48,1152]{1,0:T(8,128)(2,1)S(1)} %get-tuple-element.68), channel_id=1, source_target_pairs={{0,1},{1,0},{2,3},{3,2},{4,5},{5,4},{6,7},{7,6},{8,9},{9,8},{10,11... | collective-permute-start | bytes 331784 | tf_op jit(solution)/shard_map/ppermute | solution.py:502

commit v4 on v2

--- a/solution.py
+++ b/solution.py
@@ -18,6 +18,7 @@
 LANES = 128
 SLOTS = 32
 GROUP = 16
+BANDS = 4
 MIB = 1024 * 1024
 F32 = jnp.float32
 BF16 = jnp.bfloat16
@@ -88,10 +89,24 @@
     return x * lax.rsqrt(jnp.maximum(variance, 0.0) + 1e-06)
 
 
+def pieces_of(source, target):
+    rows = target.shape[0]
+    band = rows // BANDS if rows % (16 * BANDS) == 0 else rows
+    return [
+        (source.at[pl.ds(at, band), :], target.at[pl.ds(at, band), :])
+        for at in range(0, rows, band)
+    ]
+
+
 def loader_kernel(first, weights_ref, held_ref, semaphores):
+    pairs = [
+        pair
+        for at in range(held_ref.shape[0])
+        for pair in pieces_of(weights_ref.at[first + at], held_ref.at[at])
+    ]
     copies = [
-        pltpu.make_async_copy(weights_ref.at[first + at], held_ref.at[at], semaphores.at[at])
-        for at in range(held_ref.shape[0])
+        pltpu.make_async_copy(source, target, semaphores.at[at])
+        for at, (source, target) in enumerate(pairs)
     ]
     for copy in copies:
         copy.start()
@@ -103,12 +118,8 @@
     levels_hbm, weight_hbm, latents_hbm, embed_hbm, vectors_ref, sizes_ref, packed_ref, embed_ref,
     levels_ref, weight_ref, latents_ref, semaphores,
 ):
-    pairs = (
-        (levels_hbm, levels_ref),
-        (latents_hbm, latents_ref),
-        (weight_hbm, weight_ref),
-        (embed_hbm, embed_ref),
-    )
+    bands = pieces_of(weight_hbm, weight_ref)
+    pairs = [(levels_hbm, levels_ref), (latents_hbm, latents_ref), *bands, (embed_hbm, embed_ref)]
     copies = [
         pltpu.make_async_copy(source, target, semaphores.at[at])
         for at, (source, target) in enumerate(pairs)
@@ -134,9 +145,9 @@
     gap = jnp.zeros((CH // 2, LANES // 2 - shard), F32)
     packed = [latents_ref[0, : CH // 2], gap, latents_ref[0, CH // 2 :], gap]
     packed_ref[0] = jnp.concatenate(packed, 1)
-    copies[2].wait()
+    for copy in copies[2:]:
+        copy.wait()
     vectors_ref[...] = product(features, weight_ref[...]).astype(BF16)
-    copies[3].wait()
 
 
 def join_kernel(*refs):
@@ -352,8 +363,12 @@
     stream_ref[...] = own_half(stream) if halved else stream
     normed = layer_norm(stream) * (1.0 + piece_of(mods_ref, 4, share)) + piece_of(mods_ref, 3, share)
     normed = normed.astype(BF16)
-    for ref, through in zip((query_ref, keys_ref, values_ref), projected(normed, weights_ref)):
-        ref[...] = through.astype(BF16)
+    if halved:
+        parts = [rows_by(normed, weights_ref[matrix]) for matrix in range(3)]
+    else:
+        parts = projected(normed, weights_ref)
+    for ref, part in zip((query_ref, keys_ref, values_ref), parts):
+        ref[...] = part.astype(BF16)
     half = 1 - lax.axis_index("space") if halved else None
     term_ref[...] = attend(half, blocks, query_ref, keys_ref, values_ref, weights_ref)
 
@@ -447,7 +462,7 @@
         out_shape=pltpu.VMEM(shape, weights.dtype),
         in_specs=[pl.BlockSpec(memory_space=pltpu.HBM)],
         out_specs=pl.BlockSpec(memory_space=pltpu.VMEM),
-        scratch_shapes=[pltpu.SemaphoreType.DMA((count,))],
+        scratch_shapes=[pltpu.SemaphoreType.DMA((count * BANDS,))],
         compiler_params=small(1),
         cost_estimate=pl.CostEstimate(
             flops=0, bytes_accessed=2 * math.prod(shape), transcendentals=0
@@ -545,17 +560,18 @@
                 pltpu.SMEM(levels.shape, levels.dtype),
                 pltpu.VMEM(modulation_weight.shape, modulation_weight.dtype),
                 pltpu.VMEM(latents.shape, latents.dtype),
-                pltpu.SemaphoreType.DMA((len(operands),)),
+                pltpu.SemaphoreType.DMA((len(operands) + BANDS,)),
             ],
             from_hbm=operands,
         )
         vectors = over_space(vectors)
         spatial_weights = load(after(attention_weights, packed), 0, 4)
-        arrivals = [apart(packed, mask) for mask in range(1, 8)]
-        arrivals[-1] = after(arrivals[-1], spatial_weights)
-        gathered = joined(packed, *arrivals)
+        gathered = joined(packed, after(apart(packed, 1), spatial_weights))
+        arrivals = [apart(gathered, mask) for mask in (2, 4, 6)]
+        mods, cov, *seen = basis(vectors, spatial_weights)
+        arrivals[-1] = after(arrivals[-1], *seen)
+        gathered = joined(gathered, *arrivals)
         arrivals = [apart(gathered, mask) for mask in (8, 16, 24)]
-        mods, cov, *seen = basis(vectors, spatial_weights)
         scores, values = forms(seen)
         arrivals[-1] = after(arrivals[-1], scores)
         gathered = [joined(gathered, *arrivals)]

time: 83.3 us -> 79.3 us (0.952)
  starting transfers between devices: 19.7 us -> 15.6 us
  waiting for transfers between devices: 16.4 us -> 18.2 us
  blocking collectives: 21.4 us -> 19.7 us
    ppermute x10 -> x7, starting transfers between devices: 11.7 us -> 6.36 us  [apart(): lax.ppermute(x, ('queue', 'space'), [(i, i ^ mask) for i in range(count)])]
    ppermute x10 -> x7, waiting for transfers between devices: 1.26 us -> 3.47 us  [apart(): lax.ppermute(x, ('queue', 'space'), [(i, i ^ mask) for i in range(count)])]
    all_to_all x1, blocking collectives: 11.9 us -> 10.2 us  [local(): gathered = [lax.all_to_all(sent, 'queue', 0, 0, tiled=True)]]
    ppermute x6, starting transfers between devices: 8.08 us -> 9.28 us  [over_space(): return [x, lax.ppermute(x, 'space', [(0, 1), (1, 0)])]]
    pallas_call x13 -> x14, Pallas kernels: 19.6 us -> 19.5 us  [call(): pl.pallas_call(kernel, out_shape=[place(shape, dtype) for shape, dtype in...]
  transfers between devices with their start and end apart: 16 -> 13, of which waited for: 6 -> 7; matrix products, arithmetic and copies ran while one was open for 0% -> 0% of each run, Pallas kernels for 11% -> 12%
where the time goes in v4:
time: 79.3 us; the launch traced here: 79.1 us
  Pallas kernels  24.7 us (31%)
  blocking collectives  19.7 us (25%)
  waiting for transfers between devices  18.2 us (23%)
  starting transfers between devices  15.6 us (20%)
    pallas_call x14, Pallas kernels, call(): pl.pallas_call(kernel, out_shape=[place(shape, dtype) for shape, dtype in...  19.5 us
    ppermute x6, waiting for transfers between devices, over_space(): return [x, lax.ppermute(x, 'space', [(0, 1), (1, 0)])]  14.8 us
    all_to_all x1, blocking collectives, local(): gathered = [lax.all_to_all(sent, 'queue', 0, 0, tiled=True)]  10.2 us
    all_to_all x1, blocking collectives, local(): arrived = lax.all_to_all(sent, 'queue', 0, 0, tiled=True)  9.48 us
    ppermute x6, starting transfers between devices, over_space(): return [x, lax.ppermute(x, 'space', [(0, 1), (1, 0)])]  9.28 us
    ppermute x7, starting transfers between devices, apart(): lax.ppermute(x, ('queue', 'space'), [(i, i ^ mask) for i in range(count)])  6.36 us
    pallas_call x2, Pallas kernels, load(): pl.pallas_call(functools.partial(loader_kernel, first), out_shape=pltpu.V...  5.22 us
    ppermute x7, waiting for transfers between devices, apart(): lax.ppermute(x, ('queue', 'space'), [(i, i ^ mask) for i in range(count)])  3.47 us
  transfers between devices with their start and end apart: 13, of which 7 were waited for; matrix products, arithmetic and copies ran while one was open for 0% of the time, Pallas kernels for 12%

profile of v4, /device:TPU:0, one launch (start us, length us, event | category | flops | bytes accessed | tf_op | source)
XLA Modules:
  0.0 79.1 jit_solution(1887357796130245078)
XLA Ops:
  0.6 1.9 %shard_map.86 = (bf16[16,3456]{1,0:T(8,128)(2,1)S(1)}, f32[16,128]{1,0:T(8,128)S(1)}, f32[1,8,128]{2,1,0:T(8,128)S(1)}, bf16[16,1152]{1,0:T(8,128)(2,1)S(1)}) custom-call(s32[16]{0:T(128)} %levels_hbm.1, bf16[256,3456]{1,0:T(8,128)(2,1)} %weight_hbm.1, f32[1,16,48]{2,1,0:T(8,128)} %bitcast.10, bf16[16,1152]{1,0:T(8,128)(2,1)} %embed_hbm.1), custom_call_target="tpu_custom_call" | custom-call | tf_op jit(solution)/shard_map/pallas_call | solution.py:479
  2.5 3.0 %collective-permute-start.4 = (bf16[16,3456]{1,0:T(8,128)(2,1)S(1)}, bf16[16,3456]{1,0:T(8,128)(2,1)S(1)}, u32[]{:S(2)}, u32[]{:S(2)}) collective-permute-start(bf16[16,3456]{1,0:T(8,128)(2,1)S(1)} %get-tuple-element.37.refs_0_), channel_id=1, source_target_pairs={{0,1},{1,0},{2,3},{3,2},{4,5},{5,4},{6,7},{7,6},{8,9},{9,8},{10,11... | collective-permute-start | bytes 331784 | tf_op jit(solution)/shard_map/ppermute | solution.py:510
  5.5 0.1 collective-permute-start
  5.6 2.6 %shard_map.87.refs_3_.refs_4_.refs_5_ = bf16[4,576,1152]{2,1,0:T(8,128)(2,1)S(1)} custom-call(bf16[8,576,1152]{2,1,0:T(8,128)(2,1)} %weights_ref.1), custom_call_target="tpu_custom_call" | custom-call | bytes 5308416 | tf_op jit(solution)/shard_map/pallas_call | solution.py:460
  8.2 0.9 %collective-permute-done.refs_1_ = f32[1,8,128]{2,1,0:T(8,128)S(1)} collective-permute-done((f32[1,8,128]{2,1,0:T(8,128)S(1)}, f32[1,8,128]{2,1,0:T(8,128)S(1)}, u32[]{:S(2)}, u32[]{:S(2)}) %collective-permute-start) | collective-permute-done | bytes 4128 | tf_op jit(solution)/shard_map/ppermute | solution.py:516
  9.1 0.0 collective-permute-start.3
  9.1 1.5 %collective-permute-start.2 = (f32[2,8,128]{2,1,0:T(8,128)S(1)}, f32[2,8,128]{2,1,0:T(8,128)S(1)}, u32[]{:S(2)}, u32[]{:S(2)}) collective-permute-start(f32[2,8,128]{2,1,0:T(8,128)S(1)} %shard_map.88.refs_0_), channel_id=1, source_target_pairs={{0,4},{1,5},{2,6},{3,7},{4,0},{5,1},{6,2},{7,3},{8,12},{9,13},{10,... | collective-permute-start | bytes 24584 | tf_op jit(solution)/shard_map/ppermute | solution.py:516
  10.7 0.3 collective-permute-start.1
  11.0 0.0 collective-permute-done.4.refs_1_
  11.0 1.7 %shard_map.89 = (f32[96,1152]{1,0:T(8,128)S(1)}, f32[16,16]{1,0:T(8,128)S(1)}, bf16[3,256,576]{2,1,0:T(8,128)(2,1)S(1)}, f32[3,16,576]{2,1,0:T(8,128)S(1)}) custom-call(bf16[16,3456]{1,0:T(8,128)(2,1)S(1)} %get-tuple-element.37.refs_0_, bf16[16,3456]{1,0:T(8,128)(2,1)S(1)} %collective-permute-done.4.refs_1_, ...), custom_call_target="tpu_custom_call" | custom-call | tf_op jit(solution)/shard_map/pallas_call | solution.py:479
  12.6 0.0 copy-start.1
  12.7 0.0 collective-permute-done.3.refs_3_
  12.7 0.1 collective-permute-done.2.refs_2_
  12.8 0.0 collective-permute-done.1.refs_1_
  12.8 3.6 %collective-permute-start.7 = (f32[8,8,128]{2,1,0:T(8,128)S(1)}, f32[8,8,128]{2,1,0:T(8,128)S(1)}, u32[]{:S(2)}, u32[]{:S(2)}) collective-permute-start(f32[8,8,128]{2,1,0:T(8,128)S(1)} %shard_map.90.refs_0_), channel_id=1, source_target_pairs={{0,24},{1,25},{2,26},{3,27},{4,28},{5,29},{6,30},{7,31},{8,16},{9,... | collective-permute-start | bytes 98312 | tf_op jit(solution)/shard_map/ppermute | solution.py:516
  16.4 0.0 collective-permute-start.6
  16.4 0.8 collective-permute-start.5
  17.2 1.6 %shard_map.91 = (bf16[16,256,128]{2,1,0:T(8,128)(2,1)S(1)}, bf16[16,128,576]{2,1,0:T(8,128)(2,1)S(1)}) custom-call(bf16[3,256,576]{2,1,0:T(8,128)(2,1)S(1)} %get-tuple-element.39.rows_ref, f32[3,16,576]{2,1,0:T(8,128)S(1)} %get-tuple-element.40.last_ref), custom_call_target="tpu_custom_call" | custom-call | tf_op jit(solution)/shard_map/pallas_call | solution.py:479
  18.8 0.0 collective-permute-done.7.refs_3_
  18.8 2.4 %collective-permute-done.6.refs_2_ = f32[8,8,128]{2,1,0:T(8,128)S(1)} collective-permute-done((f32[8,8,128]{2,1,0:T(8,128)S(1)}, f32[8,8,128]{2,1,0:T(8,128)S(1)}, u32[]{:S(2)}, u32[]{:S(2)}) %collective-permute-start.6) | collective-permute-done | bytes 32800 | tf_op jit(solution)/shard_map/ppermute | solution.py:516
  21.3 0.0 collective-permute-done.5.refs_1_
  21.3 3.1 %shard_map.93 = (bf16[96,1152]{1,0:T(8,128)(2,1)S(1)}, f32[96,16]{1,0:T(8,128)S(1)}) custom-call(f32[32,8,128]{2,1,0:T(8,128)S(1)} %shard_map.92.refs_0_, f32[16,16]{1,0:T(8,128)S(1)} %get-tuple-element.44.refs_1_.refs_9_.refs_2_, bf16[16,256,128]{2,1,0:T(8,128)(2,1)S(1)} %get-tuple-element.42.refs_2_.refs_3_, ...), custom_call_target="tpu_custom_call" | custom-call | tf_op jit(solution)/shard_map/pallas_call | solution.py:479
  24.4 1.5 %collective-permute-start.8 = (bf16[96,1152]{1,0:T(8,128)(2,1)S(1)}, bf16[96,1152]{1,0:T(8,128)(2,1)S(1)}, u32[]{:S(2)}, u32[]{:S(2)}) collective-permute-start(bf16[96,1152]{1,0:T(8,128)(2,1)S(1)} %get-tuple-element.50.refs_0_), channel_id=1, source_target_pairs={{0,1},{1,0},{2,3},{3,2},{4,5},{5,4},{6,7},{7,6},{8,9},{9,8},{10,11... | collective-permute-start | bytes 663560 | tf_op jit(solution)/shard_map/ppermute | solution.py:510
  25.9 0.0 copy-done.1
  25.9 0.6 collective-permute-start.9
  26.4 2.6 %shard_map.94.weights_ref = bf16[4,576,1152]{2,1,0:T(8,128)(2,1)S(1)} custom-call(bf16[8,576,1152]{2,1,0:T(8,128)(2,1)} %weights_ref.1), custom_call_target="tpu_custom_call" | custom-call | bytes 5308416 | tf_op jit(solution)/shard_map/pallas_call | solution.py:460
  29.1 0.0 copy-start
  29.1 2.3 %collective-permute-done.9.refs_8_ = f32[2,16,48]{2,1,0:T(8,128)S(1)} collective-permute-done((f32[2,16,48]{2,1,0:T(8,128)S(1)}, f32[2,16,48]{2,1,0:T(8,128)S(1)}, u32[]{:S(2)}, u32[]{:S(2)}) %collective-permute-start.9) | collective-permute-done | bytes 6176 | tf_op jit(solution)/shard_map/ppermute | solution.py:510
  31.4 0.0 collective-permute-done.8.refs_1_
  31.4 3.1 %shard_map.95 = (f32[96,1152]{1,0:T(8,128)S(1)}, bf16[96,1152]{1,0:T(8,128)(2,1)S(1)}) custom-call(f32[96,16]{1,0:T(8,128)S(1)} %get-tuple-element.46.own_ref.refs_0_, f32[96,1152]{1,0:T(8,128)S(1)} %get-tuple-element.47.mods_ref.refs_2_, bf16[16,1152]{1,0:T(8,128)(2,1)S(1)} %get-tuple-element.38.refs_2_.embed_ref, ...), custom_call_target="tpu_custom_call" | custom-call | tf_op jit(solution)/shard_map/pallas_call | solution.py:479
  34.5 1.5 %collective-permute-start.10 = (bf16[96,1152]{1,0:T(8,128)(2,1)S(1)}, bf16[96,1152]{1,0:T(8,128)(2,1)S(1)}, u32[]{:S(2)}, u32[]{:S(2)}) collective-permute-start(bf16[96,1152]{1,0:T(8,128)(2,1)S(1)} %get-tuple-element.55.refs_5_), channel_id=1, source_target_pairs={{0,1},{1,0},{2,3},{3,2},{4,5},{5,4},{6,7},{7,6},{8,9},{9,8},{10,11... | collective-permute-start | bytes 663560 | tf_op jit(solution)/shard_map/ppermute | solution.py:510
  36.0 4.5 %collective-permute-done.10.refs_6_ = bf16[96,1152]{1,0:T(8,128)(2,1)S(1)} collective-permute-done((bf16[96,1152]{1,0:T(8,128)(2,1)S(1)}, bf16[96,1152]{1,0:T(8,128)(2,1)S(1)}, u32[]{:S(2)}, u32[]{:S(2)}) %collective-permute-start.10) | collective-permute-done | bytes 221216 | tf_op jit(solution)/shard_map/ppermute | solution.py:510
  40.5 0.0 copy-done
  40.5 0.8 %shard_map.96 = (f32[96,16]{1,0:T(8,128)S(1)}, f32[96,16]{1,0:T(8,128)S(1)}, bf16[16,16,128]{2,1,0:T(8,128)(2,1)S(1)}) custom-call(f32[96,16]{1,0:T(8,128)S(1)} %get-tuple-element.46.own_ref.refs_0_, f32[96,1152]{1,0:T(8,128)S(1)} %get-tuple-element.53.refs_1_, f32[96,1152]{1,0:T(8,128)S(1)} %get-tuple-element.47.mods_ref.refs_2_, ...), custom_call_target="tpu_custom_call" | custom-call | tf_op jit(solution)/shard_map/pallas_call | solution.py:479
  41.3 10.2 %all_to_all.10.refs_0_ = bf16[16,16,128]{2,1,0:T(8,128)(2,1)S(1)} all-to-all(bf16[16,16,128]{2,1,0:T(8,128)(2,1)S(1)} %get-tuple-element.57), channel_id=1, replica_groups=mesh['queue'=16,'space'=2] {'queue'}, dimensions={0} | all-to-all | bytes 131072 | tf_op jit(solution)/shard_map/all_to_all | solution.py:656
  51.5 2.4 %shard_map.97.refs_0_ = bf16[96,1152]{1,0:T(8,128)(2,1)S(1)} custom-call(bf16[16,16,128]{2,1,0:T(8,128)(2,1)S(1)} %all_to_all.10.refs_0_, f32[96,16]{1,0:T(8,128)S(1)} %get-tuple-element.56.refs_1_.own_ref.refs_0_, f32[16,16]{1,0:T(8,128)S(1)} %get-tuple-element.44.refs_1_.refs_9_.refs_2_, bf16[16,256,128]{2,1,0:T(8,128)(2,1)S(1)} %get-tuple-element.42.refs_2_.refs_3_, ...), custom_call_target="tpu_custom_call" | custom-call | tf_op jit(solution)/shard_map/pallas_call | solution.py:479
  53.9 1.3 %collective-permute-start.11 = (bf16[96,1152]{1,0:T(8,128)(2,1)S(1)}, bf16[96,1152]{1,0:T(8,128)(2,1)S(1)}, u32[]{:S(2)}, u32[]{:S(2)}) collective-permute-start(bf16[96,1152]{1,0:T(8,128)(2,1)S(1)} %shard_map.97.refs_0_), channel_id=1, source_target_pairs={{0,1},{1,0},{2,3},{3,2},{4,5},{5,4},{6,7},{7,6},{8,9},{9,8},{10,11... | collective-permute-start | bytes 663560 | tf_op jit(solution)/shard_map/ppermute | solution.py:510
  55.3 5.6 %collective-permute-done.11.refs_1_ = bf16[96,1152]{1,0:T(8,128)(2,1)S(1)} collective-permute-done((bf16[96,1152]{1,0:T(8,128)(2,1)S(1)}, bf16[96,1152]{1,0:T(8,128)(2,1)S(1)}, u32[]{:S(2)}, u32[]{:S(2)}) %collective-permute-start.11) | collective-permute-done | bytes 221216 | tf_op jit(solution)/shard_map/ppermute | solution.py:510
  60.9 2.6 %shard_map.98 = (f32[48,1152]{1,0:T(8,128)S(1)}, bf16[48,1152]{1,0:T(8,128)(2,1)S(1)}, bf16[96,576]{1,0:T(8,128)(2,1)S(1)}, bf16[96,576]{1,0:T(8,128)(2,1)S(1)}, bf16[96,576]{1,0:T(8,128)(2,1)S(1)}) custom-call(f32[96,16]{1,0:T(8,128)S(1)} %get-tuple-element.56.refs_1_.own_ref.refs_0_, f32[96,1152]{1,0:T(8,128)S(1)} %get-tuple-element.47.mods_ref.refs_2_, ...), custom_call_target="tpu_custom_call" | custom-call | tf_op jit(solution)/shard_map/pallas_call | solution.py:479
  63.5 1.3 %collective-permute-start.12 = (bf16[48,1152]{1,0:T(8,128)(2,1)S(1)}, bf16[48,1152]{1,0:T(8,128)(2,1)S(1)}, u32[]{:S(2)}, u32[]{:S(2)}) collective-permute-start(bf16[48,1152]{1,0:T(8,128)(2,1)S(1)} %get-tuple-element.62), channel_id=1, source_target_pairs={{0,1},{1,0},{2,3},{3,2},{4,5},{5,4},{6,7},{7,6},{8,9},{9,8},{10,11... | collective-permute-start | bytes 331784 | tf_op jit(solution)/shard_map/ppermute | solution.py:510
  64.9 1.1 %shard_map.99.refs_5_ = bf16[48,1152]{1,0:T(8,128)(2,1)S(1)} custom-call(bf16[96,576]{1,0:T(8,128)(2,1)S(1)} %get-tuple-element.59.query_ref, bf16[96,576]{1,0:T(8,128)(2,1)S(1)} %get-tuple-element.60.keys_ref, bf16[96,576]{1,0:T(8,128)(2,1)S(1)} %get-tuple-element.61.values_ref, bf16[4,576,1152]{2,1,0:T(8,128)(2,1)S(1)} %shard_map.94.weights_ref), custom_call_target="tpu_custom_call" | custom-call | tf_op jit(solution)/shard_map/pallas_call | solution.py:479
  66.0 2.4 %collective-permute-done.12.refs_6_ = bf16[48,1152]{1,0:T(8,128)(2,1)S(1)} collective-permute-done((bf16[48,1152]{1,0:T(8,128)(2,1)S(1)}, bf16[48,1152]{1,0:T(8,128)(2,1)S(1)}, u32[]{:S(2)}, u32[]{:S(2)}) %collective-permute-start.12) | collective-permute-done | bytes 110624 | tf_op jit(solution)/shard_map/ppermute | solution.py:510
  68.3 0.5 shard_map.100
  68.8 9.5 %all_to_all.11.arrived_ref = f32[16,8,128]{2,1,0:T(8,128)S(1)} all-to-all(f32[16,8,128]{2,1,0:T(8,128)S(1)} %shard_map.100), channel_id=1, replica_groups=mesh['queue'=16,'space'=2] {'queue'}, dimensions={0} | all-to-all | bytes 131072 | tf_op jit(solution)/shard_map/all_to_all | solution.py:668
  78.3 0.8 shard_map.101
  (3 shorter events, 0.0 us)
Async XLA Ops:
  2.5 8.5 %collective-permute-start.4 = (bf16[16,3456]{1,0:T(8,128)(2,1)S(1)}, bf16[16,3456]{1,0:T(8,128)(2,1)S(1)}, u32[]{:S(2)}, u32[]{:S(2)}) collective-permute-start(bf16[16,3456]{1,0:T(8,128)(2,1)S(1)} %get-tuple-element.37.refs_0_), channel_id=1, source_target_pairs={{0,1},{1,0},{2,3},{3,2},{4,5},{5,4},{6,7},{7,6},{8,9},{9,8},{10,11... | collective-permute-start | bytes 331784 | tf_op jit(solution)/shard_map/ppermute | solution.py:510
  5.5 3.6 %collective-permute-start = (f32[1,8,128]{2,1,0:T(8,128)S(1)}, f32[1,8,128]{2,1,0:T(8,128)S(1)}, u32[]{:S(2)}, u32[]{:S(2)}) collective-permute-start(f32[1,8,128]{2,1,0:T(8,128)S(1)} %get-tuple-element.34.refs_0_), channel_id=1, source_target_pairs={{0,1},{1,0},{2,3},{3,2},{4,5},{5,4},{6,7},{7,6},{8,9},{9,8},{10,11... | collective-permute-start | bytes 12296 | tf_op jit(solution)/shard_map/ppermute | solution.py:516
  9.1 3.6 %collective-permute-start.3 = (f32[2,8,128]{2,1,0:T(8,128)S(1)}, f32[2,8,128]{2,1,0:T(8,128)S(1)}, u32[]{:S(2)}, u32[]{:S(2)}) collective-permute-start(f32[2,8,128]{2,1,0:T(8,128)S(1)} %shard_map.88.refs_0_), channel_id=1, source_target_pairs={{0,6},{1,7},{2,4},{3,5},{4,2},{5,3},{6,0},{7,1},{8,14},{9,15},{10,... | collective-permute-start | bytes 24584 | tf_op jit(solution)/shard_map/ppermute | solution.py:516
  9.1 3.7 %collective-permute-start.2 = (f32[2,8,128]{2,1,0:T(8,128)S(1)}, f32[2,8,128]{2,1,0:T(8,128)S(1)}, u32[]{:S(2)}, u32[]{:S(2)}) collective-permute-start(f32[2,8,128]{2,1,0:T(8,128)S(1)} %shard_map.88.refs_0_), channel_id=1, source_target_pairs={{0,4},{1,5},{2,6},{3,7},{4,0},{5,1},{6,2},{7,3},{8,12},{9,13},{10,... | collective-permute-start | bytes 24584 | tf_op jit(solution)/shard_map/ppermute | solution.py:516
  10.7 2.1 %collective-permute-start.1 = (f32[2,8,128]{2,1,0:T(8,128)S(1)}, f32[2,8,128]{2,1,0:T(8,128)S(1)}, u32[]{:S(2)}, u32[]{:S(2)}) collective-permute-start(f32[2,8,128]{2,1,0:T(8,128)S(1)} %shard_map.88.refs_0_), channel_id=1, source_target_pairs={{0,2},{1,3},{2,0},{3,1},{4,6},{5,7},{6,4},{7,5},{8,10},{9,11},{10,... | collective-permute-start | bytes 24584 | tf_op jit(solution)/shard_map/ppermute | solution.py:516
  12.6 13.2 %copy-start.1 = (f32[2,48,16]{1,2,0:T(8,128)S(1)}, f32[2,48,16]{1,2,0:T(8,128)}, u32[]{:S(2)}) copy-start(f32[2,48,16]{1,2,0:T(8,128)} %param.8) | copy-start | bytes 18436
  12.8 6.0 %collective-permute-start.7 = (f32[8,8,128]{2,1,0:T(8,128)S(1)}, f32[8,8,128]{2,1,0:T(8,128)S(1)}, u32[]{:S(2)}, u32[]{:S(2)}) collective-permute-start(f32[8,8,128]{2,1,0:T(8,128)S(1)} %shard_map.90.refs_0_), channel_id=1, source_target_pairs={{0,24},{1,25},{2,26},{3,27},{4,28},{5,29},{6,30},{7,31},{8,16},{9,... | collective-permute-start | bytes 98312 | tf_op jit(solution)/shard_map/ppermute | solution.py:516
  16.4 4.8 %collective-permute-start.6 = (f32[8,8,128]{2,1,0:T(8,128)S(1)}, f32[8,8,128]{2,1,0:T(8,128)S(1)}, u32[]{:S(2)}, u32[]{:S(2)}) collective-permute-start(f32[8,8,128]{2,1,0:T(8,128)S(1)} %shard_map.90.refs_0_), channel_id=1, source_target_pairs={{0,16},{1,17},{2,18},{3,19},{4,20},{5,21},{6,22},{7,23},{8,24},{9,... | collective-permute-start | bytes 98312 | tf_op jit(solution)/shard_map/ppermute | solution.py:516
  16.4 4.8 %collective-permute-start.5 = (f32[8,8,128]{2,1,0:T(8,128)S(1)}, f32[8,8,128]{2,1,0:T(8,128)S(1)}, u32[]{:S(2)}, u32[]{:S(2)}) collective-permute-start(f32[8,8,128]{2,1,0:T(8,128)S(1)} %shard_map.90.refs_0_), channel_id=1, source_target_pairs={{0,8},{1,9},{2,10},{3,11},{4,12},{5,13},{6,14},{7,15},{8,0},{9,1},... | collective-permute-start | bytes 98312 | tf_op jit(solution)/shard_map/ppermute | solution.py:516
  24.4 7.0 %collective-permute-start.8 = (bf16[96,1152]{1,0:T(8,128)(2,1)S(1)}, bf16[96,1152]{1,0:T(8,128)(2,1)S(1)}, u32[]{:S(2)}, u32[]{:S(2)}) collective-permute-start(bf16[96,1152]{1,0:T(8,128)(2,1)S(1)} %get-tuple-element.50.refs_0_), channel_id=1, source_target_pairs={{0,1},{1,0},{2,3},{3,2},{4,5},{5,4},{6,7},{7,6},{8,9},{9,8},{10,11... | collective-permute-start | bytes 663560 | tf_op jit(solution)/shard_map/ppermute | solution.py:510
  25.9 5.5 %collective-permute-start.9 = (f32[2,16,48]{2,1,0:T(8,128)S(1)}, f32[2,16,48]{2,1,0:T(8,128)S(1)}, u32[]{:S(2)}, u32[]{:S(2)}) collective-permute-start(f32[2,16,48]{2,1,0:T(8,128)S(1)} %bitcast.7), channel_id=1, source_target_pairs={{0,1},{1,0},{2,3},{3,2},{4,5},{5,4},{6,7},{7,6},{8,9},{9,8},{10,11... | collective-permute-start | bytes 18440 | tf_op jit(solution)/shard_map/ppermute | solution.py:510
  29.1 11.4 %copy-start = (bf16[1152,16]{0,1:T(8,128)(2,1)S(1)}, bf16[1152,16]{0,1:T(8,128)(2,1)}, u32[]{:S(2)}) copy-start(bf16[1152,16]{0,1:T(8,128)(2,1)} %param.13) | copy-start | bytes 110596
  34.5 6.0 %collective-permute-start.10 = (bf16[96,1152]{1,0:T(8,128)(2,1)S(1)}, bf16[96,1152]{1,0:T(8,128)(2,1)S(1)}, u32[]{:S(2)}, u32[]{:S(2)}) collective-permute-start(bf16[96,1152]{1,0:T(8,128)(2,1)S(1)} %get-tuple-element.55.refs_5_), channel_id=1, source_target_pairs={{0,1},{1,0},{2,3},{3,2},{4,5},{5,4},{6,7},{7,6},{8,9},{9,8},{10,11... | collective-permute-start | bytes 663560 | tf_op jit(solution)/shard_map/ppermute | solution.py:510
  53.9 7.0 %collective-permute-start.11 = (bf16[96,1152]{1,0:T(8,128)(2,1)S(1)}, bf16[96,1152]{1,0:T(8,128)(2,1)S(1)}, u32[]{:S(2)}, u32[]{:S(2)}) collective-permute-start(bf16[96,1152]{1,0:T(8,128)(2,1)S(1)} %shard_map.97.refs_0_), channel_id=1, source_target_pairs={{0,1},{1,0},{2,3},{3,2},{4,5},{5,4},{6,7},{7,6},{8,9},{9,8},{10,11... | collective-permute-start | bytes 663560 | tf_op jit(solution)/shard_map/ppermute | solution.py:510
  63.5 4.8 %collective-permute-start.12 = (bf16[48,1152]{1,0:T(8,128)(2,1)S(1)}, bf16[48,1152]{1,0:T(8,128)(2,1)S(1)}, u32[]{:S(2)}, u32[]{:S(2)}) collective-permute-start(bf16[48,1152]{1,0:T(8,128)(2,1)S(1)} %get-tuple-element.62), channel_id=1, source_target_pairs={{0,1},{1,0},{2,3},{3,2},{4,5},{5,4},{6,7},{7,6},{8,9},{9,8},{10,11... | collective-permute-start | bytes 331784 | tf_op jit(solution)/shard_map/ppermute | solution.py:510

commit v5 on v2

--- a/solution.py
+++ b/solution.py
@@ -264,7 +264,7 @@
             )
 
     rows = share * blocks
-    hat = scaled(own_ref[...], cov).astype(BF16)
+    hat = (scaled(own_ref[...], cov) if first else own_ref[...]).astype(BF16)
     lanes = head_count * SLOTS
     wide = product(hat, ones_where(iota((CH, lanes), 1) % SLOTS == iota((CH, lanes), 0)))
     wide = jnp.where(iota((rows, lanes), 1) % SLOTS == CH, 1.0, wide).astype(BF16)
@@ -352,8 +352,12 @@
     stream_ref[...] = own_half(stream) if halved else stream
     normed = layer_norm(stream) * (1.0 + piece_of(mods_ref, 4, share)) + piece_of(mods_ref, 3, share)
     normed = normed.astype(BF16)
-    for ref, through in zip((query_ref, keys_ref, values_ref), projected(normed, weights_ref)):
-        ref[...] = through.astype(BF16)
+    if halved:
+        parts = [rows_by(normed, weights_ref[matrix]) for matrix in range(3)]
+    else:
+        parts = projected(normed, weights_ref)
+    for ref, part in zip((query_ref, keys_ref, values_ref), parts):
+        ref[...] = part.astype(BF16)
     half = 1 - lax.axis_index("space") if halved else None
     term_ref[...] = attend(half, blocks, query_ref, keys_ref, values_ref, weights_ref)
 
@@ -383,7 +387,7 @@
 
 def between_kernel(share, term_count, iteration, noise_count, *refs):
     blocks, rows, velocity, moved, refs = final_kernel(share, False, term_count, *refs)
-    noises, (cov_ref, velocity_ref, next_ref, sent_ref, noise_ref) = (
+    noises, (cov_ref, velocity_ref, next_ref, hat_ref, sent_ref, noise_ref) = (
         refs[:noise_count],
         refs[noise_count:],
     )
@@ -404,7 +408,9 @@
         next_ref[(position + 1) * blocks - 1 : (position + 1) * blocks, :] = noise_ref[
             pl.ds(position * devices + here, 1), :
         ]
-    hat = side_by_side(scaled(next_ref[...], cov_ref[...]), blocks, share)
+    hat = scaled(next_ref[...], cov_ref[...])
+    hat_ref[...] = hat
+    hat = side_by_side(hat, blocks, share)
     hat = jnp.where(iota((blocks, LANES), 1) == share * CH, 1.0, hat)
     sent_ref[...] = jnp.broadcast_to(hat.astype(BF16), sent_ref.shape)
 
@@ -551,11 +557,12 @@
         )
         vectors = over_space(vectors)
         spatial_weights = load(after(attention_weights, packed), 0, 4)
-        arrivals = [apart(packed, mask) for mask in range(1, 8)]
-        arrivals[-1] = after(arrivals[-1], spatial_weights)
-        gathered = joined(packed, *arrivals)
+        gathered = joined(packed, after(apart(packed, 1), spatial_weights))
+        arrivals = [apart(gathered, mask) for mask in (2, 4, 6)]
+        mods, cov, *seen = basis(vectors, spatial_weights)
+        arrivals[-1] = after(arrivals[-1], *seen)
+        gathered = joined(gathered, *arrivals)
         arrivals = [apart(gathered, mask) for mask in (8, 16, 24)]
-        mods, cov, *seen = basis(vectors, spatial_weights)
         scores, values = forms(seen)
         arrivals[-1] = after(arrivals[-1], scores)
         gathered = [joined(gathered, *arrivals)]
@@ -590,7 +597,7 @@
         spatial_term, *new = run(
             functools.partial(spatial_kernel, first, paired, share),
             outs,
-            [*gathered, *([] if first else [own]), cov, scores, values, spatial_weights],
+            [*gathered, *([] if first else [hat]), cov, scores, values, spatial_weights],
             scratch,
         )
         if first:
@@ -623,13 +630,12 @@
             )
         operands = [own, stream, mods, final_rows, sizes, *temporal_terms]
         if not last:
-            velocity, own, sent = run(
+            velocity, own, hat, sent = run(
                 functools.partial(
                     between_kernel, share, len(temporal_terms), iteration, len(noises)
                 ),
-                [
-                    ((rows, CH), F32),
-                    ((rows, CH), F32),
+                [((rows, CH), F32)] * 3
+                + [
                     ((devices if paired else 1, blocks, LANES), BF16),
                 ],
                 operands + [*noises, cov],

time: 83.3 us -> 79 us (0.948)
  starting transfers between devices: 19.7 us -> 15.6 us
  waiting for transfers between devices: 16.4 us -> 18.4 us
  blocking collectives: 21.4 us -> 19.7 us
    ppermute x10 -> x7, starting transfers between devices: 11.7 us -> 6.36 us  [apart(): lax.ppermute(x, ('queue', 'space'), [(i, i ^ mask) for i in range(count)])]
    ppermute x10 -> x7, waiting for transfers between devices: 1.26 us -> 3.53 us  [apart(): lax.ppermute(x, ('queue', 'space'), [(i, i ^ mask) for i in range(count)])]
    all_to_all x1, blocking collectives: 11.9 us -> 10.3 us  [local(): gathered = [lax.all_to_all(sent, 'queue', 0, 0, tiled=True)]]
    ppermute x6, starting transfers between devices: 8.08 us -> 9.24 us  [over_space(): return [x, lax.ppermute(x, 'space', [(0, 1), (1, 0)])]]
    pallas_call x13 -> x14, Pallas kernels: 19.6 us -> 19.2 us  [call(): pl.pallas_call(kernel, out_shape=[place(shape, dtype) for shape, dtype in...]
  transfers between devices with their start and end apart: 16 -> 13, of which waited for: 6 -> 7; matrix products, arithmetic and copies ran while one was open for 0% -> 0% of each run, Pallas kernels for 11% -> 12%
where the time goes in v5:
time: 79 us; the launch traced here: 78.8 us
  Pallas kernels  24.3 us (31%)
  blocking collectives  19.7 us (25%)
  waiting for transfers between devices  18.4 us (23%)
  starting transfers between devices  15.6 us (20%)
    pallas_call x14, Pallas kernels, call(): pl.pallas_call(kernel, out_shape=[place(shape, dtype) for shape, dtype in...  19.2 us
    ppermute x6, waiting for transfers between devices, over_space(): return [x, lax.ppermute(x, 'space', [(0, 1), (1, 0)])]  14.8 us
    all_to_all x1, blocking collectives, local(): gathered = [lax.all_to_all(sent, 'queue', 0, 0, tiled=True)]  10.3 us
    all_to_all x1, blocking collectives, local(): arrived = lax.all_to_all(sent, 'queue', 0, 0, tiled=True)  9.48 us
    ppermute x6, starting transfers between devices, over_space(): return [x, lax.ppermute(x, 'space', [(0, 1), (1, 0)])]  9.24 us
    ppermute x7, starting transfers between devices, apart(): lax.ppermute(x, ('queue', 'space'), [(i, i ^ mask) for i in range(count)])  6.36 us
    pallas_call x2, Pallas kernels, load(): pl.pallas_call(functools.partial(loader_kernel, first), out_shape=pltpu.V...  5.11 us
    ppermute x7, waiting for transfers between devices, apart(): lax.ppermute(x, ('queue', 'space'), [(i, i ^ mask) for i in range(count)])  3.53 us
  transfers between devices with their start and end apart: 13, of which 7 were waited for; matrix products, arithmetic and copies ran while one was open for 0% of the time, Pallas kernels for 12%

profile of v5, /device:TPU:0, one launch (start us, length us, event | category | flops | bytes accessed | tf_op | source)
XLA Modules:
  0.0 78.8 jit_solution(16399247008870042576)
XLA Ops:
  0.6 1.9 %shard_map.86 = (bf16[16,3456]{1,0:T(8,128)(2,1)S(1)}, f32[16,128]{1,0:T(8,128)S(1)}, f32[1,8,128]{2,1,0:T(8,128)S(1)}, bf16[16,1152]{1,0:T(8,128)(2,1)S(1)}) custom-call(s32[16]{0:T(128)} %levels_hbm.1, bf16[256,3456]{1,0:T(8,128)(2,1)} %weight_hbm.1, f32[1,16,48]{2,1,0:T(8,128)} %bitcast.10, bf16[16,1152]{1,0:T(8,128)(2,1)} %embed_hbm.1), custom_call_target="tpu_custom_call" | custom-call | tf_op jit(solution)/shard_map/pallas_call | solution.py:470
  2.5 3.0 %collective-permute-start.4 = (bf16[16,3456]{1,0:T(8,128)(2,1)S(1)}, bf16[16,3456]{1,0:T(8,128)(2,1)S(1)}, u32[]{:S(2)}, u32[]{:S(2)}) collective-permute-start(bf16[16,3456]{1,0:T(8,128)(2,1)S(1)} %get-tuple-element.38.refs_0_), channel_id=1, source_target_pairs={{0,1},{1,0},{2,3},{3,2},{4,5},{5,4},{6,7},{7,6},{8,9},{9,8},{10,11... | collective-permute-start | bytes 331784 | tf_op jit(solution)/shard_map/ppermute | solution.py:501
  5.5 0.1 collective-permute-start
  5.6 2.6 %shard_map.87.refs_3_.refs_4_.refs_5_ = bf16[4,576,1152]{2,1,0:T(8,128)(2,1)S(1)} custom-call(bf16[8,576,1152]{2,1,0:T(8,128)(2,1)} %weights_ref.1), custom_call_target="tpu_custom_call" | custom-call | bytes 5308416 | tf_op jit(solution)/shard_map/pallas_call | solution.py:451
  8.2 1.0 %collective-permute-done.refs_1_ = f32[1,8,128]{2,1,0:T(8,128)S(1)} collective-permute-done((f32[1,8,128]{2,1,0:T(8,128)S(1)}, f32[1,8,128]{2,1,0:T(8,128)S(1)}, u32[]{:S(2)}, u32[]{:S(2)}) %collective-permute-start) | collective-permute-done | bytes 4128 | tf_op jit(solution)/shard_map/ppermute | solution.py:507
  9.1 0.0 collective-permute-start.3
  9.1 1.6 %collective-permute-start.2 = (f32[2,8,128]{2,1,0:T(8,128)S(1)}, f32[2,8,128]{2,1,0:T(8,128)S(1)}, u32[]{:S(2)}, u32[]{:S(2)}) collective-permute-start(f32[2,8,128]{2,1,0:T(8,128)S(1)} %shard_map.88.refs_0_), channel_id=1, source_target_pairs={{0,4},{1,5},{2,6},{3,7},{4,0},{5,1},{6,2},{7,3},{8,12},{9,13},{10,... | collective-permute-start | bytes 24584 | tf_op jit(solution)/shard_map/ppermute | solution.py:507
  10.7 0.3 collective-permute-start.1
  11.0 0.0 collective-permute-done.4.refs_1_
  11.0 1.7 %shard_map.89 = (f32[96,1152]{1,0:T(8,128)S(1)}, f32[16,16]{1,0:T(8,128)S(1)}, bf16[3,256,576]{2,1,0:T(8,128)(2,1)S(1)}, f32[3,16,576]{2,1,0:T(8,128)S(1)}) custom-call(bf16[16,3456]{1,0:T(8,128)(2,1)S(1)} %get-tuple-element.38.refs_0_, bf16[16,3456]{1,0:T(8,128)(2,1)S(1)} %collective-permute-done.4.refs_1_, ...), custom_call_target="tpu_custom_call" | custom-call | tf_op jit(solution)/shard_map/pallas_call | solution.py:470
  12.7 0.0 copy-start.1
  12.7 0.0 collective-permute-done.3.refs_3_
  12.7 0.1 collective-permute-done.2.refs_2_
  12.8 0.0 collective-permute-done.1.refs_1_
  12.8 3.6 %collective-permute-start.7 = (f32[8,8,128]{2,1,0:T(8,128)S(1)}, f32[8,8,128]{2,1,0:T(8,128)S(1)}, u32[]{:S(2)}, u32[]{:S(2)}) collective-permute-start(f32[8,8,128]{2,1,0:T(8,128)S(1)} %shard_map.90.refs_0_), channel_id=1, source_target_pairs={{0,24},{1,25},{2,26},{3,27},{4,28},{5,29},{6,30},{7,31},{8,16},{9,... | collective-permute-start | bytes 98312 | tf_op jit(solution)/shard_map/ppermute | solution.py:507
  16.5 0.0 collective-permute-start.6
  16.5 0.8 collective-permute-start.5
  17.3 1.6 %shard_map.91 = (bf16[16,256,128]{2,1,0:T(8,128)(2,1)S(1)}, bf16[16,128,576]{2,1,0:T(8,128)(2,1)S(1)}) custom-call(bf16[3,256,576]{2,1,0:T(8,128)(2,1)S(1)} %get-tuple-element.40.rows_ref, f32[3,16,576]{2,1,0:T(8,128)S(1)} %get-tuple-element.41.last_ref), custom_call_target="tpu_custom_call" | custom-call | tf_op jit(solution)/shard_map/pallas_call | solution.py:470
  18.9 0.0 collective-permute-done.7.refs_3_
  18.9 2.4 %collective-permute-done.6.refs_2_ = f32[8,8,128]{2,1,0:T(8,128)S(1)} collective-permute-done((f32[8,8,128]{2,1,0:T(8,128)S(1)}, f32[8,8,128]{2,1,0:T(8,128)S(1)}, u32[]{:S(2)}, u32[]{:S(2)}) %collective-permute-start.6) | collective-permute-done | bytes 32800 | tf_op jit(solution)/shard_map/ppermute | solution.py:507
  21.3 0.0 collective-permute-done.5.refs_1_
  21.3 3.1 %shard_map.93 = (bf16[96,1152]{1,0:T(8,128)(2,1)S(1)}, f32[96,16]{1,0:T(8,128)S(1)}) custom-call(f32[32,8,128]{2,1,0:T(8,128)S(1)} %shard_map.92.refs_0_, f32[16,16]{1,0:T(8,128)S(1)} %get-tuple-element.45.refs_1_.refs_9_.refs_2_, bf16[16,256,128]{2,1,0:T(8,128)(2,1)S(1)} %get-tuple-element.43.refs_2_.refs_3_, ...), custom_call_target="tpu_custom_call" | custom-call | tf_op jit(solution)/shard_map/pallas_call | solution.py:470
  24.4 1.5 %collective-permute-start.8 = (bf16[96,1152]{1,0:T(8,128)(2,1)S(1)}, bf16[96,1152]{1,0:T(8,128)(2,1)S(1)}, u32[]{:S(2)}, u32[]{:S(2)}) collective-permute-start(bf16[96,1152]{1,0:T(8,128)(2,1)S(1)} %get-tuple-element.51.refs_0_), channel_id=1, source_target_pairs={{0,1},{1,0},{2,3},{3,2},{4,5},{5,4},{6,7},{7,6},{8,9},{9,8},{10,11... | collective-permute-start | bytes 663560 | tf_op jit(solution)/shard_map/ppermute | solution.py:501
  25.8 0.0 copy-done.1
  25.8 0.7 collective-permute-start.9
  26.5 2.6 %shard_map.94.weights_ref = bf16[4,576,1152]{2,1,0:T(8,128)(2,1)S(1)} custom-call(bf16[8,576,1152]{2,1,0:T(8,128)(2,1)} %weights_ref.1), custom_call_target="tpu_custom_call" | custom-call | bytes 5308416 | tf_op jit(solution)/shard_map/pallas_call | solution.py:451
  29.1 0.0 copy-start
  29.1 2.3 %collective-permute-done.9.refs_8_ = f32[2,16,48]{2,1,0:T(8,128)S(1)} collective-permute-done((f32[2,16,48]{2,1,0:T(8,128)S(1)}, f32[2,16,48]{2,1,0:T(8,128)S(1)}, u32[]{:S(2)}, u32[]{:S(2)}) %collective-permute-start.9) | collective-permute-done | bytes 6176 | tf_op jit(solution)/shard_map/ppermute | solution.py:501
  31.4 0.0 collective-permute-done.8.refs_1_
  31.4 3.1 %shard_map.95 = (f32[96,1152]{1,0:T(8,128)S(1)}, bf16[96,1152]{1,0:T(8,128)(2,1)S(1)}) custom-call(f32[96,16]{1,0:T(8,128)S(1)} %get-tuple-element.47.own_ref.refs_0_, f32[96,1152]{1,0:T(8,128)S(1)} %get-tuple-element.48.mods_ref.refs_2_, bf16[16,1152]{1,0:T(8,128)(2,1)S(1)} %get-tuple-element.39.refs_2_.embed_ref, ...), custom_call_target="tpu_custom_call" | custom-call | tf_op jit(solution)/shard_map/pallas_call | solution.py:470
  34.5 1.5 %collective-permute-start.10 = (bf16[96,1152]{1,0:T(8,128)(2,1)S(1)}, bf16[96,1152]{1,0:T(8,128)(2,1)S(1)}, u32[]{:S(2)}, u32[]{:S(2)}) collective-permute-start(bf16[96,1152]{1,0:T(8,128)(2,1)S(1)} %get-tuple-element.56.refs_5_), channel_id=1, source_target_pairs={{0,1},{1,0},{2,3},{3,2},{4,5},{5,4},{6,7},{7,6},{8,9},{9,8},{10,11... | collective-permute-start | bytes 663560 | tf_op jit(solution)/shard_map/ppermute | solution.py:501
  36.0 4.5 %collective-permute-done.10.refs_6_ = bf16[96,1152]{1,0:T(8,128)(2,1)S(1)} collective-permute-done((bf16[96,1152]{1,0:T(8,128)(2,1)S(1)}, bf16[96,1152]{1,0:T(8,128)(2,1)S(1)}, u32[]{:S(2)}, u32[]{:S(2)}) %collective-permute-start.10) | collective-permute-done | bytes 221216 | tf_op jit(solution)/shard_map/ppermute | solution.py:501
  40.5 0.0 copy-done
  40.5 0.8 %shard_map.96 = (f32[96,16]{1,0:T(8,128)S(1)}, f32[96,16]{1,0:T(8,128)S(1)}, f32[96,16]{1,0:T(8,128)S(1)}, bf16[16,16,128]{2,1,0:T(8,128)(2,1)S(1)}) custom-call(f32[96,16]{1,0:T(8,128)S(1)} %get-tuple-element.47.own_ref.refs_0_, f32[96,1152]{1,0:T(8,128)S(1)} %get-tuple-element.54.refs_1_, f32[96,1152]{1,0:T(8,128)S(1)} %get-tuple-element.48.mods_ref.refs_2_, ...), custom_call_target="tpu_custom_call" | custom-call | tf_op jit(solution)/shard_map/pallas_call | solution.py:470
  41.3 10.3 %all_to_all.10.refs_0_ = bf16[16,16,128]{2,1,0:T(8,128)(2,1)S(1)} all-to-all(bf16[16,16,128]{2,1,0:T(8,128)(2,1)S(1)} %get-tuple-element.58), channel_id=1, replica_groups=mesh['queue'=16,'space'=2] {'queue'}, dimensions={0} | all-to-all | bytes 131072 | tf_op jit(solution)/shard_map/all_to_all | solution.py:646
  51.6 2.1 %shard_map.97.refs_0_ = bf16[96,1152]{1,0:T(8,128)(2,1)S(1)} custom-call(bf16[16,16,128]{2,1,0:T(8,128)(2,1)S(1)} %all_to_all.10.refs_0_, f32[96,16]{1,0:T(8,128)S(1)} %get-tuple-element.59.refs_1_, f32[16,16]{1,0:T(8,128)S(1)} %get-tuple-element.45.refs_1_.refs_9_.refs_2_, bf16[16,256,128]{2,1,0:T(8,128)(2,1)S(1)} %get-tuple-element.43.refs_2_.refs_3_, ...), custom_call_target="tpu_custom_call" | custom-call | tf_op jit(solution)/shard_map/pallas_call | solution.py:470
  53.7 1.3 %collective-permute-start.11 = (bf16[96,1152]{1,0:T(8,128)(2,1)S(1)}, bf16[96,1152]{1,0:T(8,128)(2,1)S(1)}, u32[]{:S(2)}, u32[]{:S(2)}) collective-permute-start(bf16[96,1152]{1,0:T(8,128)(2,1)S(1)} %shard_map.97.refs_0_), channel_id=1, source_target_pairs={{0,1},{1,0},{2,3},{3,2},{4,5},{5,4},{6,7},{7,6},{8,9},{9,8},{10,11... | collective-permute-start | bytes 663560 | tf_op jit(solution)/shard_map/ppermute | solution.py:501
  55.0 5.6 %collective-permute-done.11.refs_1_ = bf16[96,1152]{1,0:T(8,128)(2,1)S(1)} collective-permute-done((bf16[96,1152]{1,0:T(8,128)(2,1)S(1)}, bf16[96,1152]{1,0:T(8,128)(2,1)S(1)}, u32[]{:S(2)}, u32[]{:S(2)}) %collective-permute-start.11) | collective-permute-done | bytes 221216 | tf_op jit(solution)/shard_map/ppermute | solution.py:501
  60.6 2.6 %shard_map.98 = (f32[48,1152]{1,0:T(8,128)S(1)}, bf16[48,1152]{1,0:T(8,128)(2,1)S(1)}, bf16[96,576]{1,0:T(8,128)(2,1)S(1)}, bf16[96,576]{1,0:T(8,128)(2,1)S(1)}, bf16[96,576]{1,0:T(8,128)(2,1)S(1)}) custom-call(f32[96,16]{1,0:T(8,128)S(1)} %get-tuple-element.57.own_ref.refs_0_, f32[96,1152]{1,0:T(8,128)S(1)} %get-tuple-element.48.mods_ref.refs_2_, ...), custom_call_target="tpu_custom_call" | custom-call | tf_op jit(solution)/shard_map/pallas_call | solution.py:470
  63.3 1.3 %collective-permute-start.12 = (bf16[48,1152]{1,0:T(8,128)(2,1)S(1)}, bf16[48,1152]{1,0:T(8,128)(2,1)S(1)}, u32[]{:S(2)}, u32[]{:S(2)}) collective-permute-start(bf16[48,1152]{1,0:T(8,128)(2,1)S(1)} %get-tuple-element.64), channel_id=1, source_target_pairs={{0,1},{1,0},{2,3},{3,2},{4,5},{5,4},{6,7},{7,6},{8,9},{9,8},{10,11... | collective-permute-start | bytes 331784 | tf_op jit(solution)/shard_map/ppermute | solution.py:501
  64.6 1.1 %shard_map.99.refs_5_ = bf16[48,1152]{1,0:T(8,128)(2,1)S(1)} custom-call(bf16[96,576]{1,0:T(8,128)(2,1)S(1)} %get-tuple-element.61.query_ref, bf16[96,576]{1,0:T(8,128)(2,1)S(1)} %get-tuple-element.62.keys_ref, bf16[96,576]{1,0:T(8,128)(2,1)S(1)} %get-tuple-element.63.values_ref, bf16[4,576,1152]{2,1,0:T(8,128)(2,1)S(1)} %shard_map.94.weights_ref), custom_call_target="tpu_custom_call" | custom-call | tf_op jit(solution)/shard_map/pallas_call | solution.py:470
  65.7 2.4 %collective-permute-done.12.refs_6_ = bf16[48,1152]{1,0:T(8,128)(2,1)S(1)} collective-permute-done((bf16[48,1152]{1,0:T(8,128)(2,1)S(1)}, bf16[48,1152]{1,0:T(8,128)(2,1)S(1)}, u32[]{:S(2)}, u32[]{:S(2)}) %collective-permute-start.12) | collective-permute-done | bytes 110624 | tf_op jit(solution)/shard_map/ppermute | solution.py:501
  68.1 0.4 shard_map.100
  68.5 9.5 %all_to_all.11.arrived_ref = f32[16,8,128]{2,1,0:T(8,128)S(1)} all-to-all(f32[16,8,128]{2,1,0:T(8,128)S(1)} %shard_map.100), channel_id=1, replica_groups=mesh['queue'=16,'space'=2] {'queue'}, dimensions={0} | all-to-all | bytes 131072 | tf_op jit(solution)/shard_map/all_to_all | solution.py:658
  78.0 0.8 shard_map.101
  (3 shorter events, 0.0 us)
Async XLA Ops:
  2.5 8.5 %collective-permute-start.4 = (bf16[16,3456]{1,0:T(8,128)(2,1)S(1)}, bf16[16,3456]{1,0:T(8,128)(2,1)S(1)}, u32[]{:S(2)}, u32[]{:S(2)}) collective-permute-start(bf16[16,3456]{1,0:T(8,128)(2,1)S(1)} %get-tuple-element.38.refs_0_), channel_id=1, source_target_pairs={{0,1},{1,0},{2,3},{3,2},{4,5},{5,4},{6,7},{7,6},{8,9},{9,8},{10,11... | collective-permute-start | bytes 331784 | tf_op jit(solution)/shard_map/ppermute | solution.py:501
  5.5 3.6 %collective-permute-start = (f32[1,8,128]{2,1,0:T(8,128)S(1)}, f32[1,8,128]{2,1,0:T(8,128)S(1)}, u32[]{:S(2)}, u32[]{:S(2)}) collective-permute-start(f32[1,8,128]{2,1,0:T(8,128)S(1)} %get-tuple-element.35.refs_0_), channel_id=1, source_target_pairs={{0,1},{1,0},{2,3},{3,2},{4,5},{5,4},{6,7},{7,6},{8,9},{9,8},{10,11... | collective-permute-start | bytes 12296 | tf_op jit(solution)/shard_map/ppermute | solution.py:507
  9.1 3.5 %collective-permute-start.3 = (f32[2,8,128]{2,1,0:T(8,128)S(1)}, f32[2,8,128]{2,1,0:T(8,128)S(1)}, u32[]{:S(2)}, u32[]{:S(2)}) collective-permute-start(f32[2,8,128]{2,1,0:T(8,128)S(1)} %shard_map.88.refs_0_), channel_id=1, source_target_pairs={{0,6},{1,7},{2,4},{3,5},{4,2},{5,3},{6,0},{7,1},{8,14},{9,15},{10,... | collective-permute-start | bytes 24584 | tf_op jit(solution)/shard_map/ppermute | solution.py:507
  9.1 3.7 %collective-permute-start.2 = (f32[2,8,128]{2,1,0:T(8,128)S(1)}, f32[2,8,128]{2,1,0:T(8,128)S(1)}, u32[]{:S(2)}, u32[]{:S(2)}) collective-permute-start(f32[2,8,128]{2,1,0:T(8,128)S(1)} %shard_map.88.refs_0_), channel_id=1, source_target_pairs={{0,4},{1,5},{2,6},{3,7},{4,0},{5,1},{6,2},{7,3},{8,12},{9,13},{10,... | collective-permute-start | bytes 24584 | tf_op jit(solution)/shard_map/ppermute | solution.py:507
  10.7 2.1 %collective-permute-start.1 = (f32[2,8,128]{2,1,0:T(8,128)S(1)}, f32[2,8,128]{2,1,0:T(8,128)S(1)}, u32[]{:S(2)}, u32[]{:S(2)}) collective-permute-start(f32[2,8,128]{2,1,0:T(8,128)S(1)} %shard_map.88.refs_0_), channel_id=1, source_target_pairs={{0,2},{1,3},{2,0},{3,1},{4,6},{5,7},{6,4},{7,5},{8,10},{9,11},{10,... | collective-permute-start | bytes 24584 | tf_op jit(solution)/shard_map/ppermute | solution.py:507
  12.7 13.2 %copy-start.1 = (f32[2,48,16]{1,2,0:T(8,128)S(1)}, f32[2,48,16]{1,2,0:T(8,128)}, u32[]{:S(2)}) copy-start(f32[2,48,16]{1,2,0:T(8,128)} %param.8) | copy-start | bytes 18436
  12.8 6.0 %collective-permute-start.7 = (f32[8,8,128]{2,1,0:T(8,128)S(1)}, f32[8,8,128]{2,1,0:T(8,128)S(1)}, u32[]{:S(2)}, u32[]{:S(2)}) collective-permute-start(f32[8,8,128]{2,1,0:T(8,128)S(1)} %shard_map.90.refs_0_), channel_id=1, source_target_pairs={{0,24},{1,25},{2,26},{3,27},{4,28},{5,29},{6,30},{7,31},{8,16},{9,... | collective-permute-start | bytes 98312 | tf_op jit(solution)/shard_map/ppermute | solution.py:507
  16.5 4.8 %collective-permute-start.6 = (f32[8,8,128]{2,1,0:T(8,128)S(1)}, f32[8,8,128]{2,1,0:T(8,128)S(1)}, u32[]{:S(2)}, u32[]{:S(2)}) collective-permute-start(f32[8,8,128]{2,1,0:T(8,128)S(1)} %shard_map.90.refs_0_), channel_id=1, source_target_pairs={{0,16},{1,17},{2,18},{3,19},{4,20},{5,21},{6,22},{7,23},{8,24},{9,... | collective-permute-start | bytes 98312 | tf_op jit(solution)/shard_map/ppermute | solution.py:507
  16.5 4.8 %collective-permute-start.5 = (f32[8,8,128]{2,1,0:T(8,128)S(1)}, f32[8,8,128]{2,1,0:T(8,128)S(1)}, u32[]{:S(2)}, u32[]{:S(2)}) collective-permute-start(f32[8,8,128]{2,1,0:T(8,128)S(1)} %shard_map.90.refs_0_), channel_id=1, source_target_pairs={{0,8},{1,9},{2,10},{3,11},{4,12},{5,13},{6,14},{7,15},{8,0},{9,1},... | collective-permute-start | bytes 98312 | tf_op jit(solution)/shard_map/ppermute | solution.py:507
  24.4 7.0 %collective-permute-start.8 = (bf16[96,1152]{1,0:T(8,128)(2,1)S(1)}, bf16[96,1152]{1,0:T(8,128)(2,1)S(1)}, u32[]{:S(2)}, u32[]{:S(2)}) collective-permute-start(bf16[96,1152]{1,0:T(8,128)(2,1)S(1)} %get-tuple-element.51.refs_0_), channel_id=1, source_target_pairs={{0,1},{1,0},{2,3},{3,2},{4,5},{5,4},{6,7},{7,6},{8,9},{9,8},{10,11... | collective-permute-start | bytes 663560 | tf_op jit(solution)/shard_map/ppermute | solution.py:501
  25.8 5.5 %collective-permute-start.9 = (f32[2,16,48]{2,1,0:T(8,128)S(1)}, f32[2,16,48]{2,1,0:T(8,128)S(1)}, u32[]{:S(2)}, u32[]{:S(2)}) collective-permute-start(f32[2,16,48]{2,1,0:T(8,128)S(1)} %bitcast.7), channel_id=1, source_target_pairs={{0,1},{1,0},{2,3},{3,2},{4,5},{5,4},{6,7},{7,6},{8,9},{9,8},{10,11... | collective-permute-start | bytes 18440 | tf_op jit(solution)/shard_map/ppermute | solution.py:501
  29.1 11.4 %copy-start = (bf16[1152,16]{0,1:T(8,128)(2,1)S(1)}, bf16[1152,16]{0,1:T(8,128)(2,1)}, u32[]{:S(2)}) copy-start(bf16[1152,16]{0,1:T(8,128)(2,1)} %param.13) | copy-start | bytes 110596
  34.5 6.0 %collective-permute-start.10 = (bf16[96,1152]{1,0:T(8,128)(2,1)S(1)}, bf16[96,1152]{1,0:T(8,128)(2,1)S(1)}, u32[]{:S(2)}, u32[]{:S(2)}) collective-permute-start(bf16[96,1152]{1,0:T(8,128)(2,1)S(1)} %get-tuple-element.56.refs_5_), channel_id=1, source_target_pairs={{0,1},{1,0},{2,3},{3,2},{4,5},{5,4},{6,7},{7,6},{8,9},{9,8},{10,11... | collective-permute-start | bytes 663560 | tf_op jit(solution)/shard_map/ppermute | solution.py:501
  53.7 7.0 %collective-permute-start.11 = (bf16[96,1152]{1,0:T(8,128)(2,1)S(1)}, bf16[96,1152]{1,0:T(8,128)(2,1)S(1)}, u32[]{:S(2)}, u32[]{:S(2)}) collective-permute-start(bf16[96,1152]{1,0:T(8,128)(2,1)S(1)} %shard_map.97.refs_0_), channel_id=1, source_target_pairs={{0,1},{1,0},{2,3},{3,2},{4,5},{5,4},{6,7},{7,6},{8,9},{9,8},{10,11... | collective-permute-start | bytes 663560 | tf_op jit(solution)/shard_map/ppermute | solution.py:501
  63.3 4.8 %collective-permute-start.12 = (bf16[48,1152]{1,0:T(8,128)(2,1)S(1)}, bf16[48,1152]{1,0:T(8,128)(2,1)S(1)}, u32[]{:S(2)}, u32[]{:S(2)}) collective-permute-start(bf16[48,1152]{1,0:T(8,128)(2,1)S(1)} %get-tuple-element.64), channel_id=1, source_target_pairs={{0,1},{1,0},{2,3},{3,2},{4,5},{5,4},{6,7},{7,6},{8,9},{9,8},{10,11... | collective-permute-start | bytes 331784 | tf_op jit(solution)/shard_map/ppermute | solution.py:501
